TPU v7x, 32 devices: a whole 2x2x4 slice. The times are simulated.
32 devices in a mesh: dp: 32 (over z, y, x, core).
Axes of the slice: x: 2, y: 2, z: 4, core: 2. Of those that a mesh axis runs over, the one named last changes fastest.
Arguments:
- block_in: bfloat16 [4096, 2048], P('dp'), may hold values from -6 to 6
- out_grad: bfloat16 [4096, 2048], P('dp'), may hold values from -6 to 6
- norm1_gain: float32 [2048], P('dp'), may hold values from 0.5 to 1.5
- conv_weight: float32 [6144, 4], P('dp'), may hold values from -3 to 3
- head_gain: float32 [2048], P('dp'), may hold values from 0.5 to 1.5
- qkv_weight: float32 [2048, 6144], P('dp'), may hold values from -0.125 to 0.125
- beta_weight: float32 [2048, 16], P('dp'), may hold values from -0.125 to 0.125
- gate_weight: float32 [2048, 2048], P('dp'), may hold values from -0.125 to 0.125
- out_weight: float32 [2048, 2048], P('dp'), may hold values from -0.125 to 0.125
- norm2_gain: float32 [2048], P('dp'), may hold values from 0.5 to 1.5
- updown_weight: float32 [2048, 11264], P('dp'), may hold values from -0.125 to 0.125
- down_weight: float32 [5632, 2048], P('dp'), may hold values from -0.078125 to 0.078125
- seq_blocks: int32 [32, 2], P('dp'), may hold values from 0 to 2, as said below
- lead_blocks: int32 [32], P('dp'), may hold values from 0 to 1, as said below
Outputs:
- block_out: bfloat16 [4096, 2048], P('dp')
- input_grad: bfloat16 [4096, 2048], P('dp')
- norm1_gain_grad: float32 [2048], P('dp')
- conv_weight_grad: float32 [6144, 4], P('dp')
- head_gain_grad: float32 [2048], P('dp')
- qkv_weight_grad: float32 [2048, 6144], P('dp')
- beta_weight_grad: float32 [2048, 16], P('dp')
- gate_weight_grad: float32 [2048, 2048], P('dp')
- out_weight_grad: float32 [2048, 2048], P('dp')
- norm2_gain_grad: float32 [2048], P('dp')
- updown_weight_grad: float32 [2048, 11264], P('dp')
- down_weight_grad: float32 [5632, 2048], P('dp')
Inputs may be any that keep to these rules, and one draw needn't show every extreme that they name: `seq_blocks`: row r gives device r's two sequence lengths in blocks of 64 rows; the first is at least 1, the second may be 0, both together at most 2; some device holds one sequence of 2 blocks. `lead_blocks`: padding blocks before device r's sequences; together with both lengths at most 2; the blocks after the sequences are padding.
All inputs are finite; a program needn't handle non-finite values.
Results may differ from a plain program's by a relative error of at most 0.012.
The roundings to bfloat16 on the way count: a program that leaves them out, or rounds other values in their place, can miss the bound.
Values may be sent and summed in bfloat16 or wider, within the bound.
No kernel may reach another device: no remote copies, remote signals or barrier semaphores. Data moves between devices by JAX's collectives and lax.ppermute only.
A program may use at most 448 MiB of HBM per device.

v0:
```python
import functools

import jax
import jax.numpy as jnp
from jax import lax
from jax.experimental import pallas as pl
from jax.experimental.pallas import tpu as pltpu
from jax.sharding import PartitionSpec as P

D = 2048
HEADS = 16
HEAD_DIM = 128
FF = 5632
KERNEL = 4
BLOCK_ROWS = 64
BLOCKS_DEV = 2
GROUP_ROWS = BLOCK_ROWS * BLOCKS_DEV
SMALL = 128
MODEL = 4

f32 = jnp.float32
bf = jnp.bfloat16


def block_layouts(first, second, lead):
    def doc(block):
        in_first = (block >= lead) & (block < lead + first)
        in_second = (block >= lead + first) & (block < lead + first + second)
        return jnp.where(in_first, 1, jnp.where(in_second, 2, 0))

    starts = (lead == 1) | (lead + first == 1) & (second > 0)
    columns = [doc(0) > 0, doc(1) > 0, doc(0) == doc(1), ~starts]
    return jnp.stack(columns, 1).astype(f32)


def plain_product(left, right):
    return jnp.dot(left, right, preferred_element_type=f32)


def rows_product(left, right):
    return lax.dot_general(left, right, (((0,), (0,)), ((), ())), preferred_element_type=f32)


def transposed_product(left, right):
    return lax.dot_general(left, right, (((1,), (1,)), ((), ())), preferred_element_type=f32)


def halves(values):
    high = values.astype(bf)
    return high, (values - high.astype(f32)).astype(bf)


def exact(left, right, left_dim, right_dim):
    left_high, left_low = left if isinstance(left, tuple) else halves(left)
    right_high, right_low = right if isinstance(right, tuple) else halves(right)
    return lax.dot_general(
        jnp.concatenate([left_high, left_high, left_low], left_dim),
        jnp.concatenate([right_high, right_low, right_high], right_dim),
        (((left_dim,), (right_dim,)), ((), ())),
        preferred_element_type=f32,
    )


def stacked(first, second):
    return tuple(jnp.concatenate([a, b], 0) for a, b in zip(first, second))


class Tile:
    def __init__(self, layout_ref, group):
        live_first, live_second, same, persist = (layout_ref[group, i] for i in range(4))
        shape = (GROUP_ROWS, HEAD_DIM)
        row = lax.broadcasted_iota(jnp.int32, shape, 0)
        col = lax.broadcasted_iota(jnp.int32, shape, 1)
        late = row >= BLOCK_ROWS
        self.row, self.col = row, col
        self.live = jnp.where(late, live_second, live_first)
        self.taps = [None] + [
            jnp.where(
                row < offset,
                0.0,
                jnp.where(late & (row < BLOCK_ROWS + offset), same, 1.0),
            )
            for offset in range(1, KERNEL)
        ]
        cross = jnp.where(late & (col < BLOCK_ROWS), persist, 1.0)
        self.lower = jnp.where(row > col, cross, 0.0)
        self.lower_full = jnp.where(row >= col, cross, 0.0)

    def earlier(self, values, offset):
        return pltpu.roll(values, offset, 0) * self.taps[offset]

    def later(self, values, offset):
        return pltpu.roll(values * self.taps[offset], GROUP_ROWS - offset, 0)


def convolve(tile, values, taps):
    total = values * taps[0]
    for offset in range(1, KERNEL):
        total = total + tile.earlier(values, offset) * taps[offset]
    return total


def unit_scale(values):
    return lax.rsqrt(jnp.sum(values * values, -1, keepdims=True) + 1e-06)


def head_columns(part_width, section, head):
    return pl.ds(section * part_width + head * HEAD_DIM, HEAD_DIM)


def unit_inverses(tile, lowers):
    eye = jnp.where(tile.row == tile.col, 1.0, 0.0)
    inverses = None
    size = 1
    while size < GROUP_ROWS:
        pair = tile.row // (2 * size) == tile.col // (2 * size)
        split = pair & (tile.row // size != tile.col // size)
        parts = [jnp.where(split, lower, 0.0) for lower in lowers]
        if inverses is None:
            inverses = [eye - part for part in parts]
        else:
            kept = [halves(inverse) for inverse in inverses]
            inner = [exact(part, known, 1, 0) for part, known in zip(parts, kept)]
            outer = [exact(known, value, 1, 0) for known, value in zip(kept, inner)]
            inverses = [inverse - value for inverse, value in zip(inverses, outer)]
        size *= 2
    return inverses


def mixer_forward_kernel(
    layout_ref, pre_ref, param_ref, mixed_ref, inverse_ref, score_ref, solved_ref, out_ref
):
    width = mixed_ref.shape[1]
    heads = range(width // HEAD_DIM)
    tile = Tile(layout_ref, pl.program_id(0))
    queries, keys, values, strengths = [], [], [], []
    for head in heads:
        parts = []
        for section in range(3):
            columns = head_columns(width, section, head)
            taps = [param_ref[offset : offset + 1, columns] for offset in range(KERNEL)]
            convolved = convolve(tile, pre_ref[:, columns], taps)
            parts.append(convolved * jax.nn.sigmoid(convolved))
        queries.append(parts[0] * (unit_scale(parts[0]) * HEAD_DIM**-0.5))
        keys.append(parts[1] * unit_scale(parts[1]))
        values.append(parts[2])
        start = 4 * width + head
        strengths.append(jax.nn.sigmoid(pre_ref[:, start : start + 1]) * tile.live)
    lowers, scores = [], []
    for head in heads:
        key_halves = halves(keys[head])
        both = exact(stacked(key_halves, halves(queries[head])), key_halves, 1, 1)
        lowers.append(both[:GROUP_ROWS] * strengths[head] * tile.lower)
        scores.append(both[GROUP_ROWS:] * tile.lower_full)
    inverses = unit_inverses(tile, lowers)
    solved = [exact(inverses[head], values[head] * strengths[head], 1, 0) for head in heads]
    outs = [exact(scores[head], solved[head], 1, 0) for head in heads]
    for head in heads:
        out = outs[head]
        scaled = out * lax.rsqrt(jnp.mean(out * out, -1, keepdims=True) + 1e-05)
        gate = pre_ref[:, head_columns(width, 3, head)]
        gain = param_ref[KERNEL : KERNEL + 1, head_columns(width, 0, head)]
        mixed = scaled * gain * (gate * jax.nn.sigmoid(gate)) * tile.live
        mixed_ref[:, head_columns(width, 0, head)] = mixed.astype(bf)
        inverse_ref[head] = inverses[head]
        score_ref[head] = scores[head]
        solved_ref[head] = solved[head]
        out_ref[head] = out


def mixer_backward_kernel(
    layout_ref,
    pre_ref,
    param_ref,
    weight_ref,
    inverse_ref,
    score_ref,
    solved_ref,
    out_ref,
    *refs,
):
    *mixed_refs, d_pre_ref, d_param_ref, grad_ref = refs
    width = grad_ref.shape[1]
    heads = range(width // HEAD_DIM)
    tile = Tile(layout_ref, pl.program_id(0))
    for group, mixed_ref in enumerate(mixed_refs):

        @pl.when(pl.program_id(0) == group)
        def _():
            grad_ref[...] = transposed_product(mixed_ref[...], weight_ref[...])

    @pl.when(pl.program_id(0) == 0)
    def _():
        d_param_ref[...] = jnp.zeros_like(d_param_ref)

    def along(values):
        return jnp.sum(values, -1, keepdims=True)

    d_outs = []
    for head in heads:
        columns = head_columns(width, 0, head)
        d_mixed = grad_ref[:, columns] * tile.live
        out = out_ref[head]
        scale = lax.rsqrt(jnp.mean(out * out, -1, keepdims=True) + 1e-05)
        scaled = out * scale
        gate = pre_ref[:, head_columns(width, 3, head)]
        gate_open = jax.nn.sigmoid(gate)
        gain = param_ref[KERNEL : KERNEL + 1, columns]
        gated = d_mixed * (gate * gate_open)
        d_param_ref[KERNEL : KERNEL + 1, columns] += jnp.sum(gated * scaled, 0, keepdims=True)
        d_gate = d_mixed * scaled * gain * (gate_open * (1.0 + gate * (1.0 - gate_open)))
        d_pre_ref[:, head_columns(width, 3, head)] = d_gate.astype(bf)
        d_scaled = gated * gain
        mean = jnp.mean(d_scaled * out, -1, keepdims=True)
        d_outs.append(scale * d_scaled - out * (scale * scale * scale * mean))
    d_out_halves = [halves(value) for value in d_outs]
    solved_halves = [halves(solved_ref[head]) for head in heads]
    d_solved = [exact(score_ref[head], d_out_halves[head], 0, 0) for head in heads]
    d_scores = [
        exact(d_out_halves[head], solved_halves[head], 1, 1) * tile.lower_full for head in heads
    ]
    d_inner = [exact(inverse_ref[head], d_solved[head], 0, 0) for head in heads]
    d_lowers = [exact(d_inner[head], solved_halves[head], 1, 1) * -tile.lower for head in heads]
    d_beta = jnp.zeros((GROUP_ROWS, SMALL), f32)
    for head in heads:
        pres, convolved, opened, active = [], [], [], []
        for section in range(3):
            columns = head_columns(width, section, head)
            taps = [param_ref[offset : offset + 1, columns] for offset in range(KERNEL)]
            pres.append(pre_ref[:, columns])
            convolved.append(convolve(tile, pres[section], taps))
            opened.append(jax.nn.sigmoid(convolved[section]))
            active.append(convolved[section] * opened[section])
        query_scale = unit_scale(active[0])
        key_scale = unit_scale(active[1])
        query_unit = active[0] * query_scale
        key = active[1] * key_scale
        start = 4 * width + head
        opening = jax.nn.sigmoid(pre_ref[:, start : start + 1])
        strength = opening * tile.live
        d_both = stacked(halves(d_lowers[head]), halves(d_scores[head]))
        by_key = exact(d_both, key, 1, 0)
        d_query = by_key[GROUP_ROWS:] * HEAD_DIM**-0.5
        from_lower = by_key[:GROUP_ROWS]
        weighted = stacked(halves(key * strength), halves(query_unit * HEAD_DIM**-0.5))
        d_key = strength * from_lower + exact(d_both, weighted, 0, 0)
        d_strength = along(d_inner[head] * active[2] + from_lower * key)
        d_value = d_inner[head] * strength
        d_opening = d_strength * (opening * (1.0 - opening)) * tile.live
        d_beta = d_beta + jnp.where(tile.col == head, d_opening, 0.0)
        d_active = [
            (d_query - query_unit * along(query_unit * d_query)) * query_scale,
            (d_key - key * along(key * d_key)) * key_scale,
            d_value,
        ]
        for section in range(3):
            columns = head_columns(width, section, head)
            taps = [param_ref[offset : offset + 1, columns] for offset in range(KERNEL)]
            slope = opened[section] * (1.0 + convolved[section] * (1.0 - opened[section]))
            d_convolved = d_active[section] * slope
            d_pre = d_convolved * taps[0]
            sums = [jnp.sum(d_convolved * pres[section], 0, keepdims=True)]
            for offset in range(1, KERNEL):
                d_pre = d_pre + tile.later(d_convolved, offset) * taps[offset]
                sums.append(
                    jnp.sum(d_convolved * tile.earlier(pres[section], offset), 0, keepdims=True)
                )
            d_param_ref[0:KERNEL, columns] += jnp.concatenate(sums, 0)
            d_pre_ref[:, columns] = d_pre.astype(bf)
    d_pre_ref[:, 4 * width :] = d_beta.astype(bf)


NO_COST = pl.CostEstimate(flops=0, bytes_accessed=0, transcendentals=0)


def call(kernel, operands, in_specs, out_specs, out_shape, grid=(), scratch=(), micros=0):
    results = pl.pallas_call(
        kernel,
        grid=grid,
        in_specs=in_specs,
        out_specs=out_specs,
        out_shape=out_shape,
        scratch_shapes=scratch,
        compiler_params=pltpu.CompilerParams(
            dimension_semantics=("arbitrary",) * len(grid), vmem_limit_bytes=48 * 2**20
        ),
        cost_estimate=pl.CostEstimate(
            flops=micros * 10**9, bytes_accessed=0, transcendentals=0
        ),
    )(*operands)
    return list(results)


def whole(array):
    return pl.BlockSpec(array.shape, lambda *step: (0,) * len(array.shape))


def mixer_specs(width):
    wide = 4 * width + SMALL
    heads = width // HEAD_DIM
    layout = pl.BlockSpec(memory_space=pltpu.SMEM)
    pre = pl.BlockSpec((GROUP_ROWS, wide), lambda group: (group, 0))
    param = pl.BlockSpec((2 * KERNEL, 3 * width), lambda group: (0, 0))
    narrow = pl.BlockSpec((GROUP_ROWS, width), lambda group: (group, 0))
    square = pl.BlockSpec((heads, GROUP_ROWS, HEAD_DIM), lambda group: (group, 0, 0))
    return layout, pre, param, narrow, square


def mixer_forward(layout, pre, params, width):
    groups = layout.shape[0]
    layout_spec, pre_spec, param_spec, narrow, square = mixer_specs(width)
    squares = pltpu.HBM((groups * width // HEAD_DIM, GROUP_ROWS, HEAD_DIM), f32)
    return call(
        mixer_forward_kernel,
        [layout, pre, params],
        [layout_spec, pre_spec, param_spec],
        [narrow] + [square] * 4,
        [jax.ShapeDtypeStruct((groups * GROUP_ROWS, width), bf)] + [squares] * 4,
        (groups,),
    )


def mixer_backward(layout, pre, params, weight, d_mixed, kept, width):
    groups = layout.shape[0]
    layout_spec, pre_spec, param_spec, _, square = mixer_specs(width)
    kept = [pltpu.with_memory_space_constraint(array, pltpu.HBM) for array in kept]
    return call(
        mixer_backward_kernel,
        [layout, pre, params, weight, *kept, *d_mixed],
        [layout_spec, pre_spec, param_spec, whole(weight)]
        + [square] * 4
        + [whole(block) for block in d_mixed],
        [pre_spec, param_spec],
        [jax.ShapeDtypeStruct(pre.shape, bf), jax.ShapeDtypeStruct(params.shape, f32)],
        (groups,),
        [pltpu.VMEM((GROUP_ROWS, width), f32)],
        micros=60,
    )


def first_kernel(gain_ref, weight_ref, *refs):
    *value_refs, normed_ref, out_ref, scale_ref, total_ref = refs
    step, depth = pl.program_id(0), weight_ref.shape[0]

    @pl.when(step == 0)
    def _():
        for group, ref in enumerate(value_refs):
            values = ref[...].astype(f32)
            scale = lax.rsqrt(jnp.mean(values * values, -1, keepdims=True) + 1e-06)
            rows = pl.ds(group * GROUP_ROWS, GROUP_ROWS)
            scale_ref[rows, :] = jnp.broadcast_to(scale, (GROUP_ROWS, 128))
        total_ref[...] = jnp.zeros_like(total_ref)

    columns = pl.ds(pl.multiple_of(step * depth, depth), depth)
    for group, ref in enumerate(value_refs):
        rows = pl.ds(group * GROUP_ROWS, GROUP_ROWS)
        values = ref[:, columns].astype(f32) * scale_ref[rows, :1] * gain_ref[...]
        normed_ref[rows, :] = values.astype(bf)
    total_ref[...] += plain_product(normed_ref[...], weight_ref[...])

    @pl.when(step == pl.num_programs(0) - 1)
    def _():
        out_ref[...] = total_ref[...]


def normed_product(blocks, gain, weight, depth=512):
    rows, (features, columns) = len(blocks) * GROUP_ROWS, weight.shape
    return call(
        first_kernel,
        [gain, weight, *blocks],
        [
            pl.BlockSpec((1, depth), lambda step: (0, step)),
            pl.BlockSpec((depth, columns), lambda step: (step, 0)),
        ]
        + [whole(block) for block in blocks],
        [
            pl.BlockSpec((rows, depth), lambda step: (0, step)),
            pl.BlockSpec((rows, columns), lambda step: (0, 0)),
        ],
        [
            jax.ShapeDtypeStruct((rows, features), bf),
            jax.ShapeDtypeStruct((rows, columns), f32),
        ],
        (features // depth,),
        [pltpu.VMEM((rows, 128), f32), pltpu.VMEM((rows, columns), f32)],
    )


def product_blocks(left, right, transposed=False, block=512, micros=0):
    product = transposed_product if transposed else plain_product
    columns = right.shape[0] if transposed else right.shape[1]
    groups = left.shape[0] // GROUP_ROWS

    def kernel(left_ref, right_ref, *out_refs):
        total = product(left_ref[...], right_ref[...])
        for group, ref in enumerate(out_refs):
            ref[...] = total[group * GROUP_ROWS : (group + 1) * GROUP_ROWS].astype(ref.dtype)

    if transposed:
        right_spec = pl.BlockSpec((block, right.shape[1]), lambda step: (step, 0))
    else:
        right_spec = pl.BlockSpec((right.shape[0], block), lambda step: (0, step))
    return call(
        kernel,
        [left, right],
        [whole(left), right_spec],
        [pl.BlockSpec((GROUP_ROWS, block), lambda step: (0, step))] * groups,
        [
            jax.ShapeDtypeStruct((GROUP_ROWS, columns), bf if group else f32)
            for group in range(groups)
        ],
        (columns // block,),
        micros=micros,
    )


def grad_product(left, right, block=256, micros=0):
    rows, features = left.shape
    if features % block:
        block = 128

    def kernel(left_ref, right_ref, out_ref):
        out_ref[...] = rows_product(left_ref[...], right_ref[...]).astype(bf)

    return call(
        kernel,
        [left, right],
        [pl.BlockSpec((rows, block), lambda step: (0, step)), whole(right)],
        [pl.BlockSpec((block, right.shape[1]), lambda step: (step, 0))],
        [pltpu.HBM((features, right.shape[1]), bf)],
        (features // block,),
        micros=micros,
    )[0]


def from_own(part, values):
    groups = values.shape[0] // GROUP_ROWS

    def kernel(part_ref, values_ref, out_ref):
        for step in range(groups):
            source = lax.rem(part_ref[0] + groups - step, groups) * GROUP_ROWS
            rows = pl.ds(pl.multiple_of(source, GROUP_ROWS), GROUP_ROWS)
            out_ref[step * GROUP_ROWS : (step + 1) * GROUP_ROWS] = values_ref[rows]

    return call(
        kernel,
        [part.reshape(1).astype(jnp.int32), values],
        [pl.BlockSpec(memory_space=pltpu.SMEM), whole(values)],
        [whole(values)],
        [jax.ShapeDtypeStruct(values.shape, values.dtype)],
        (1,),
    )[0]


def tie_all(values, *others):
    anywhere = pl.BlockSpec(memory_space=pl.ANY)
    others = [
        pltpu.with_memory_space_constraint(other, pltpu.HBM) if other.size > 2**21 else other
        for other in others
    ]
    tied = pl.pallas_call(
        lambda *refs: None,
        in_specs=[anywhere] * (len(values) + len(others)),
        out_specs=[anywhere] * len(values),
        out_shape=[
            (pltpu.HBM if value.size > 2**21 else jax.ShapeDtypeStruct)(value.shape, value.dtype)
            for value in values
        ],
        input_output_aliases={i: i for i in range(len(values))},
        cost_estimate=NO_COST,
    )(*values, *others)
    return list(tied)


def tie(value, *others):
    return tie_all([value], *others)[0]


def assemble(part, values, received, others):
    parts = values.shape[0]

    def kernel(part_ref, values_ref, *refs):
        own = part_ref[0]
        out_ref = refs[-1]
        out_ref[own] = values_ref[own]
        for step in range(1, parts):
            out_ref[lax.rem(own + parts - step, parts)] = refs[step - 1][...]

    vmem = pl.BlockSpec(memory_space=pltpu.VMEM)
    anywhere = pl.BlockSpec(memory_space=pl.ANY)
    return pl.pallas_call(
        kernel,
        in_specs=[pl.BlockSpec(memory_space=pltpu.SMEM)]
        + [vmem] * parts
        + [anywhere] * len(others),
        out_specs=vmem,
        out_shape=jax.ShapeDtypeStruct(values.shape, values.dtype),
        compiler_params=pltpu.CompilerParams(vmem_limit_bytes=32 * 2**20),
        cost_estimate=NO_COST,
    )(part.reshape(1).astype(jnp.int32), values, *received, *others)


def copy_columns(count, *refs):
    target = refs[-1]
    start = 0
    for source in refs[:count]:
        block = source[...].reshape(source.shape[-2:])
        columns = pl.ds(start, block.shape[1])
        if len(target.shape) == 3:
            target[0, :, columns] = block.astype(target.dtype)
        else:
            target[:, columns] = block.astype(target.dtype)
        start += block.shape[1]


def to_parts(sources, parts, dtype, others=()):
    rows = sources[0][0].shape[0]

    def spec(section, width):
        return pl.BlockSpec((rows, width), lambda p: (0, section * parts + p))

    total = sum(width for _, _, width in sources)
    return pl.pallas_call(
        functools.partial(copy_columns, len(sources)),
        grid=(parts,),
        in_specs=[spec(section, width) for _, section, width in sources]
        + [pl.BlockSpec(memory_space=pl.ANY)] * len(others),
        out_specs=pl.BlockSpec((1, rows, total), lambda p: (p, 0, 0)),
        out_shape=jax.ShapeDtypeStruct((parts, rows, total), dtype),
        cost_estimate=NO_COST,
    )(*[array for array, _, _ in sources], *others)


def updown_from_parts(slabs):
    parts, rows, width = slabs.shape
    units = width // 2

    def kernel(slabs_ref, out_ref):
        for p in range(parts):
            out_ref[:, p * units : (p + 1) * units] = slabs_ref[p].astype(f32)

    return pl.pallas_call(
        kernel,
        grid=(2,),
        in_specs=[pl.BlockSpec((parts, rows, units), lambda half: (0, 0, half))],
        out_specs=pl.BlockSpec((rows, parts * units), lambda half: (0, half)),
        out_shape=jax.ShapeDtypeStruct((rows, parts * width), f32),
        compiler_params=pltpu.CompilerParams(vmem_limit_bytes=32 * 2**20),
        cost_estimate=NO_COST,
    )(slabs)


def mixer_from_parts(slabs, width):
    parts, rows, _ = slabs.shape

    def kernel(slabs_ref, qkv_ref, gate_ref, strength_ref):
        for p in range(parts):
            for section in range(4):
                block = slabs_ref[p, :, section * width : (section + 1) * width].astype(f32)
                if section < 3:
                    start = (section * parts + p) * width
                    qkv_ref[:, start : start + width] = block
                else:
                    gate_ref[:, p * width : (p + 1) * width] = block
            last = slabs_ref[p, :, 4 * width :].astype(f32)
            strength_ref[:, p * SMALL : (p + 1) * SMALL] = last

    widths = [3 * parts * width, parts * width, parts * SMALL]
    return pl.pallas_call(
        kernel,
        out_shape=[jax.ShapeDtypeStruct((rows, size), f32) for size in widths],
        compiler_params=pltpu.CompilerParams(vmem_limit_bytes=32 * 2**20),
        cost_estimate=NO_COST,
    )(slabs)


def own_order(values, parts, copies):
    size = values.shape[1] // (parts * copies)
    pieces = [
        values[:, (t * parts + m) * size : (t * parts + m + 1) * size]
        for m in range(parts)
        for t in range(copies)
    ]
    return jnp.concatenate(pieces, 1)


def total_of(own_ref, received_refs):
    total = own_ref[...]
    for ref in received_refs:
        total = total + ref[...].astype(f32)
    return total


def row_scale(values):
    return lax.rsqrt(jnp.mean(values * values, -1, keepdims=True) + 1e-06)


def norm_slope(values, scale, gain, grad):
    mean = jnp.mean(gain * grad * values, -1, keepdims=True)
    return scale * gain * grad - values * (scale * scale * scale * mean)


def hidden_kernel(own_ref, *refs):
    *received, input_ref, gain_ref, hidden_ref, normed_ref = refs
    hidden = input_ref[...].astype(f32) + total_of(own_ref, received)
    hidden_ref[...] = hidden
    normed_ref[...] = (hidden * row_scale(hidden) * gain_ref[...]).astype(bf)


def hidden_back_kernel(own_ref, *refs):
    *received, hidden_ref, gain_ref, cot_ref, d_hidden_ref, d_mixed_ref, d_gain_ref = refs
    grad = total_of(own_ref, received)
    hidden = hidden_ref[...]
    scale = row_scale(hidden)

    @pl.when(pl.program_id(0) == 0)
    def _():
        d_gain_ref[...] = jnp.zeros_like(d_gain_ref)

    d_gain_ref[...] += jnp.sum(grad * hidden * scale, 0, keepdims=True)
    d_hidden = cot_ref[...].astype(f32) + norm_slope(hidden, scale, gain_ref[...], grad)
    d_hidden_ref[...] = d_hidden
    d_mixed_ref[...] = d_hidden.astype(bf)


def input_back_kernel(parts, copies, own_ref, *refs):
    *received, input_ref, gain_ref, d_hidden_ref, out_ref = refs
    grad = total_of(own_ref, received)
    values = input_ref[...].astype(f32)
    slope = norm_slope(values, row_scale(values), gain_ref[...], grad)
    out_ref[...] = own_order(d_hidden_ref[...] + slope, parts, copies).astype(bf)


def block_out_kernel(parts, copies, own_ref, *refs):
    *received, hidden_ref, out_ref = refs
    total = hidden_ref[...] + total_of(own_ref, received)
    out_ref[...] = own_order(total, parts, copies).astype(bf)


def last_sum(sides, others, parts, copies):
    rows, columns = sides[0].shape

    def kernel(*refs):
        first, first_other, second, second_other = (ref[...].astype(f32) for ref in refs[:4])
        total = jnp.concatenate([first + first_other, second + second_other], 1)
        refs[-1][...] = own_order(total, parts, copies)

    vmem = pl.BlockSpec(memory_space=pltpu.VMEM)
    return pl.pallas_call(
        kernel,
        in_specs=[vmem] * 4 + [pl.BlockSpec(memory_space=pl.ANY)] * len(others),
        out_specs=vmem,
        out_shape=jax.ShapeDtypeStruct((rows, 2 * columns), f32),
        compiler_params=pltpu.CompilerParams(vmem_limit_bytes=32 * 2**20),
        cost_estimate=NO_COST,
    )(*sides, *others)


def by_rows(kernel, arrays, outs, block=64):
    def spec(shape):
        if shape[0] == 1:
            return pl.BlockSpec(shape, lambda i: (0, 0))
        return pl.BlockSpec((block, shape[1]), lambda i: (i, 0))

    return pl.pallas_call(
        kernel,
        grid=(GROUP_ROWS // block,),
        in_specs=[spec(array.shape) for array in arrays],
        out_specs=[spec(shape) for shape, _ in outs],
        out_shape=[jax.ShapeDtypeStruct(shape, dtype) for shape, dtype in outs],
        compiler_params=pltpu.CompilerParams(dimension_semantics=("arbitrary",)),
        cost_estimate=NO_COST,
    )(*arrays)


def body(
    block_in,
    out_grad,
    norm1_gain,
    conv_weight,
    head_gain,
    qkv_weight,
    beta_weight,
    gate_weight,
    out_weight,
    norm2_gain,
    updown_weight,
    down_weight,
    seq_blocks,
    lead_blocks,
):
    devices = lax.axis_size("dp")
    parts = MODEL
    copies = devices // parts
    part = lax.axis_index("dp") // copies
    copy = lax.axis_index("dp") % copies
    rows_own = qkv_weight.shape[0]
    width = D // parts
    units = FF // parts
    heads_part = HEADS // parts
    wide = 4 * width + SMALL
    model_groups = [[m * copies + t for m in range(parts)] for t in range(copies)]
    copy_groups = [[m * copies + t for t in range(copies)] for m in range(parts)]

    def exchange(values):
        return lax.all_to_all(
            values, "dp", split_axis=0, concat_axis=0, axis_index_groups=model_groups, tiled=True
        )

    def shift(values, step):
        pairs = [
            (m * copies + t, (m + step) % parts * copies + t)
            for m in range(parts)
            for t in range(copies)
        ]
        return lax.ppermute(values, "dp", pairs)

    def exchange_apart(values, before, after=()):
        cut = [
            lax.dynamic_index_in_dim(values, (part + step) % parts, 0, keepdims=False)
            for step in range(1, parts)
        ]
        received = [shift(piece, step) for step, piece in enumerate(tie_all(cut, *before), 1)]
        return assemble(part, values, received, after)

    def gather_rows(values):
        return [values] + [shift(values, step) for step in range(1, parts)]

    def scatter_rows(terms):
        return [terms[0]] + [shift(block, -step) for step, block in enumerate(terms[1:], 1)]

    def gather_copies(values):
        return lax.all_gather(values, "dp", axis=0, axis_index_groups=copy_groups, tiled=True)

    def scatter_copies(values):
        return lax.psum_scatter(
            values.astype(bf),
            "dp",
            scatter_dimension=0,
            axis_index_groups=copy_groups,
            tiled=True,
        )

    def halves_across(values, bit, axis):
        pairs = [(i, i ^ (1 << bit)) for i in range(devices)]
        side = (copy >> bit) & 1
        own = lax.dynamic_index_in_dim(values, side, axis, keepdims=False)
        other = lax.dynamic_index_in_dim(values, 1 - side, axis, keepdims=False)
        return own, lax.ppermute(other, "dp", pairs)

    def halve(values, bit, axis, *others):
        own, received = halves_across(values, bit, axis)
        if others:
            received = tie(received, *others)
        return (own.astype(f32) + received.astype(f32)).astype(bf)

    by_halves = copies == 8

    def halve_cores(values, *others):
        if not by_halves:
            return values
        rows, columns = values.shape
        return halve(values.reshape(2, 2, 2, rows // 8, columns), 0, 2, *others)

    def halve_first(values):
        if not by_halves:
            return [values]
        middle = values.shape[-1] // 2
        return [halve(values[..., :middle], 1, 1), halve(values[..., middle:], 2, 0)]

    def halve_second(values, *others):
        if not by_halves:
            return from_wire(scatter_copies(values[0]).astype(f32))
        sides = halves_across(values[0], 2, 0) + halves_across(values[1], 1, 0)
        return last_sum(sides, others, parts, copies)

    def to_wire(values):
        return values.reshape(-1, parts, copies, rows_own).swapaxes(1, 2).reshape(-1, D)

    def from_wire(values):
        return values.reshape(-1, copies, parts, rows_own).swapaxes(1, 2).reshape(-1, D)

    w_out_own = to_wire(out_weight.astype(bf))
    w_out = gather_copies(w_out_own)
    strengths = beta_weight.reshape(rows_own, parts, heads_part)
    strengths = jnp.pad(strengths, ((0, 0), (0, 0), (0, SMALL - heads_part)))
    strengths = tie(strengths.reshape(rows_own, parts * SMALL), w_out_own)
    pieces = [(qkv_weight, section, width) for section in range(3)]
    pieces = to_parts(pieces + [(gate_weight, 0, width), (strengths, 0, SMALL)], parts, bf)
    mixer_pieces = tie(exchange(pieces), w_out)
    w_mixer = gather_copies(mixer_pieces.reshape(parts * rows_own, wide))
    inputs = tie(to_wire(block_in), mixer_pieces)
    input_rows = gather_rows(inputs)

    lanes = -(-3 * rows_own // 128) * 128
    numbers = jnp.concatenate([seq_blocks[0], lead_blocks]).astype(f32)
    small = [conv_weight.T, norm1_gain[None], head_gain[None], norm2_gain[None], numbers[None]]
    small = [jnp.pad(rows, ((0, 0), (0, lanes - rows.shape[1]))) for rows in small]
    small = jnp.pad(jnp.concatenate(small, 0).astype(bf), ((0, 2 * KERNEL), (0, 0)))
    small = jnp.broadcast_to(small[None], (devices,) + small.shape)
    small = lax.all_to_all(tie(small, *input_rows[1:]), "dp", 0, 0, tiled=True)
    taps = small[:, :KERNEL, : 3 * rows_own].swapaxes(0, 1).reshape(KERNEL, 3, parts, width)
    taps = lax.dynamic_index_in_dim(taps, part, 2, keepdims=False).reshape(KERNEL, 3 * width)
    gain_one, head_full, gain_two = (
        small[:, KERNEL + i, :rows_own].reshape(1, D).astype(f32) for i in range(3)
    )
    gain_one, gain_two = to_wire(gain_one), to_wire(gain_two)
    head_part = lax.dynamic_slice_in_dim(head_full, part * width, width, 1)
    params = jnp.concatenate([taps.astype(f32), jnp.pad(head_part, ((0, 0), (0, 2 * width)))], 0)
    params = jnp.pad(params, ((0, KERNEL - 1), (0, 0)))
    numbers = small[:, KERNEL + 3, :3].astype(f32).astype(jnp.int32)
    layouts = block_layouts(numbers[:, 0], numbers[:, 1], numbers[:, 2])
    layouts = layouts.reshape(parts, copies, 4)
    layouts = lax.dynamic_index_in_dim(layouts, copy, 1, keepdims=False)
    wanted = (part - jnp.arange(parts)) % parts
    wanted = (wanted[:, None] == jnp.arange(parts)).astype(f32)
    layouts = jnp.sum(wanted[:, :, None] * layouts, 1)

    pieces = [(updown_weight, half, units) for half in range(2)]
    updown_pieces = to_parts(pieces, parts, bf, [mixer_pieces])
    w_down_own = to_wire(down_weight.astype(bf))
    w_down = gather_copies(tie(w_down_own, *input_rows[1:]))
    cotangent_own = to_wire(out_grad)

    cotangent = lax.all_gather(
        tie(cotangent_own, *input_rows[1:]), "dp", axis=0, axis_index_groups=model_groups, tiled=True
    )
    gain_first = tie(gain_one, w_down_own, cotangent_own, updown_pieces)
    normed, pre = normed_product(input_rows, gain_first, w_mixer)
    mixed, *kept = mixer_forward(layouts, pre, params, width)
    out_terms = product_blocks(mixed, w_out)
    updown_pieces = exchange_apart(updown_pieces, input_rows[1:], out_terms[1:])
    w_updown = gather_copies(updown_pieces.reshape(parts * rows_own, 2 * units))
    stream = ((GROUP_ROWS, D), f32)
    narrow = ((GROUP_ROWS, D), bf)
    hidden, normed_two = by_rows(
        hidden_kernel,
        scatter_rows(out_terms) + [inputs, gain_two],
        [stream, narrow],
    )
    cotangent = from_own(part, cotangent)
    normed_two = jnp.concatenate(gather_rows(normed_two), 0)

    def swiglu_units(updown):
        return jax.nn.silu(updown[:, :units]) * updown[:, units:]

    updown = plain_product(normed_two, w_updown)
    active, swiglu_back = jax.vjp(swiglu_units, updown)
    active = active.astype(bf)
    d_active = transposed_product(cotangent, w_down)
    d_updown = swiglu_back(d_active)[0].astype(bf)
    d_normed_two = product_blocks(d_updown, w_updown, transposed=True)
    active = tie(active, *d_normed_two[1:])
    down_terms = grad_product(active, cotangent)
    updown_terms = grad_product(normed_two, tie(d_updown, down_terms))
    gain_late = tie(gain_two, updown_terms)
    d_normed_two = scatter_rows(d_normed_two)
    updown_grad = scatter_copies(tie(updown_terms, gain_late, *d_normed_two[1:]))
    d_hidden, d_mixed, gain_two_grad = by_rows(
        hidden_back_kernel,
        d_normed_two + [hidden, gain_late, cotangent_own],
        [stream, narrow, ((1, D), f32)],
    )


    out_terms = product_blocks(tie(active, d_mixed), w_down)
    down_terms = tie(down_terms, *out_terms[1:])
    d_mixed = gather_rows(d_mixed)
    late = tie(params, *out_terms)
    out_terms[1:] = tie_all(out_terms[1:], *d_mixed[1:])
    d_pre, d_params = mixer_backward(layouts, pre, late, w_out, d_mixed, kept, width)
    mixer_terms = tie(grad_product(normed, d_pre, micros=20), updown_grad)
    mixer_grad = scatter_copies(mixer_terms)

    d_normed_terms = product_blocks(
        tie(d_pre, mixer_terms), w_mixer, transposed=True, micros=150
    )
    hidden = tie(hidden, d_normed_terms[0])
    (block_out,) = by_rows(
        functools.partial(block_out_kernel, parts, copies),
        scatter_rows(out_terms) + [hidden],
        [narrow],
    )
    d_normed_terms[1:] = tie_all(d_normed_terms[1:], block_out)
    d_normed = scatter_rows(d_normed_terms)
    down_grad = halve_first(halve_cores(down_terms, *d_normed_terms[1:]))
    gain_one_grad = 0.0
    for values, terms in zip(input_rows, d_normed_terms):
        values = values.astype(f32)
        terms = terms.astype(f32) * (values * row_scale(values))
        gain_one_grad = gain_one_grad + jnp.sum(terms, 0, keepdims=True)

    d_params = tie(d_params, mixer_terms)
    here = (jnp.arange(parts) == part).astype(f32)[:, None]
    taps_grad = d_params[:KERNEL].reshape(KERNEL, 3, 1, width) * here
    taps_grad = taps_grad.reshape(KERNEL, parts, copies, 3, rows_own).transpose(1, 2, 3, 0, 4)
    taps_grad = taps_grad.reshape(devices, 3 * KERNEL, rows_own)
    head_grad = (d_params[KERNEL, :width] * here).reshape(devices, 1, rows_own)
    gain_grads = [
        grad.reshape(copies, parts, 1, rows_own).swapaxes(0, 1).reshape(devices, 1, rows_own)
        for grad in (gain_one_grad, gain_two_grad)
    ]
    small_grad = jnp.concatenate([taps_grad, head_grad] + gain_grads, 1)
    small_grad = jnp.pad(small_grad, ((0, 0), (0, 1), (0, 128 - rows_own)))
    small_grad = jnp.sum(lax.all_to_all(small_grad, "dp", 0, 0, tiled=True), 0)[:, :rows_own]
    taps_shard = small_grad[: 3 * KERNEL].reshape(3, KERNEL, rows_own).swapaxes(1, 2)
    taps_shard = taps_shard.reshape(3 * rows_own, KERNEL)
    head_shard, gain_one_shard, gain_two_shard = small_grad[3 * KERNEL : 3 * KERNEL + 3]

    out_grads = grad_product(tie(mixed, d_normed_terms[0]), jnp.concatenate(d_mixed, 0))
    late = tie(gain_one, out_grads)
    (input_grad,) = by_rows(
        functools.partial(input_back_kernel, parts, copies),
        d_normed + [inputs, late, d_hidden],
        [narrow],
    )
    updown_grad = tie(updown_grad, mixer_terms).reshape(parts, rows_own, 2 * units)
    updown_grad = exchange(updown_grad)
    mixer_grad = tie(mixer_grad, updown_grad, input_grad)
    updown_shard = updown_from_parts(updown_grad)
    down_shard = halve_second(tie_all(down_grad, input_grad), mixer_grad)
    out_grads = tie(halve_cores(tie(out_grads, input_grad)), mixer_grad)
    out_shard = halve_second(halve_first(out_grads))
    mixer_grad = exchange(mixer_grad.reshape(parts, rows_own, wide))
    qkv_shard, gate_shard, strengths = mixer_from_parts(mixer_grad, width)
    beta_shard = strengths.reshape(rows_own, parts, SMALL)[:, :, :heads_part]
    return (
        block_out,
        input_grad,
        gain_one_shard,
        taps_shard,
        head_shard,
        qkv_shard,
        beta_shard.reshape(rows_own, HEADS),
        gate_shard,
        out_shard,
        gain_two_shard,
        updown_shard,
        down_shard,
    )


def solution(mesh):
    placed = (
        P("dp", None),
        P("dp", None),
        P("dp"),
        P("dp", None),
        P("dp"),
        P("dp", None),
        P("dp", None),
        P("dp", None),
        P("dp", None),
        P("dp"),
        P("dp", None),
        P("dp", None),
        P("dp", None),
        P("dp"),
    )
    return jax.shard_map(
        body,
        mesh=mesh,
        in_specs=placed,
        out_specs=(
            P("dp", None),
            P("dp", None),
            P("dp"),
            P("dp", None),
            P("dp"),
            P("dp", None),
            P("dp", None),
            P("dp", None),
            P("dp", None),
            P("dp"),
            P("dp", None),
            P("dp", None),
        ),
        check_vma=False,
    )
```

profile of v0, /device:TPU:0, one launch (start us, length us, event | category | flops | bytes accessed | tf_op | source)
XLA Modules:
  0.0 609.4 jit_solution(14648002925529518718)
XLA Ops:
  14.8 33.6 %all_to_all.25.refs_0_ = bf16[4,64,2176]{2,1,0:T(8,128)(2,1)} all-to-all(bf16[4,64,2176]{2,1,0:T(8,128)(2,1)} %shard_map.230), channel_id=1, replica_groups={{0,8,16,24},{1,9,17,25},{2,10,18,26},{3,11,19,27},{4,12,20,28},{5,13,21..., dimensions={0} | all-to-all | bytes 2228224 | tf_op jit(solution)/shard_map/all_to_all | solution.py:706
  56.0 11.7 %collective-permute-done.refs_1_.refs_3_ = bf16[128,2048]{1,0:T(8,128)(2,1)S(1)} collective-permute-done((bf16[128,2048]{1,0:T(8,128)(2,1)}, bf16[128,2048]{1,0:T(8,128)(2,1)S(1)}, u32[]{:S(2)}, u32[]{:S(2)}) %collective-permute-start) | collective-permute-done | bytes 524320 | tf_op jit(solution)/shard_map/ppermute | solution.py:716
  67.7 20.5 %collective-permute-done.1.refs_2_.refs_4_ = bf16[128,2048]{1,0:T(8,128)(2,1)S(1)} collective-permute-done((bf16[128,2048]{1,0:T(8,128)(2,1)}, bf16[128,2048]{1,0:T(8,128)(2,1)S(1)}, u32[]{:S(2)}, u32[]{:S(2)}) %collective-permute-start.1) | collective-permute-done | bytes 524320 | tf_op jit(solution)/shard_map/ppermute | solution.py:716
  94.5 12.8 %all-to-all-start.1 = ((bf16[32,16,256]{2,1,0:T(8,128)(2,1)}), bf16[32,16,256]{2,1,0:T(8,128)(2,1)S(1)}, u32[]{:S(2)}, u32[]{:S(2)}) async-start(bf16[32,16,256]{2,1,0:T(8,128)(2,1)} %shard_map.233), calls=%async_computation.1 | async-start | bytes 524288 | tf_op jit(solution)/shard_map/all_to_all | solution.py:801
  123.8 10.9 %shard_map.236 = (bf16[512,2048]{1,0:T(8,128)(2,1)S(1)}, f32[512,2176]{1,0:T(8,128)}) custom-call(f32[1,2048]{1,0:T(1,128)S(1)} %copy-done.56, bf16[2048,2176]{1,0:T(8,128)(2,1)} %all-gather.8.cloned.1.call-done.weight_ref.right_ref, bf16[128,2048]{1,0:T(8,128)(2,1)S(1)} %copy-done.2, bf16[128,2048]{1,0:T(8,128)(2,1)S(1)} %copy-done.6, ...), custom_call_target="tpu_custom_call" | custom-call | tf_op jit(solution)/shard_map/pallas_call | solution.py:277
  138.3 14.7 %shard_map.237 = (bf16[512,512]{1,0:T(8,128)(2,1)S(1)}, f32[16,128,128]{2,1,0:T(8,128)}, f32[16,128,128]{2,1,0:T(8,128)}, f32[16,128,128]{2,1,0:T(8,128)}, f32[16,128,128]{2,1,0:T(8,128)}) custom-call(f32[4,4]{1,0:T(4,128)S(1)} %multiply_reduce_fusion.layout_ref, f32[512,2176]{1,0:T(8,128)S(1)} %copy-done.37, f32[8,1536]{1,0:T(8,128)S(1)} %pad.57.param_ref.refs_0_), custom_call_target="tpu_custom_call" | custom-call | tf_op jit(solution)/shard_map/pallas_call | solution.py:277
  155.1 5.3 collective-permute-done.10.refs_1_
  164.4 20.4 %collective-permute-start.3 = (bf16[128,2048]{1,0:T(8,128)(2,1)S(1)}, bf16[128,2048]{1,0:T(8,128)(2,1)S(1)}, u32[]{:S(2)}, u32[]{:S(2)}) collective-permute-start(bf16[128,2048]{1,0:T(8,128)(2,1)S(1)} %get-tuple-element.59.refs_3_), channel_id=1, source_target_pairs={{0,24},{1,25},{2,26},{3,27},{4,28},{5,29},{6,30},{7,31},{8,0},{9,1... | collective-permute-start | bytes 1572872 | tf_op jit(solution)/shard_map/ppermute | solution.py:716
  186.2 11.1 %collective-permute-done.3.refs_0_ = bf16[128,2048]{1,0:T(8,128)(2,1)S(1)} collective-permute-done((bf16[128,2048]{1,0:T(8,128)(2,1)S(1)}, bf16[128,2048]{1,0:T(8,128)(2,1)S(1)}, u32[]{:S(2)}, u32[]{:S(2)}) %collective-permute-start.3) | collective-permute-done | bytes 524320 | tf_op jit(solution)/shard_map/ppermute | solution.py:716
  197.2 33.6 %collective-permute-done.4.refs_1_ = bf16[128,2048]{1,0:T(8,128)(2,1)S(1)} collective-permute-done((bf16[128,2048]{1,0:T(8,128)(2,1)S(1)}, bf16[128,2048]{1,0:T(8,128)(2,1)S(1)}, u32[]{:S(2)}, u32[]{:S(2)}) %collective-permute-start.4) | collective-permute-done | bytes 524320 | tf_op jit(solution)/shard_map/ppermute | solution.py:716
  242.3 9.7 %collective-permute-done.6 = bf16[128,2048]{1,0:T(8,128)(2,1)S(1)} collective-permute-done((bf16[128,2048]{1,0:T(8,128)(2,1)}, bf16[128,2048]{1,0:T(8,128)(2,1)S(1)}, u32[]{:S(2)}, u32[]{:S(2)}) %collective-permute-start.6) | collective-permute-done | bytes 524320 | tf_op jit(solution)/shard_map/ppermute | solution.py:716
  252.8 19.8 %collective-permute-done.7 = bf16[128,2048]{1,0:T(8,128)(2,1)S(1)} collective-permute-done((bf16[128,2048]{1,0:T(8,128)(2,1)}, bf16[128,2048]{1,0:T(8,128)(2,1)S(1)}, u32[]{:S(2)}, u32[]{:S(2)}) %collective-permute-start.7) | collective-permute-done | bytes 524320 | tf_op jit(solution)/shard_map/ppermute | solution.py:716
  274.3 13.4 %fusion.30 = f32[512,2816]{1,0:T(8,128)} fusion(bf16[512,2048]{1,0:T(8,128)(2,1)} %constant_dynamic-update-slice_fusion.left_ref, bf16[2048,2816]{1,0:T(8,128)(2,1)} %all-gather.10.cloned.1.call-done.right_ref), kind=kOutput, calls=%fused_computation.122 | convolution fusion | flops 5905580032 | bytes 19398656 | tf_op jit(solution)/shard_map/dot_general | solution.py:37
  287.7 8.6 %all-gather.14.cloned.1.call-done.right_ref = bf16[1408,2048]{1,0:T(8,128)(2,1)} async-done(((bf16[176,2048]{1,0:T(8,128)(2,1)}), bf16[1408,2048]{1,0:T(8,128)(2,1)}) %all-gather.14.cloned.1.call-update) | async-done | bytes 5767184 | tf_op jit(solution)/shard_map/all_gather | solution.py:733
  296.3 8.9 %fusion.21 = (f32[512,1408]{1,0:T(8,128)S(1)}, f32[512,1408]{1,0:T(8,128)S(1)}, bf16[512,1408]{1,0:T(8,128)(2,1)}) fusion(f32[512,2816]{1,0:T(8,128)} %fusion.30, bf16[512,2048]{1,0:T(8,128)(2,1)S(1)} %shard_map.243.right_ref, bf16[1408,2048]{1,0:T(8,128)(2,1)} %all-gather.14.cloned.1.call-done.right_ref), kind=kOutput, calls=%fused_computation.52 | convolution fusion | flops 2962882560 | bytes 20840448 | tf_op jit(solution)/shard_map/dot_general | solution.py:45
  305.5 10.5 %shard_map.245 = (f32[128,2048]{1,0:T(8,128)S(1)}, bf16[128,2048]{1,0:T(8,128)(2,1)}, bf16[128,2048]{1,0:T(8,128)(2,1)S(1)}, bf16[128,2048]{1,0:T(8,128)(2,1)S(1)}) custom-call(bf16[512,2816]{1,0:T(8,128)(2,1)S(1)} %add_convert_fusion.left_ref.refs_0_, bf16[2048,2816]{1,0:T(8,128)(2,1)} %all-gather.10.cloned.1.call-done.right_ref), custom_call_target="tpu_custom_call" | custom-call | tf_op jit(solution)/shard_map/pallas_call | solution.py:277
  322.8 7.8 %shard_map.247.refs_1_.refs_0_ = bf16[1408,2048]{1,0:T(8,128)(2,1)} custom-call(bf16[512,1408]{1,0:T(8,128)(2,1)S(1)} %copy-done.17, bf16[512,2048]{1,0:T(8,128)(2,1)S(1)} %shard_map.243.right_ref), custom_call_target="tpu_custom_call" | custom-call | tf_op jit(solution)/shard_map/pallas_call | solution.py:277
  332.5 10.6 %shard_map.249.refs_1_.refs_0_ = bf16[2048,2816]{1,0:T(8,128)(2,1)} custom-call(bf16[512,2048]{1,0:T(8,128)(2,1)} %constant_dynamic-update-slice_fusion.left_ref, bf16[512,2816]{1,0:T(8,128)(2,1)S(1)} %copy-done.1), custom_call_target="tpu_custom_call" | custom-call | tf_op jit(solution)/shard_map/pallas_call | solution.py:277
  343.1 22.9 %collective-permute-done.13.refs_1_.refs_3_ = bf16[128,2048]{1,0:T(8,128)(2,1)} collective-permute-done((bf16[128,2048]{1,0:T(8,128)(2,1)S(1)}, bf16[128,2048]{1,0:T(8,128)(2,1)}, u32[]{:S(2)}, u32[]{:S(2)}) %collective-permute-start.13) | collective-permute-done | bytes 524320 | tf_op jit(solution)/shard_map/ppermute | solution.py:716
  382.2 6.0 shard_map.253
  397.4 14.3 %collective-permute-done.16.refs_4_.refs_2_ = bf16[128,2048]{1,0:T(8,128)(2,1)S(1)} collective-permute-done((bf16[128,2048]{1,0:T(8,128)(2,1)}, bf16[128,2048]{1,0:T(8,128)(2,1)S(1)}, u32[]{:S(2)}, u32[]{:S(2)}) %collective-permute-start.16) | collective-permute-done | bytes 524320 | tf_op jit(solution)/shard_map/ppermute | solution.py:716
  413.4 12.0 %collective-permute-start.18 = (bf16[128,2048]{1,0:T(8,128)(2,1)}, bf16[128,2048]{1,0:T(8,128)(2,1)}, u32[]{:S(2)}, u32[]{:S(2)}) collective-permute-start(bf16[128,2048]{1,0:T(8,128)(2,1)} %get-tuple-element.76), channel_id=1, source_target_pairs={{0,24},{1,25},{2,26},{3,27},{4,28},{5,29},{6,30},{7,31},{8,0},{9,1... | collective-permute-start | bytes 1572872 | tf_op jit(solution)/shard_map/ppermute | solution.py:716
  429.3 17.3 %shard_map.256 = (bf16[512,2176]{1,0:T(8,128)(2,1)}, f32[8,1536]{1,0:T(8,128)S(1)}) custom-call(f32[4,4]{1,0:T(4,128)S(1)} %copy-done.59, f32[512,2176]{1,0:T(8,128)} %get-tuple-element.56.pre_ref, f32[8,1536]{1,0:T(8,128)S(1)} %copy-done.54, bf16[512,2048]{1,0:T(8,128)(2,1)S(1)} %copy-done.26, f32[16,128,128]{2,1,0:T(8,128)} %get-tuple-element.79.inverse_ref, ...), custom_call_target="tpu_custom_call" | custom-call | flops 60000002048 | tf_op jit(solution)/shard_map/pallas_call | solution.py:277
  448.9 8.3 %shard_map.257.refs_0_ = bf16[2048,2176]{1,0:T(8,128)(2,1)} custom-call(bf16[512,2048]{1,0:T(8,128)(2,1)S(1)} %copy-done.61, bf16[512,2176]{1,0:T(8,128)(2,1)S(1)} %copy-done.39), custom_call_target="tpu_custom_call" | custom-call | flops 20000000000 | tf_op jit(solution)/shard_map/pallas_call | solution.py:277
  458.9 8.1 %shard_map.261 = (f32[128,2048]{1,0:T(8,128)S(1)}, bf16[128,2048]{1,0:T(8,128)(2,1)S(1)}, bf16[128,2048]{1,0:T(8,128)(2,1)S(1)}, bf16[128,2048]{1,0:T(8,128)(2,1)S(1)}) custom-call(bf16[512,2176]{1,0:T(8,128)(2,1)S(1)} %copy-done.40, bf16[2048,2176]{1,0:T(8,128)(2,1)} %all-gather.8.cloned.1.call-done.weight_ref.right_ref), custom_call_target="tpu_custom_call" | custom-call | flops 149999992832 | tf_op jit(solution)/shard_map/pallas_call | solution.py:277
  484.8 5.1 all-to-all-start.2
  490.0 5.7 fusion
  501.0 26.3 %all-to-all-done.2 = f32[32,16,128]{2,1,0:T(8,128)S(1)} async-done(((f32[32,16,128]{2,1,0:T(8,128)}), f32[32,16,128]{2,1,0:T(8,128)S(1)}, u32[]{:S(2)}, u32[]{:S(2)}) %all-to-all-start.2) | async-done | bytes 262176 | tf_op jit(solution)/shard_map/all_to_all | solution.py:905
  544.9 8.8 %collective-permute-done.30 = bf16[2,176,1024]{2,1,0:T(8,128)(2,1)} collective-permute-done((bf16[2,176,1024]{2,1,0:T(8,128)(2,1)}, bf16[2,176,1024]{2,1,0:T(8,128)(2,1)}, u32[]{:S(2)}, u32[]{:S(2)}) %collective-permute-start.30) | collective-permute-done | bytes 720928 | tf_op jit(solution)/shard_map/ppermute | solution.py:749
  556.2 5.6 collective-permute-done.31
  567.8 5.1 all-to-all-start.4
  585.1 7.3 %collective-permute-done.27 = bf16[2,64,1024]{2,1,0:T(8,128)(2,1)S(1)} collective-permute-done((bf16[2,64,1024]{2,1,0:T(8,128)(2,1)S(1)}, bf16[2,64,1024]{2,1,0:T(8,128)(2,1)S(1)}, u32[]{:S(2)}, u32[]{:S(2)}) %collective-permute-start.27) | collective-permute-done | bytes 262176 | tf_op jit(solution)/shard_map/ppermute | solution.py:749
  (427 shorter events, 176.0 us)
Async XLA Ops:
  7.2 41.1 %all-gather.6.cloned.1.call-start = ((), (), s32[]{:S(2)}) async-start(), calls=%async_computation.7 | async-start | bytes 2359296 | tf_op jit(solution)/shard_map/all_gather | solution.py:733
  10.2 112.8 %all-gather.8.cloned.1.call-start = ((), (), s32[]{:S(2)}) async-start(), calls=%async_computation.8 | async-start | bytes 10027008 | tf_op jit(solution)/shard_map/all_gather | solution.py:733
  48.4 187.6 %all-gather.12.cloned.1.call-start = ((), (), s32[]{:S(2)}) async-start(), calls=%async_computation.10 | async-start | bytes 2621440 | tf_op jit(solution)/shard_map/all_gather | solution.py:825
  51.1 37.1 %collective-permute-start.1 = (bf16[128,2048]{1,0:T(8,128)(2,1)}, bf16[128,2048]{1,0:T(8,128)(2,1)S(1)}, u32[]{:S(2)}, u32[]{:S(2)}) collective-permute-start(bf16[128,2048]{1,0:T(8,128)(2,1)} %shard_map.232.refs_0_.refs_3_), channel_id=1, source_target_pairs={{0,16},{1,17},{2,18},{3,19},{4,20},{5,21},{6,22},{7,23},{8,24},{9,... | collective-permute-start | bytes 1572872 | tf_op jit(solution)/shard_map/ppermute | solution.py:716
  52.7 35.5 %collective-permute-start.2 = (bf16[128,2048]{1,0:T(8,128)(2,1)}, bf16[128,2048]{1,0:T(8,128)(2,1)S(1)}, u32[]{:S(2)}, u32[]{:S(2)}) collective-permute-start(bf16[128,2048]{1,0:T(8,128)(2,1)} %shard_map.232.refs_0_.refs_3_), channel_id=1, source_target_pairs={{0,24},{1,25},{2,26},{3,27},{4,28},{5,29},{6,30},{7,31},{8,0},{9,1... | collective-permute-start | bytes 1572872 | tf_op jit(solution)/shard_map/ppermute | solution.py:716
  107.3 167.0 %all-gather.10.cloned.1.call-start = ((), (), s32[]{:S(2)}) async-start(), calls=%async_computation.9 | async-start | bytes 12976128 | tf_op jit(solution)/shard_map/all_gather | solution.py:733
  114.1 41.0 %collective-permute-start.9 = (bf16[64,2816]{1,0:T(8,128)(2,1)}, bf16[64,2816]{1,0:T(8,128)(2,1)S(1)}, u32[]{:S(2)}, u32[]{:S(2)}) collective-permute-start(bf16[64,2816]{1,0:T(8,128)(2,1)} %get-tuple-element.63), channel_id=1, source_target_pairs={{0,8},{1,9},{2,10},{3,11},{4,12},{5,13},{6,14},{7,15},{8,16},{9,17... | collective-permute-start | bytes 1081352 | tf_op jit(solution)/shard_map/ppermute | solution.py:716
  115.9 44.6 %collective-permute-start.10 = (bf16[64,2816]{1,0:T(8,128)(2,1)}, bf16[64,2816]{1,0:T(8,128)(2,1)S(1)}, u32[]{:S(2)}, u32[]{:S(2)}) collective-permute-start(bf16[64,2816]{1,0:T(8,128)(2,1)} %get-tuple-element.64), channel_id=1, source_target_pairs={{0,16},{1,17},{2,18},{3,19},{4,20},{5,21},{6,22},{7,23},{8,24},{9,... | collective-permute-start | bytes 1081352 | tf_op jit(solution)/shard_map/ppermute | solution.py:716
  118.3 44.2 %collective-permute-start.11 = (bf16[64,2816]{1,0:T(8,128)(2,1)}, bf16[64,2816]{1,0:T(8,128)(2,1)S(1)}, u32[]{:S(2)}, u32[]{:S(2)}) collective-permute-start(bf16[64,2816]{1,0:T(8,128)(2,1)} %get-tuple-element.65), channel_id=1, source_target_pairs={{0,24},{1,25},{2,26},{3,27},{4,28},{5,29},{6,30},{7,31},{8,0},{9,1... | collective-permute-start | bytes 1081352 | tf_op jit(solution)/shard_map/ppermute | solution.py:716
  163.8 132.5 %all-gather.14.cloned.1.call-start = ((), (), s32[]{:S(2)}) async-start(), calls=%async_computation.11 | async-start | bytes 6488064 | tf_op jit(solution)/shard_map/all_gather | solution.py:733
  164.4 292.9 %reduce-scatter.3.cloned.1.call-start = ((), (), s32[]{:S(2)}) async-start(), calls=%async_computation.12 | async-start | bytes 12976128 | tf_op jit(solution)/shard_map/reduce_scatter | solution.py:736
  164.4 32.8 %collective-permute-start.3 = (bf16[128,2048]{1,0:T(8,128)(2,1)S(1)}, bf16[128,2048]{1,0:T(8,128)(2,1)S(1)}, u32[]{:S(2)}, u32[]{:S(2)}) collective-permute-start(bf16[128,2048]{1,0:T(8,128)(2,1)S(1)} %get-tuple-element.59.refs_3_), channel_id=1, source_target_pairs={{0,24},{1,25},{2,26},{3,27},{4,28},{5,29},{6,30},{7,31},{8,0},{9,1... | collective-permute-start | bytes 1572872 | tf_op jit(solution)/shard_map/ppermute | solution.py:716
  184.8 46.0 %collective-permute-start.4 = (bf16[128,2048]{1,0:T(8,128)(2,1)S(1)}, bf16[128,2048]{1,0:T(8,128)(2,1)S(1)}, u32[]{:S(2)}, u32[]{:S(2)}) collective-permute-start(bf16[128,2048]{1,0:T(8,128)(2,1)S(1)} %get-tuple-element.60.refs_4_), channel_id=1, source_target_pairs={{0,16},{1,17},{2,18},{3,19},{4,20},{5,21},{6,22},{7,23},{8,24},{9,... | collective-permute-start | bytes 1572872 | tf_op jit(solution)/shard_map/ppermute | solution.py:716
  185.4 45.5 %collective-permute-start.5 = (bf16[128,2048]{1,0:T(8,128)(2,1)S(1)}, bf16[128,2048]{1,0:T(8,128)(2,1)S(1)}, u32[]{:S(2)}, u32[]{:S(2)}) collective-permute-start(bf16[128,2048]{1,0:T(8,128)(2,1)S(1)} %get-tuple-element.61.refs_5_), channel_id=1, source_target_pairs={{0,8},{1,9},{2,10},{3,11},{4,12},{5,13},{6,14},{7,15},{8,16},{9,17... | collective-permute-start | bytes 1572872 | tf_op jit(solution)/shard_map/ppermute | solution.py:716
  235.0 37.6 %collective-permute-start.7 = (bf16[128,2048]{1,0:T(8,128)(2,1)}, bf16[128,2048]{1,0:T(8,128)(2,1)S(1)}, u32[]{:S(2)}, u32[]{:S(2)}) collective-permute-start(bf16[128,2048]{1,0:T(8,128)(2,1)} %get-tuple-element.62), channel_id=1, source_target_pairs={{0,16},{1,17},{2,18},{3,19},{4,20},{5,21},{6,22},{7,23},{8,24},{9,... | collective-permute-start | bytes 1572872 | tf_op jit(solution)/shard_map/ppermute | solution.py:716
  238.5 34.9 %collective-permute-start.8 = (bf16[128,2048]{1,0:T(8,128)(2,1)S(1)}, bf16[128,2048]{1,0:T(8,128)(2,1)S(1)}, u32[]{:S(2)}, u32[]{:S(2)}) collective-permute-start(bf16[128,2048]{1,0:T(8,128)(2,1)S(1)} %copy-done.71), channel_id=1, source_target_pairs={{0,24},{1,25},{2,26},{3,27},{4,28},{5,29},{6,30},{7,31},{8,0},{9,1... | collective-permute-start | bytes 1572872 | tf_op jit(solution)/shard_map/ppermute | solution.py:716
  317.0 26.1 %collective-permute-start.12 = (bf16[128,2048]{1,0:T(8,128)(2,1)}, bf16[128,2048]{1,0:T(8,128)(2,1)}, u32[]{:S(2)}, u32[]{:S(2)}) collective-permute-start(bf16[128,2048]{1,0:T(8,128)(2,1)} %get-tuple-element.66.refs_1_), channel_id=1, source_target_pairs={{0,24},{1,25},{2,26},{3,27},{4,28},{5,29},{6,30},{7,31},{8,0},{9,1... | collective-permute-start | bytes 1572872 | tf_op jit(solution)/shard_map/ppermute | solution.py:716
  320.4 45.7 %collective-permute-start.13 = (bf16[128,2048]{1,0:T(8,128)(2,1)S(1)}, bf16[128,2048]{1,0:T(8,128)(2,1)}, u32[]{:S(2)}, u32[]{:S(2)}) collective-permute-start(bf16[128,2048]{1,0:T(8,128)(2,1)S(1)} %get-tuple-element.67.refs_2_), channel_id=1, source_target_pairs={{0,16},{1,17},{2,18},{3,19},{4,20},{5,21},{6,22},{7,23},{8,24},{9,... | collective-permute-start | bytes 1572872 | tf_op jit(solution)/shard_map/ppermute | solution.py:716
  320.4 45.7 %collective-permute-start.14 = (bf16[128,2048]{1,0:T(8,128)(2,1)S(1)}, bf16[128,2048]{1,0:T(8,128)(2,1)}, u32[]{:S(2)}, u32[]{:S(2)}) collective-permute-start(bf16[128,2048]{1,0:T(8,128)(2,1)S(1)} %get-tuple-element.68.refs_3_), channel_id=1, source_target_pairs={{0,8},{1,9},{2,10},{3,11},{4,12},{5,13},{6,14},{7,15},{8,16},{9,17... | collective-permute-start | bytes 1572872 | tf_op jit(solution)/shard_map/ppermute | solution.py:716
  366.1 200.5 %reduce-scatter.5.cloned.1.call-start = ((), (), s32[]{:S(2)}) async-start(), calls=%async_computation.13 | async-start | bytes 10027008 | tf_op jit(solution)/shard_map/reduce_scatter | solution.py:736
  374.3 37.4 %collective-permute-start.16 = (bf16[128,2048]{1,0:T(8,128)(2,1)}, bf16[128,2048]{1,0:T(8,128)(2,1)S(1)}, u32[]{:S(2)}, u32[]{:S(2)}) collective-permute-start(bf16[128,2048]{1,0:T(8,128)(2,1)} %get-tuple-element.71.refs_1_.refs_0_), channel_id=1, source_target_pairs={{0,16},{1,17},{2,18},{3,19},{4,20},{5,21},{6,22},{7,23},{8,24},{9,... | collective-permute-start | bytes 1572872 | tf_op jit(solution)/shard_map/ppermute | solution.py:716
  376.9 34.8 %collective-permute-start.17 = (bf16[128,2048]{1,0:T(8,128)(2,1)}, bf16[128,2048]{1,0:T(8,128)(2,1)S(1)}, u32[]{:S(2)}, u32[]{:S(2)}) collective-permute-start(bf16[128,2048]{1,0:T(8,128)(2,1)} %get-tuple-element.71.refs_1_.refs_0_), channel_id=1, source_target_pairs={{0,24},{1,25},{2,26},{3,27},{4,28},{5,29},{6,30},{7,31},{8,0},{9,1... | collective-permute-start | bytes 1572872 | tf_op jit(solution)/shard_map/ppermute | solution.py:716
  397.4 92.5 %collective-permute-start.29 = (bf16[2,2,176,2048]{3,2,1,0:T(8,128)(2,1)}, bf16[2,2,176,2048]{3,2,1,0:T(8,128)(2,1)}, u32[]{:S(2)}, u32[]{:S(2)}) collective-permute-start(bf16[2,2,176,2048]{3,2,1,0:T(8,128)(2,1)} %dynamic-slice_bitcast_fusion), channel_id=1, source_target_pairs={{0,1},{1,0},{2,3},{3,2},{4,5},{5,4},{6,7},{7,6},{8,9},{9,8},{10,11... | collective-permute-start | bytes 8650760 | tf_op jit(solution)/shard_map/ppermute | solution.py:749
  413.4 57.0 %collective-permute-start.18 = (bf16[128,2048]{1,0:T(8,128)(2,1)}, bf16[128,2048]{1,0:T(8,128)(2,1)}, u32[]{:S(2)}, u32[]{:S(2)}) collective-permute-start(bf16[128,2048]{1,0:T(8,128)(2,1)} %get-tuple-element.76), channel_id=1, source_target_pairs={{0,24},{1,25},{2,26},{3,27},{4,28},{5,29},{6,30},{7,31},{8,0},{9,1... | collective-permute-start | bytes 1572872 | tf_op jit(solution)/shard_map/ppermute | solution.py:716
  425.5 45.0 %collective-permute-start.19 = (bf16[128,2048]{1,0:T(8,128)(2,1)}, bf16[128,2048]{1,0:T(8,128)(2,1)}, u32[]{:S(2)}, u32[]{:S(2)}) collective-permute-start(bf16[128,2048]{1,0:T(8,128)(2,1)} %get-tuple-element.77), channel_id=1, source_target_pairs={{0,16},{1,17},{2,18},{3,19},{4,20},{5,21},{6,22},{7,23},{8,24},{9,... | collective-permute-start | bytes 1572872 | tf_op jit(solution)/shard_map/ppermute | solution.py:716
  425.5 45.0 %collective-permute-start.20 = (bf16[128,2048]{1,0:T(8,128)(2,1)}, bf16[128,2048]{1,0:T(8,128)(2,1)}, u32[]{:S(2)}, u32[]{:S(2)}) collective-permute-start(bf16[128,2048]{1,0:T(8,128)(2,1)} %get-tuple-element.78), channel_id=1, source_target_pairs={{0,8},{1,9},{2,10},{3,11},{4,12},{5,13},{6,14},{7,15},{8,16},{9,17... | collective-permute-start | bytes 1572872 | tf_op jit(solution)/shard_map/ppermute | solution.py:716
  474.3 62.1 %collective-permute-start.21 = (bf16[128,2048]{1,0:T(8,128)(2,1)}, bf16[128,2048]{1,0:T(8,128)(2,1)}, u32[]{:S(2)}, u32[]{:S(2)}) collective-permute-start(bf16[128,2048]{1,0:T(8,128)(2,1)} %get-tuple-element.89.refs_1_), channel_id=1, source_target_pairs={{0,24},{1,25},{2,26},{3,27},{4,28},{5,29},{6,30},{7,31},{8,0},{9,1... | collective-permute-start | bytes 1572872 | tf_op jit(solution)/shard_map/ppermute | solution.py:716
  477.4 59.0 %collective-permute-start.22 = (bf16[128,2048]{1,0:T(8,128)(2,1)}, bf16[128,2048]{1,0:T(8,128)(2,1)}, u32[]{:S(2)}, u32[]{:S(2)}) collective-permute-start(bf16[128,2048]{1,0:T(8,128)(2,1)} %get-tuple-element.90.refs_2_), channel_id=1, source_target_pairs={{0,16},{1,17},{2,18},{3,19},{4,20},{5,21},{6,22},{7,23},{8,24},{9,... | collective-permute-start | bytes 1572872 | tf_op jit(solution)/shard_map/ppermute | solution.py:716
  478.3 58.1 %collective-permute-start.23 = (bf16[128,2048]{1,0:T(8,128)(2,1)}, bf16[128,2048]{1,0:T(8,128)(2,1)}, u32[]{:S(2)}, u32[]{:S(2)}) collective-permute-start(bf16[128,2048]{1,0:T(8,128)(2,1)} %get-tuple-element.91.refs_3_), channel_id=1, source_target_pairs={{0,8},{1,9},{2,10},{3,11},{4,12},{5,13},{6,14},{7,15},{8,16},{9,17... | collective-permute-start | bytes 1572872 | tf_op jit(solution)/shard_map/ppermute | solution.py:716
  484.8 42.5 %all-to-all-start.2 = ((f32[32,16,128]{2,1,0:T(8,128)}), f32[32,16,128]{2,1,0:T(8,128)S(1)}, u32[]{:S(2)}, u32[]{:S(2)}) async-start(f32[32,16,128]{2,1,0:T(8,128)} %pad.60.clone), calls=%async_computation.3 | async-start | bytes 524288 | tf_op jit(solution)/shard_map/all_to_all | solution.py:905
  527.3 39.3 %all-to-all-start.3 = ((bf16[4,64,2816]{2,1,0:T(8,128)(2,1)}), bf16[4,64,2816]{2,1,0:T(8,128)(2,1)S(1)}, u32[]{:S(2)}, u32[]{:S(2)}) async-start(bf16[4,64,2816]{2,1,0:T(8,128)(2,1)} %bitcast.146), calls=%async_computation.5 | async-start | bytes 2883584 | tf_op jit(solution)/shard_map/all_to_all | solution.py:706
  567.8 32.1 %all-to-all-start.4 = ((bf16[4,64,2176]{2,1,0:T(8,128)(2,1)}), bf16[4,64,2176]{2,1,0:T(8,128)(2,1)S(1)}, u32[]{:S(2)}, u32[]{:S(2)}) async-start(bf16[4,64,2176]{2,1,0:T(8,128)(2,1)} %bitcast.140), calls=%async_computation.6 | async-start | bytes 2228224 | tf_op jit(solution)/shard_map/all_to_all | solution.py:706
  (103 other events, 959.9 us)
Sparse Core Ops, SparseCore 0:
  10.5 30.5 all-gather.5
  48.5 55.7 all-gather.7
  105.8 76.5 all-gather.11
  184.7 66.4 all-gather.9
  252.9 43.3 all-gather.13
  366.2 85.9 reduce-scatter.2
  457.4 75.7 reduce-scatter.4
where the time goes:
time: 620 us; the launch traced here: 609 us
  waiting for transfers between devices  215 us (35%)
  Pallas kernels  128 us (21%)
  starting transfers between devices  97.2 us (16%)
  local copies, waits for them, and re-layouts  69.9 us (11%)
  blocking collectives  33.6 us (5%)
  other arithmetic  26.8 us (4%)
  matrix products  22.3 us (4%)
  between operations  16.3 us (3%)
    ppermute x24, waiting for transfers between devices, shift(): return lax.ppermute(values, 'dp', pairs)  151 us
    pallas_call x12, Pallas kernels, call(): pl.pallas_call(kernel, grid=grid, in_specs=in_specs, out_specs=out_specs,...  99.1 us
    ppermute x24, starting transfers between devices, shift(): return lax.ppermute(values, 'dp', pairs)  61.5 us
    unnamed x191, local copies, waits for them, and re-layouts  40.8 us
    all_to_all x1, blocking collectives, exchange(): lax.all_to_all(values, 'dp', split_axis=0, concat_axis=0, axis_index_grou...  33.6 us
    ppermute x10, waiting for transfers between devices, halves_across(): return (own, lax.ppermute(other, 'dp', pairs))  27.1 us
    all_to_all x1, waiting for transfers between devices, body(): lax.all_to_all(small_grad, 'dp', 0, 0, tiled=True)  26.3 us
    pallas_call x4, Pallas kernels, by_rows(): pl.pallas_call(kernel, grid=(GROUP_ROWS // block,), in_specs=[spec(array....  14.5 us
  transfers between devices with their start and end apart: 45, of which 18 were waited for; matrix products, arithmetic and copies ran while one was open for 12% of the time, Pallas kernels for 19%

commit v1 on v0

--- a/solution.py
+++ b/solution.py
@@ -901,23 +901,24 @@
         for grad in (gain_one_grad, gain_two_grad)
     ]
     small_grad = jnp.concatenate([taps_grad, head_grad] + gain_grads, 1)
-    small_grad = jnp.pad(small_grad, ((0, 0), (0, 1), (0, 128 - rows_own)))
+    d_mixed = jnp.concatenate([tie(d_mixed[0], d_normed_terms[0])] + d_mixed[1:], 0)
+    out_grads = grad_product(mixed, d_mixed)
+    late = tie(gain_one, out_grads, *down_grad)
+    (input_grad,) = by_rows(
+        functools.partial(input_back_kernel, parts, copies),
+        d_normed + [inputs, late, d_hidden],
+        [narrow],
+    )
+    small_grad = jnp.pad(tie(small_grad, input_grad), ((0, 0), (0, 1), (0, 128 - rows_own)))
     small_grad = jnp.sum(lax.all_to_all(small_grad, "dp", 0, 0, tiled=True), 0)[:, :rows_own]
     taps_shard = small_grad[: 3 * KERNEL].reshape(3, KERNEL, rows_own).swapaxes(1, 2)
     taps_shard = taps_shard.reshape(3 * rows_own, KERNEL)
     head_shard, gain_one_shard, gain_two_shard = small_grad[3 * KERNEL : 3 * KERNEL + 3]
 
-    out_grads = grad_product(tie(mixed, d_normed_terms[0]), jnp.concatenate(d_mixed, 0))
-    late = tie(gain_one, out_grads)
-    (input_grad,) = by_rows(
-        functools.partial(input_back_kernel, parts, copies),
-        d_normed + [inputs, late, d_hidden],
-        [narrow],
-    )
     updown_grad = tie(updown_grad, mixer_terms).reshape(parts, rows_own, 2 * units)
     updown_grad = exchange(updown_grad)
     mixer_grad = tie(mixer_grad, updown_grad, input_grad)
-    updown_shard = updown_from_parts(updown_grad)
+    updown_shard = updown_from_parts(tie(updown_grad, mixer_grad))
     down_shard = halve_second(tie_all(down_grad, input_grad), mixer_grad)
     out_grads = tie(halve_cores(tie(out_grads, input_grad)), mixer_grad)
     out_shard = halve_second(halve_first(out_grads))

time: 620 us -> 616 us (level)
    ppermute x24, waiting for transfers between devices: 151 us -> 171 us  [shift(): return lax.ppermute(values, 'dp', pairs)]
    all_to_all x1, waiting for transfers between devices: 26.3 us -> 7.94 us  [body(): lax.all_to_all(small_grad, 'dp', 0, 0, tiled=True)]
    unnamed x191 -> x188, local copies, waits for them, and re-layouts: 40.8 us -> 38.4 us
  transfers between devices with their start and end apart: 45 -> 45, of which waited for: 18 -> 20; matrix products, arithmetic and copies ran while one was open for 12% -> 12% of each run, Pallas kernels for 19% -> 19%
where the time goes in v1:
time: 616 us; the launch traced here: 605 us
  waiting for transfers between devices  217 us (35%)
  Pallas kernels  129 us (21%)
  starting transfers between devices  94.7 us (15%)
  local copies, waits for them, and re-layouts  69 us (11%)
  blocking collectives  33.6 us (5%)
  other arithmetic  23.4 us (4%)
  matrix products  22.3 us (4%)
  between operations  16.3 us (3%)
    ppermute x24, waiting for transfers between devices, shift(): return lax.ppermute(values, 'dp', pairs)  171 us
    pallas_call x12, Pallas kernels, call(): pl.pallas_call(kernel, grid=grid, in_specs=in_specs, out_specs=out_specs,...  99.9 us
    ppermute x24, starting transfers between devices, shift(): return lax.ppermute(values, 'dp', pairs)  59.9 us
    unnamed x188, local copies, waits for them, and re-layouts  38.4 us
    all_to_all x1, blocking collectives, exchange(): lax.all_to_all(values, 'dp', split_axis=0, concat_axis=0, axis_index_grou...  33.6 us
    ppermute x10, waiting for transfers between devices, halves_across(): return (own, lax.ppermute(other, 'dp', pairs))  28.1 us
    pallas_call x4, Pallas kernels, by_rows(): pl.pallas_call(kernel, grid=(GROUP_ROWS // block,), in_specs=[spec(array....  14.6 us
    dot_general x1, matrix products, plain_product(): return jnp.dot(left, right, preferred_element_type=f32)  13.4 us
  transfers between devices with their start and end apart: 45, of which 20 were waited for; matrix products, arithmetic and copies ran while one was open for 12% of the time, Pallas kernels for 19%

profile of v1, /device:TPU:0, one launch (start us, length us, event | category | flops | bytes accessed | tf_op | source)
XLA Modules:
  0.0 605.1 jit_solution(4205894033277623672)
XLA Ops:
  14.8 33.6 %all_to_all.25.refs_0_ = bf16[4,64,2176]{2,1,0:T(8,128)(2,1)} all-to-all(bf16[4,64,2176]{2,1,0:T(8,128)(2,1)} %shard_map.230), channel_id=1, replica_groups={{0,8,16,24},{1,9,17,25},{2,10,18,26},{3,11,19,27},{4,12,20,28},{5,13,21..., dimensions={0} | all-to-all | bytes 2228224 | tf_op jit(solution)/shard_map/all_to_all | solution.py:706
  56.0 11.7 %collective-permute-done.refs_1_.refs_3_ = bf16[128,2048]{1,0:T(8,128)(2,1)S(1)} collective-permute-done((bf16[128,2048]{1,0:T(8,128)(2,1)}, bf16[128,2048]{1,0:T(8,128)(2,1)S(1)}, u32[]{:S(2)}, u32[]{:S(2)}) %collective-permute-start) | collective-permute-done | bytes 524320 | tf_op jit(solution)/shard_map/ppermute | solution.py:716
  67.7 20.5 %collective-permute-done.1.refs_2_.refs_4_ = bf16[128,2048]{1,0:T(8,128)(2,1)S(1)} collective-permute-done((bf16[128,2048]{1,0:T(8,128)(2,1)}, bf16[128,2048]{1,0:T(8,128)(2,1)S(1)}, u32[]{:S(2)}, u32[]{:S(2)}) %collective-permute-start.1) | collective-permute-done | bytes 524320 | tf_op jit(solution)/shard_map/ppermute | solution.py:716
  94.5 12.8 %all-to-all-start.1 = ((bf16[32,16,256]{2,1,0:T(8,128)(2,1)}), bf16[32,16,256]{2,1,0:T(8,128)(2,1)S(1)}, u32[]{:S(2)}, u32[]{:S(2)}) async-start(bf16[32,16,256]{2,1,0:T(8,128)(2,1)} %shard_map.233), calls=%async_computation.1 | async-start | bytes 524288 | tf_op jit(solution)/shard_map/all_to_all | solution.py:801
  123.3 10.9 %shard_map.236 = (bf16[512,2048]{1,0:T(8,128)(2,1)S(1)}, f32[512,2176]{1,0:T(8,128)}) custom-call(f32[1,2048]{1,0:T(1,128)S(1)} %copy-done.54, bf16[2048,2176]{1,0:T(8,128)(2,1)} %all-gather.8.cloned.1.call-done.weight_ref.right_ref, bf16[128,2048]{1,0:T(8,128)(2,1)S(1)} %copy-done.2, bf16[128,2048]{1,0:T(8,128)(2,1)S(1)} %copy-done.6, ...), custom_call_target="tpu_custom_call" | custom-call | tf_op jit(solution)/shard_map/pallas_call | solution.py:277
  137.8 14.7 %shard_map.237 = (bf16[512,512]{1,0:T(8,128)(2,1)S(1)}, f32[16,128,128]{2,1,0:T(8,128)}, f32[16,128,128]{2,1,0:T(8,128)}, f32[16,128,128]{2,1,0:T(8,128)}, f32[16,128,128]{2,1,0:T(8,128)}) custom-call(f32[4,4]{1,0:T(4,128)S(1)} %multiply_reduce_fusion.layout_ref, f32[512,2176]{1,0:T(8,128)S(1)} %copy-done.37, f32[8,1536]{1,0:T(8,128)S(1)} %pad.57.param_ref.refs_0_), custom_call_target="tpu_custom_call" | custom-call | tf_op jit(solution)/shard_map/pallas_call | solution.py:277
  154.7 5.8 collective-permute-done.10.refs_1_
  164.5 20.3 %collective-permute-start.3 = (bf16[128,2048]{1,0:T(8,128)(2,1)S(1)}, bf16[128,2048]{1,0:T(8,128)(2,1)S(1)}, u32[]{:S(2)}, u32[]{:S(2)}) collective-permute-start(bf16[128,2048]{1,0:T(8,128)(2,1)S(1)} %get-tuple-element.59.refs_3_), channel_id=1, source_target_pairs={{0,24},{1,25},{2,26},{3,27},{4,28},{5,29},{6,30},{7,31},{8,0},{9,1... | collective-permute-start | bytes 1572872 | tf_op jit(solution)/shard_map/ppermute | solution.py:716
  186.2 11.1 %collective-permute-done.3.refs_0_ = bf16[128,2048]{1,0:T(8,128)(2,1)S(1)} collective-permute-done((bf16[128,2048]{1,0:T(8,128)(2,1)S(1)}, bf16[128,2048]{1,0:T(8,128)(2,1)S(1)}, u32[]{:S(2)}, u32[]{:S(2)}) %collective-permute-start.3) | collective-permute-done | bytes 524320 | tf_op jit(solution)/shard_map/ppermute | solution.py:716
  197.3 33.5 %collective-permute-done.4.refs_1_ = bf16[128,2048]{1,0:T(8,128)(2,1)S(1)} collective-permute-done((bf16[128,2048]{1,0:T(8,128)(2,1)S(1)}, bf16[128,2048]{1,0:T(8,128)(2,1)S(1)}, u32[]{:S(2)}, u32[]{:S(2)}) %collective-permute-start.4) | collective-permute-done | bytes 524320 | tf_op jit(solution)/shard_map/ppermute | solution.py:716
  242.3 9.7 %collective-permute-done.6 = bf16[128,2048]{1,0:T(8,128)(2,1)} collective-permute-done((bf16[128,2048]{1,0:T(8,128)(2,1)}, bf16[128,2048]{1,0:T(8,128)(2,1)}, u32[]{:S(2)}, u32[]{:S(2)}) %collective-permute-start.6) | collective-permute-done | bytes 524320 | tf_op jit(solution)/shard_map/ppermute | solution.py:716
  253.9 18.5 %collective-permute-done.7 = bf16[128,2048]{1,0:T(8,128)(2,1)S(1)} collective-permute-done((bf16[128,2048]{1,0:T(8,128)(2,1)}, bf16[128,2048]{1,0:T(8,128)(2,1)S(1)}, u32[]{:S(2)}, u32[]{:S(2)}) %collective-permute-start.7) | collective-permute-done | bytes 524320 | tf_op jit(solution)/shard_map/ppermute | solution.py:716
  274.1 13.4 %fusion.30 = f32[512,2816]{1,0:T(8,128)} fusion(bf16[512,2048]{1,0:T(8,128)(2,1)} %constant_dynamic-update-slice_fusion.left_ref, bf16[2048,2816]{1,0:T(8,128)(2,1)} %all-gather.10.cloned.1.call-done.right_ref), kind=kOutput, calls=%fused_computation.120 | convolution fusion | flops 5905580032 | bytes 19398656 | tf_op jit(solution)/shard_map/dot_general | solution.py:37
  287.5 8.7 %all-gather.14.cloned.1.call-done.right_ref = bf16[1408,2048]{1,0:T(8,128)(2,1)} async-done(((bf16[176,2048]{1,0:T(8,128)(2,1)}), bf16[1408,2048]{1,0:T(8,128)(2,1)}) %all-gather.14.cloned.1.call-update) | async-done | bytes 5767184 | tf_op jit(solution)/shard_map/all_gather | solution.py:733
  296.3 8.9 %fusion.21 = (f32[512,1408]{1,0:T(8,128)S(1)}, f32[512,1408]{1,0:T(8,128)S(1)}, bf16[512,1408]{1,0:T(8,128)(2,1)}) fusion(f32[512,2816]{1,0:T(8,128)} %fusion.30, bf16[512,2048]{1,0:T(8,128)(2,1)S(1)} %shard_map.243.right_ref, bf16[1408,2048]{1,0:T(8,128)(2,1)} %all-gather.14.cloned.1.call-done.right_ref), kind=kOutput, calls=%fused_computation.52 | convolution fusion | flops 2962882560 | bytes 20840448 | tf_op jit(solution)/shard_map/dot_general | solution.py:45
  305.5 10.5 %shard_map.245 = (f32[128,2048]{1,0:T(8,128)S(1)}, bf16[128,2048]{1,0:T(8,128)(2,1)}, bf16[128,2048]{1,0:T(8,128)(2,1)S(1)}, bf16[128,2048]{1,0:T(8,128)(2,1)S(1)}) custom-call(bf16[512,2816]{1,0:T(8,128)(2,1)S(1)} %add_convert_fusion.left_ref.refs_0_, bf16[2048,2816]{1,0:T(8,128)(2,1)} %all-gather.10.cloned.1.call-done.right_ref), custom_call_target="tpu_custom_call" | custom-call | tf_op jit(solution)/shard_map/pallas_call | solution.py:277
  322.8 7.8 %shard_map.247.refs_1_.refs_0_ = bf16[1408,2048]{1,0:T(8,128)(2,1)} custom-call(bf16[512,1408]{1,0:T(8,128)(2,1)S(1)} %copy-done.17, bf16[512,2048]{1,0:T(8,128)(2,1)S(1)} %shard_map.243.right_ref), custom_call_target="tpu_custom_call" | custom-call | tf_op jit(solution)/shard_map/pallas_call | solution.py:277
  332.5 10.6 %shard_map.249.refs_1_.refs_0_ = bf16[2048,2816]{1,0:T(8,128)(2,1)} custom-call(bf16[512,2048]{1,0:T(8,128)(2,1)} %constant_dynamic-update-slice_fusion.left_ref, bf16[512,2816]{1,0:T(8,128)(2,1)S(1)} %copy-done.1), custom_call_target="tpu_custom_call" | custom-call | tf_op jit(solution)/shard_map/pallas_call | solution.py:277
  343.1 22.9 %collective-permute-done.13.refs_1_.refs_3_ = bf16[128,2048]{1,0:T(8,128)(2,1)} collective-permute-done((bf16[128,2048]{1,0:T(8,128)(2,1)S(1)}, bf16[128,2048]{1,0:T(8,128)(2,1)}, u32[]{:S(2)}, u32[]{:S(2)}) %collective-permute-start.13) | collective-permute-done | bytes 524320 | tf_op jit(solution)/shard_map/ppermute | solution.py:716
  369.8 4.5 shard_map.251
  382.2 6.0 shard_map.253
  391.5 4.2 dynamic-slice_bitcast_fusion
  397.9 13.9 %collective-permute-done.16.refs_4_.refs_2_ = bf16[128,2048]{1,0:T(8,128)(2,1)} collective-permute-done((bf16[128,2048]{1,0:T(8,128)(2,1)}, bf16[128,2048]{1,0:T(8,128)(2,1)}, u32[]{:S(2)}, u32[]{:S(2)}) %collective-permute-start.16) | collective-permute-done | bytes 524320 | tf_op jit(solution)/shard_map/ppermute | solution.py:716
  411.8 12.0 %collective-permute-start.18 = (bf16[128,2048]{1,0:T(8,128)(2,1)}, bf16[128,2048]{1,0:T(8,128)(2,1)}, u32[]{:S(2)}, u32[]{:S(2)}) collective-permute-start(bf16[128,2048]{1,0:T(8,128)(2,1)} %get-tuple-element.76), channel_id=1, source_target_pairs={{0,24},{1,25},{2,26},{3,27},{4,28},{5,29},{6,30},{7,31},{8,0},{9,1... | collective-permute-start | bytes 1572872 | tf_op jit(solution)/shard_map/ppermute | solution.py:716
  425.7 17.9 %shard_map.256 = (bf16[512,2176]{1,0:T(8,128)(2,1)}, f32[8,1536]{1,0:T(8,128)S(1)}) custom-call(f32[4,4]{1,0:T(4,128)S(1)} %multiply_reduce_fusion.layout_ref, f32[512,2176]{1,0:T(8,128)} %get-tuple-element.56.pre_ref, f32[8,1536]{1,0:T(8,128)S(1)} %copy-done.52, bf16[512,2048]{1,0:T(8,128)(2,1)S(1)} %copy-done.25, ...), custom_call_target="tpu_custom_call" | custom-call | flops 60000002048 | tf_op jit(solution)/shard_map/pallas_call | solution.py:277
  445.9 8.3 %shard_map.257.refs_0_ = bf16[2048,2176]{1,0:T(8,128)(2,1)} custom-call(bf16[512,2048]{1,0:T(8,128)(2,1)S(1)} %copy-done.57, bf16[512,2176]{1,0:T(8,128)(2,1)S(1)} %copy-done.39), custom_call_target="tpu_custom_call" | custom-call | flops 20000000000 | tf_op jit(solution)/shard_map/pallas_call | solution.py:277
  455.9 8.3 %shard_map.261 = (f32[128,2048]{1,0:T(8,128)S(1)}, bf16[128,2048]{1,0:T(8,128)(2,1)S(1)}, bf16[128,2048]{1,0:T(8,128)(2,1)S(1)}, bf16[128,2048]{1,0:T(8,128)(2,1)S(1)}) custom-call(bf16[512,2176]{1,0:T(8,128)(2,1)S(1)} %copy-done.40, bf16[2048,2176]{1,0:T(8,128)(2,1)} %all-gather.8.cloned.1.call-done.weight_ref.right_ref), custom_call_target="tpu_custom_call" | custom-call | flops 149999992832 | tf_op jit(solution)/shard_map/pallas_call | solution.py:277
  483.8 5.4 all-to-all-start.3
  495.3 18.9 %collective-permute-done.25 = bf16[2,176,1024]{2,1,0:T(8,128)(2,1)} collective-permute-done((bf16[2,176,1024]{2,1,0:T(8,128)(2,1)}, bf16[2,176,1024]{2,1,0:T(8,128)(2,1)}, u32[]{:S(2)}, u32[]{:S(2)}) %collective-permute-start.25) | collective-permute-done | bytes 720928 | tf_op jit(solution)/shard_map/ppermute | solution.py:749
  517.8 19.5 %collective-permute-done.22.refs_1_ = bf16[128,2048]{1,0:T(8,128)(2,1)} collective-permute-done((bf16[128,2048]{1,0:T(8,128)(2,1)}, bf16[128,2048]{1,0:T(8,128)(2,1)}, u32[]{:S(2)}, u32[]{:S(2)}) %collective-permute-start.22) | collective-permute-done | bytes 524320 | tf_op jit(solution)/shard_map/ppermute | solution.py:716
  556.6 7.9 %all-to-all-done.2 = f32[32,16,128]{2,1,0:T(8,128)} async-done(((f32[32,16,128]{2,1,0:T(8,128)}), f32[32,16,128]{2,1,0:T(8,128)}, u32[]{:S(2)}, u32[]{:S(2)}) %all-to-all-start.2) | async-done | bytes 262176 | tf_op jit(solution)/shard_map/all_to_all | solution.py:913
  580.3 7.0 %collective-permute-done.30 = bf16[2,64,1024]{2,1,0:T(8,128)(2,1)S(1)} collective-permute-done((bf16[2,64,1024]{2,1,0:T(8,128)(2,1)S(1)}, bf16[2,64,1024]{2,1,0:T(8,128)(2,1)S(1)}, u32[]{:S(2)}, u32[]{:S(2)}) %collective-permute-start.30) | collective-permute-done | bytes 262176 | tf_op jit(solution)/shard_map/ppermute | solution.py:749
  (428 shorter events, 168.7 us)
Async XLA Ops:
  7.2 41.1 %all-gather.6.cloned.1.call-start = ((), (), s32[]{:S(2)}) async-start(), calls=%async_computation.7 | async-start | bytes 2359296 | tf_op jit(solution)/shard_map/all_gather | solution.py:733
  10.2 112.3 %all-gather.8.cloned.1.call-start = ((), (), s32[]{:S(2)}) async-start(), calls=%async_computation.8 | async-start | bytes 10027008 | tf_op jit(solution)/shard_map/all_gather | solution.py:733
  48.4 187.6 %all-gather.12.cloned.1.call-start = ((), (), s32[]{:S(2)}) async-start(), calls=%async_computation.10 | async-start | bytes 2621440 | tf_op jit(solution)/shard_map/all_gather | solution.py:825
  51.1 37.1 %collective-permute-start.1 = (bf16[128,2048]{1,0:T(8,128)(2,1)}, bf16[128,2048]{1,0:T(8,128)(2,1)S(1)}, u32[]{:S(2)}, u32[]{:S(2)}) collective-permute-start(bf16[128,2048]{1,0:T(8,128)(2,1)} %shard_map.232.refs_0_.refs_3_), channel_id=1, source_target_pairs={{0,16},{1,17},{2,18},{3,19},{4,20},{5,21},{6,22},{7,23},{8,24},{9,... | collective-permute-start | bytes 1572872 | tf_op jit(solution)/shard_map/ppermute | solution.py:716
  52.7 35.5 %collective-permute-start.2 = (bf16[128,2048]{1,0:T(8,128)(2,1)}, bf16[128,2048]{1,0:T(8,128)(2,1)S(1)}, u32[]{:S(2)}, u32[]{:S(2)}) collective-permute-start(bf16[128,2048]{1,0:T(8,128)(2,1)} %shard_map.232.refs_0_.refs_3_), channel_id=1, source_target_pairs={{0,24},{1,25},{2,26},{3,27},{4,28},{5,29},{6,30},{7,31},{8,0},{9,1... | collective-permute-start | bytes 1572872 | tf_op jit(solution)/shard_map/ppermute | solution.py:716
  107.4 166.8 %all-gather.10.cloned.1.call-start = ((), (), s32[]{:S(2)}) async-start(), calls=%async_computation.9 | async-start | bytes 12976128 | tf_op jit(solution)/shard_map/all_gather | solution.py:733
  114.1 40.5 %collective-permute-start.9 = (bf16[64,2816]{1,0:T(8,128)(2,1)}, bf16[64,2816]{1,0:T(8,128)(2,1)S(1)}, u32[]{:S(2)}, u32[]{:S(2)}) collective-permute-start(bf16[64,2816]{1,0:T(8,128)(2,1)} %get-tuple-element.63), channel_id=1, source_target_pairs={{0,8},{1,9},{2,10},{3,11},{4,12},{5,13},{6,14},{7,15},{8,16},{9,17... | collective-permute-start | bytes 1081352 | tf_op jit(solution)/shard_map/ppermute | solution.py:716
  116.0 44.6 %collective-permute-start.10 = (bf16[64,2816]{1,0:T(8,128)(2,1)}, bf16[64,2816]{1,0:T(8,128)(2,1)S(1)}, u32[]{:S(2)}, u32[]{:S(2)}) collective-permute-start(bf16[64,2816]{1,0:T(8,128)(2,1)} %get-tuple-element.64), channel_id=1, source_target_pairs={{0,16},{1,17},{2,18},{3,19},{4,20},{5,21},{6,22},{7,23},{8,24},{9,... | collective-permute-start | bytes 1081352 | tf_op jit(solution)/shard_map/ppermute | solution.py:716
  118.4 44.3 %collective-permute-start.11 = (bf16[64,2816]{1,0:T(8,128)(2,1)}, bf16[64,2816]{1,0:T(8,128)(2,1)S(1)}, u32[]{:S(2)}, u32[]{:S(2)}) collective-permute-start(bf16[64,2816]{1,0:T(8,128)(2,1)} %get-tuple-element.65), channel_id=1, source_target_pairs={{0,24},{1,25},{2,26},{3,27},{4,28},{5,29},{6,30},{7,31},{8,0},{9,1... | collective-permute-start | bytes 1081352 | tf_op jit(solution)/shard_map/ppermute | solution.py:716
  163.9 132.4 %all-gather.14.cloned.1.call-start = ((), (), s32[]{:S(2)}) async-start(), calls=%async_computation.11 | async-start | bytes 6488064 | tf_op jit(solution)/shard_map/all_gather | solution.py:733
  164.5 289.8 %reduce-scatter.3.cloned.1.call-start = ((), (), s32[]{:S(2)}) async-start(), calls=%async_computation.12 | async-start | bytes 12976128 | tf_op jit(solution)/shard_map/reduce_scatter | solution.py:736
  164.5 32.8 %collective-permute-start.3 = (bf16[128,2048]{1,0:T(8,128)(2,1)S(1)}, bf16[128,2048]{1,0:T(8,128)(2,1)S(1)}, u32[]{:S(2)}, u32[]{:S(2)}) collective-permute-start(bf16[128,2048]{1,0:T(8,128)(2,1)S(1)} %get-tuple-element.59.refs_3_), channel_id=1, source_target_pairs={{0,24},{1,25},{2,26},{3,27},{4,28},{5,29},{6,30},{7,31},{8,0},{9,1... | collective-permute-start | bytes 1572872 | tf_op jit(solution)/shard_map/ppermute | solution.py:716
  184.9 46.0 %collective-permute-start.4 = (bf16[128,2048]{1,0:T(8,128)(2,1)S(1)}, bf16[128,2048]{1,0:T(8,128)(2,1)S(1)}, u32[]{:S(2)}, u32[]{:S(2)}) collective-permute-start(bf16[128,2048]{1,0:T(8,128)(2,1)S(1)} %get-tuple-element.60.refs_4_), channel_id=1, source_target_pairs={{0,16},{1,17},{2,18},{3,19},{4,20},{5,21},{6,22},{7,23},{8,24},{9,... | collective-permute-start | bytes 1572872 | tf_op jit(solution)/shard_map/ppermute | solution.py:716
  185.5 45.4 %collective-permute-start.5 = (bf16[128,2048]{1,0:T(8,128)(2,1)S(1)}, bf16[128,2048]{1,0:T(8,128)(2,1)S(1)}, u32[]{:S(2)}, u32[]{:S(2)}) collective-permute-start(bf16[128,2048]{1,0:T(8,128)(2,1)S(1)} %get-tuple-element.61.refs_5_), channel_id=1, source_target_pairs={{0,8},{1,9},{2,10},{3,11},{4,12},{5,13},{6,14},{7,15},{8,16},{9,17... | collective-permute-start | bytes 1572872 | tf_op jit(solution)/shard_map/ppermute | solution.py:716
  234.9 37.5 %collective-permute-start.7 = (bf16[128,2048]{1,0:T(8,128)(2,1)}, bf16[128,2048]{1,0:T(8,128)(2,1)S(1)}, u32[]{:S(2)}, u32[]{:S(2)}) collective-permute-start(bf16[128,2048]{1,0:T(8,128)(2,1)} %get-tuple-element.62), channel_id=1, source_target_pairs={{0,16},{1,17},{2,18},{3,19},{4,20},{5,21},{6,22},{7,23},{8,24},{9,... | collective-permute-start | bytes 1572872 | tf_op jit(solution)/shard_map/ppermute | solution.py:716
  238.6 34.7 %collective-permute-start.8 = (bf16[128,2048]{1,0:T(8,128)(2,1)S(1)}, bf16[128,2048]{1,0:T(8,128)(2,1)S(1)}, u32[]{:S(2)}, u32[]{:S(2)}) collective-permute-start(bf16[128,2048]{1,0:T(8,128)(2,1)S(1)} %copy-done.71), channel_id=1, source_target_pairs={{0,24},{1,25},{2,26},{3,27},{4,28},{5,29},{6,30},{7,31},{8,0},{9,1... | collective-permute-start | bytes 1572872 | tf_op jit(solution)/shard_map/ppermute | solution.py:716
  320.3 45.7 %collective-permute-start.13 = (bf16[128,2048]{1,0:T(8,128)(2,1)S(1)}, bf16[128,2048]{1,0:T(8,128)(2,1)}, u32[]{:S(2)}, u32[]{:S(2)}) collective-permute-start(bf16[128,2048]{1,0:T(8,128)(2,1)S(1)} %get-tuple-element.67.refs_2_), channel_id=1, source_target_pairs={{0,16},{1,17},{2,18},{3,19},{4,20},{5,21},{6,22},{7,23},{8,24},{9,... | collective-permute-start | bytes 1572872 | tf_op jit(solution)/shard_map/ppermute | solution.py:716
  320.3 45.7 %collective-permute-start.14 = (bf16[128,2048]{1,0:T(8,128)(2,1)S(1)}, bf16[128,2048]{1,0:T(8,128)(2,1)}, u32[]{:S(2)}, u32[]{:S(2)}) collective-permute-start(bf16[128,2048]{1,0:T(8,128)(2,1)S(1)} %get-tuple-element.68.refs_3_), channel_id=1, source_target_pairs={{0,8},{1,9},{2,10},{3,11},{4,12},{5,13},{6,14},{7,15},{8,16},{9,17... | collective-permute-start | bytes 1572872 | tf_op jit(solution)/shard_map/ppermute | solution.py:716
  366.1 190.5 %reduce-scatter.5.cloned.1.call-start = ((), (), s32[]{:S(2)}) async-start(), calls=%async_computation.13 | async-start | bytes 10027008 | tf_op jit(solution)/shard_map/reduce_scatter | solution.py:736
  374.3 37.5 %collective-permute-start.16 = (bf16[128,2048]{1,0:T(8,128)(2,1)}, bf16[128,2048]{1,0:T(8,128)(2,1)}, u32[]{:S(2)}, u32[]{:S(2)}) collective-permute-start(bf16[128,2048]{1,0:T(8,128)(2,1)} %get-tuple-element.71.refs_1_.refs_0_), channel_id=1, source_target_pairs={{0,16},{1,17},{2,18},{3,19},{4,20},{5,21},{6,22},{7,23},{8,24},{9,... | collective-permute-start | bytes 1572872 | tf_op jit(solution)/shard_map/ppermute | solution.py:716
  376.9 34.9 %collective-permute-start.17 = (bf16[128,2048]{1,0:T(8,128)(2,1)}, bf16[128,2048]{1,0:T(8,128)(2,1)}, u32[]{:S(2)}, u32[]{:S(2)}) collective-permute-start(bf16[128,2048]{1,0:T(8,128)(2,1)} %get-tuple-element.71.refs_1_.refs_0_), channel_id=1, source_target_pairs={{0,24},{1,25},{2,26},{3,27},{4,28},{5,29},{6,30},{7,31},{8,0},{9,1... | collective-permute-start | bytes 1572872 | tf_op jit(solution)/shard_map/ppermute | solution.py:716
  395.7 79.7 %collective-permute-start.24 = (bf16[2,2,176,2048]{3,2,1,0:T(8,128)(2,1)}, bf16[2,2,176,2048]{3,2,1,0:T(8,128)(2,1)}, u32[]{:S(2)}, u32[]{:S(2)}) collective-permute-start(bf16[2,2,176,2048]{3,2,1,0:T(8,128)(2,1)} %dynamic-slice_bitcast_fusion), channel_id=1, source_target_pairs={{0,1},{1,0},{2,3},{3,2},{4,5},{5,4},{6,7},{7,6},{8,9},{9,8},{10,11... | collective-permute-start | bytes 8650760 | tf_op jit(solution)/shard_map/ppermute | solution.py:749
  411.8 55.7 %collective-permute-start.18 = (bf16[128,2048]{1,0:T(8,128)(2,1)}, bf16[128,2048]{1,0:T(8,128)(2,1)}, u32[]{:S(2)}, u32[]{:S(2)}) collective-permute-start(bf16[128,2048]{1,0:T(8,128)(2,1)} %get-tuple-element.76), channel_id=1, source_target_pairs={{0,24},{1,25},{2,26},{3,27},{4,28},{5,29},{6,30},{7,31},{8,0},{9,1... | collective-permute-start | bytes 1572872 | tf_op jit(solution)/shard_map/ppermute | solution.py:716
  423.8 45.2 %collective-permute-start.19 = (bf16[128,2048]{1,0:T(8,128)(2,1)}, bf16[128,2048]{1,0:T(8,128)(2,1)}, u32[]{:S(2)}, u32[]{:S(2)}) collective-permute-start(bf16[128,2048]{1,0:T(8,128)(2,1)} %get-tuple-element.77), channel_id=1, source_target_pairs={{0,16},{1,17},{2,18},{3,19},{4,20},{5,21},{6,22},{7,23},{8,24},{9,... | collective-permute-start | bytes 1572872 | tf_op jit(solution)/shard_map/ppermute | solution.py:716
  424.1 45.0 %collective-permute-start.20 = (bf16[128,2048]{1,0:T(8,128)(2,1)}, bf16[128,2048]{1,0:T(8,128)(2,1)}, u32[]{:S(2)}, u32[]{:S(2)}) collective-permute-start(bf16[128,2048]{1,0:T(8,128)(2,1)} %get-tuple-element.78), channel_id=1, source_target_pairs={{0,8},{1,9},{2,10},{3,11},{4,12},{5,13},{6,14},{7,15},{8,16},{9,17... | collective-permute-start | bytes 1572872 | tf_op jit(solution)/shard_map/ppermute | solution.py:716
  472.8 45.1 %collective-permute-start.21 = (bf16[128,2048]{1,0:T(8,128)(2,1)}, bf16[128,2048]{1,0:T(8,128)(2,1)}, u32[]{:S(2)}, u32[]{:S(2)}) collective-permute-start(bf16[128,2048]{1,0:T(8,128)(2,1)} %get-tuple-element.89.refs_1_), channel_id=1, source_target_pairs={{0,24},{1,25},{2,26},{3,27},{4,28},{5,29},{6,30},{7,31},{8,0},{9,1... | collective-permute-start | bytes 1572872 | tf_op jit(solution)/shard_map/ppermute | solution.py:716
  474.6 62.7 %collective-permute-start.22 = (bf16[128,2048]{1,0:T(8,128)(2,1)}, bf16[128,2048]{1,0:T(8,128)(2,1)}, u32[]{:S(2)}, u32[]{:S(2)}) collective-permute-start(bf16[128,2048]{1,0:T(8,128)(2,1)} %get-tuple-element.90.refs_2_), channel_id=1, source_target_pairs={{0,16},{1,17},{2,18},{3,19},{4,20},{5,21},{6,22},{7,23},{8,24},{9,... | collective-permute-start | bytes 1572872 | tf_op jit(solution)/shard_map/ppermute | solution.py:716
  475.1 62.3 %collective-permute-start.23 = (bf16[128,2048]{1,0:T(8,128)(2,1)}, bf16[128,2048]{1,0:T(8,128)(2,1)}, u32[]{:S(2)}, u32[]{:S(2)}) collective-permute-start(bf16[128,2048]{1,0:T(8,128)(2,1)} %get-tuple-element.91.refs_3_), channel_id=1, source_target_pairs={{0,8},{1,9},{2,10},{3,11},{4,12},{5,13},{6,14},{7,15},{8,16},{9,17... | collective-permute-start | bytes 1572872 | tf_op jit(solution)/shard_map/ppermute | solution.py:716
  480.7 33.4 %collective-permute-start.25 = (bf16[2,176,1024]{2,1,0:T(8,128)(2,1)}, bf16[2,176,1024]{2,1,0:T(8,128)(2,1)}, u32[]{:S(2)}, u32[]{:S(2)}) collective-permute-start(bf16[2,176,1024]{2,1,0:T(8,128)(2,1)} %dynamic-slice_bitcast_fusion.3), channel_id=1, source_target_pairs={{0,2},{1,3},{2,0},{3,1},{4,6},{5,7},{6,4},{7,5},{8,10},{9,11},{10,... | collective-permute-start | bytes 2162696 | tf_op jit(solution)/shard_map/ppermute | solution.py:749
  483.0 33.7 %collective-permute-start.26 = (bf16[2,176,1024]{2,1,0:T(8,128)(2,1)}, bf16[2,176,1024]{2,1,0:T(8,128)(2,1)S(1)}, u32[]{:S(2)}, u32[]{:S(2)}) collective-permute-start(bf16[2,176,1024]{2,1,0:T(8,128)(2,1)} %dynamic-slice_bitcast_fusion.2), channel_id=1, source_target_pairs={{0,4},{1,5},{2,6},{3,7},{4,0},{5,1},{6,2},{7,3},{8,12},{9,13},{10,... | collective-permute-start | bytes 2162696 | tf_op jit(solution)/shard_map/ppermute | solution.py:749
  483.8 66.4 %all-to-all-start.3 = ((bf16[4,64,2816]{2,1,0:T(8,128)(2,1)}), bf16[4,64,2816]{2,1,0:T(8,128)(2,1)S(1)}, u32[]{:S(2)}, u32[]{:S(2)}) async-start(bf16[4,64,2816]{2,1,0:T(8,128)(2,1)} %bitcast.140), calls=%async_computation.5 | async-start | bytes 2883584 | tf_op jit(solution)/shard_map/all_to_all | solution.py:706
  564.5 31.1 %all-to-all-start.4 = ((bf16[4,64,2176]{2,1,0:T(8,128)(2,1)}), bf16[4,64,2176]{2,1,0:T(8,128)(2,1)S(1)}, u32[]{:S(2)}, u32[]{:S(2)}) async-start(bf16[4,64,2176]{2,1,0:T(8,128)(2,1)} %bitcast.48), calls=%async_computation.6 | async-start | bytes 2228224 | tf_op jit(solution)/shard_map/all_to_all | solution.py:706
  (102 other events, 884.1 us)
Sparse Core Ops, SparseCore 0:
  10.5 30.5 all-gather.5
  48.5 55.7 all-gather.7
  105.8 76.5 all-gather.11
  184.7 66.4 all-gather.9
  252.9 43.3 all-gather.13
  366.2 85.9 reduce-scatter.2
  455.8 88.5 reduce-scatter.4

commit v2 on v1

--- a/solution.py
+++ b/solution.py
@@ -715,13 +715,11 @@
         ]
         return lax.ppermute(values, "dp", pairs)
 
-    def exchange_apart(values, before, after=()):
-        cut = [
+    def cut_pieces(values):
+        return [
             lax.dynamic_index_in_dim(values, (part + step) % parts, 0, keepdims=False)
             for step in range(1, parts)
         ]
-        received = [shift(piece, step) for step, piece in enumerate(tie_all(cut, *before), 1)]
-        return assemble(part, values, received, after)
 
     def gather_rows(values):
         return [values] + [shift(values, step) for step in range(1, parts)]
@@ -792,13 +790,17 @@
     inputs = tie(to_wire(block_in), mixer_pieces)
     input_rows = gather_rows(inputs)
 
+    pieces = [(updown_weight, half, units) for half in range(2)]
+    updown_pieces = to_parts(pieces, parts, bf, [mixer_pieces])
+    cut = cut_pieces(updown_pieces)
+
     lanes = -(-3 * rows_own // 128) * 128
     numbers = jnp.concatenate([seq_blocks[0], lead_blocks]).astype(f32)
     small = [conv_weight.T, norm1_gain[None], head_gain[None], norm2_gain[None], numbers[None]]
     small = [jnp.pad(rows, ((0, 0), (0, lanes - rows.shape[1]))) for rows in small]
     small = jnp.pad(jnp.concatenate(small, 0).astype(bf), ((0, 2 * KERNEL), (0, 0)))
     small = jnp.broadcast_to(small[None], (devices,) + small.shape)
-    small = lax.all_to_all(tie(small, *input_rows[1:]), "dp", 0, 0, tiled=True)
+    small = lax.all_to_all(tie(small, *cut, *input_rows[1:]), "dp", 0, 0, tiled=True)
     taps = small[:, :KERNEL, : 3 * rows_own].swapaxes(0, 1).reshape(KERNEL, 3, parts, width)
     taps = lax.dynamic_index_in_dim(taps, part, 2, keepdims=False).reshape(KERNEL, 3 * width)
     gain_one, head_full, gain_two = (
@@ -816,8 +818,6 @@
     wanted = (wanted[:, None] == jnp.arange(parts)).astype(f32)
     layouts = jnp.sum(wanted[:, :, None] * layouts, 1)
 
-    pieces = [(updown_weight, half, units) for half in range(2)]
-    updown_pieces = to_parts(pieces, parts, bf, [mixer_pieces])
     w_down_own = to_wire(down_weight.astype(bf))
     w_down = gather_copies(tie(w_down_own, *input_rows[1:]))
     cotangent_own = to_wire(out_grad)
@@ -829,7 +829,9 @@
     normed, pre = normed_product(input_rows, gain_first, w_mixer)
     mixed, *kept = mixer_forward(layouts, pre, params, width)
     out_terms = product_blocks(mixed, w_out)
-    updown_pieces = exchange_apart(updown_pieces, input_rows[1:], out_terms[1:])
+    cut = tie_all(cut, *input_rows[1:])
+    received = [shift(piece, step) for step, piece in enumerate(cut, 1)]
+    updown_pieces = assemble(part, updown_pieces, received, out_terms[1:])
     w_updown = gather_copies(updown_pieces.reshape(parts * rows_own, 2 * units))
     stream = ((GROUP_ROWS, D), f32)
     narrow = ((GROUP_ROWS, D), bf)

time: 616 us -> 618 us (level)
    ppermute x24, waiting for transfers between devices: 171 us -> 159 us  [shift(): return lax.ppermute(values, 'dp', pairs)]
    all_to_all x1, waiting for transfers between devices: 0.01 us -> 10.3 us  [body(): lax.all_to_all(tie(small, *cut, *input_rows[1:]), 'dp', 0, 0, tiled=True)]
    unnamed x188 -> x190, local copies, waits for them, and re-layouts: 38.4 us -> 37.3 us
  transfers between devices with their start and end apart: 45 -> 45, of which waited for: 20 -> 19; matrix products, arithmetic and copies ran while one was open for 12% -> 12% of each run, Pallas kernels for 19% -> 19%
where the time goes in v2:
time: 618 us; the launch traced here: 608 us
  waiting for transfers between devices  218 us (35%)
  Pallas kernels  129 us (21%)
  starting transfers between devices  95.6 us (15%)
  local copies, waits for them, and re-layouts  68.6 us (11%)
  blocking collectives  33.6 us (5%)
  other arithmetic  24.7 us (4%)
  matrix products  21.4 us (3%)
  between operations  16.4 us (3%)
    ppermute x24, waiting for transfers between devices, shift(): return lax.ppermute(values, 'dp', pairs)  159 us
    pallas_call x12, Pallas kernels, call(): pl.pallas_call(kernel, grid=grid, in_specs=in_specs, out_specs=out_specs,...  100 us
    ppermute x24, starting transfers between devices, shift(): return lax.ppermute(values, 'dp', pairs)  60.6 us
    unnamed x190, local copies, waits for them, and re-layouts  37.3 us
    all_to_all x1, blocking collectives, exchange(): lax.all_to_all(values, 'dp', split_axis=0, concat_axis=0, axis_index_grou...  33.6 us
    ppermute x10, waiting for transfers between devices, halves_across(): return (own, lax.ppermute(other, 'dp', pairs))  28 us
    pallas_call x4, Pallas kernels, by_rows(): pl.pallas_call(kernel, grid=(GROUP_ROWS // block,), in_specs=[spec(array....  14.6 us
    all_to_all x1, starting transfers between devices, body(): lax.all_to_all(tie(small, *cut, *input_rows[1:]), 'dp', 0, 0, tiled=True)  12.9 us
  transfers between devices with their start and end apart: 45, of which 19 were waited for; matrix products, arithmetic and copies ran while one was open for 12% of the time, Pallas kernels for 19%

profile of v2, /device:TPU:0, one launch (start us, length us, event | category | flops | bytes accessed | tf_op | source)
XLA Modules:
  0.0 607.6 jit_solution(16945324361739712580)
XLA Ops:
  14.8 33.6 %all_to_all.25.refs_0_ = bf16[4,64,2176]{2,1,0:T(8,128)(2,1)} all-to-all(bf16[4,64,2176]{2,1,0:T(8,128)(2,1)} %shard_map.230), channel_id=1, replica_groups={{0,8,16,24},{1,9,17,25},{2,10,18,26},{3,11,19,27},{4,12,20,28},{5,13,21..., dimensions={0} | all-to-all | bytes 2228224 | tf_op jit(solution)/shard_map/all_to_all | solution.py:706
  55.9 11.7 %collective-permute-done.refs_4_.refs_1_.refs_3_ = bf16[128,2048]{1,0:T(8,128)(2,1)S(1)} collective-permute-done((bf16[128,2048]{1,0:T(8,128)(2,1)}, bf16[128,2048]{1,0:T(8,128)(2,1)S(1)}, u32[]{:S(2)}, u32[]{:S(2)}) %collective-permute-start) | collective-permute-done | bytes 524320 | tf_op jit(solution)/shard_map/ppermute | solution.py:716
  67.7 20.5 %collective-permute-done.1.refs_5_.refs_2_.refs_4_ = bf16[128,2048]{1,0:T(8,128)(2,1)S(1)} collective-permute-done((bf16[128,2048]{1,0:T(8,128)(2,1)}, bf16[128,2048]{1,0:T(8,128)(2,1)S(1)}, u32[]{:S(2)}, u32[]{:S(2)}) %collective-permute-start.1) | collective-permute-done | bytes 524320 | tf_op jit(solution)/shard_map/ppermute | solution.py:716
  97.7 12.9 %all-to-all-start.1 = ((bf16[32,16,256]{2,1,0:T(8,128)(2,1)}), bf16[32,16,256]{2,1,0:T(8,128)(2,1)}, u32[]{:S(2)}, u32[]{:S(2)}) async-start(bf16[32,16,256]{2,1,0:T(8,128)(2,1)} %shard_map.234), calls=%async_computation.1 | async-start | bytes 524288 | tf_op jit(solution)/shard_map/all_to_all | solution.py:803
  118.3 10.3 %all-to-all-done.1 = bf16[32,16,256]{2,1,0:T(8,128)(2,1)} async-done(((bf16[32,16,256]{2,1,0:T(8,128)(2,1)}), bf16[32,16,256]{2,1,0:T(8,128)(2,1)}, u32[]{:S(2)}, u32[]{:S(2)}) %all-to-all-start.1) | async-done | bytes 262176 | tf_op jit(solution)/shard_map/all_to_all | solution.py:803
  134.9 10.9 %shard_map.236 = (bf16[512,2048]{1,0:T(8,128)(2,1)S(1)}, f32[512,2176]{1,0:T(8,128)}) custom-call(f32[1,2048]{1,0:T(1,128)S(1)} %copy-done.54, bf16[2048,2176]{1,0:T(8,128)(2,1)} %all-gather.8.cloned.1.call-done.weight_ref.right_ref, bf16[128,2048]{1,0:T(8,128)(2,1)S(1)} %copy-done.2, bf16[128,2048]{1,0:T(8,128)(2,1)S(1)} %copy-done.6, ...), custom_call_target="tpu_custom_call" | custom-call | tf_op jit(solution)/shard_map/pallas_call | solution.py:277
  149.4 14.8 %shard_map.237 = (bf16[512,512]{1,0:T(8,128)(2,1)S(1)}, f32[16,128,128]{2,1,0:T(8,128)}, f32[16,128,128]{2,1,0:T(8,128)}, f32[16,128,128]{2,1,0:T(8,128)}, f32[16,128,128]{2,1,0:T(8,128)}) custom-call(f32[4,4]{1,0:T(4,128)S(1)} %multiply_reduce_fusion.layout_ref, f32[512,2176]{1,0:T(8,128)S(1)} %copy-done.37, f32[8,1536]{1,0:T(8,128)S(1)} %pad.57.param_ref.refs_0_), custom_call_target="tpu_custom_call" | custom-call | tf_op jit(solution)/shard_map/pallas_call | solution.py:277
  168.4 19.4 %collective-permute-start.3 = (bf16[128,2048]{1,0:T(8,128)(2,1)S(1)}, bf16[128,2048]{1,0:T(8,128)(2,1)S(1)}, u32[]{:S(2)}, u32[]{:S(2)}) collective-permute-start(bf16[128,2048]{1,0:T(8,128)(2,1)S(1)} %get-tuple-element.59.refs_3_), channel_id=1, source_target_pairs={{0,24},{1,25},{2,26},{3,27},{4,28},{5,29},{6,30},{7,31},{8,0},{9,1... | collective-permute-start | bytes 1572872 | tf_op jit(solution)/shard_map/ppermute | solution.py:716
  189.3 10.9 %collective-permute-done.3.refs_0_ = bf16[128,2048]{1,0:T(8,128)(2,1)S(1)} collective-permute-done((bf16[128,2048]{1,0:T(8,128)(2,1)S(1)}, bf16[128,2048]{1,0:T(8,128)(2,1)S(1)}, u32[]{:S(2)}, u32[]{:S(2)}) %collective-permute-start.3) | collective-permute-done | bytes 524320 | tf_op jit(solution)/shard_map/ppermute | solution.py:716
  200.2 32.5 %collective-permute-done.4.refs_1_ = bf16[128,2048]{1,0:T(8,128)(2,1)S(1)} collective-permute-done((bf16[128,2048]{1,0:T(8,128)(2,1)S(1)}, bf16[128,2048]{1,0:T(8,128)(2,1)S(1)}, u32[]{:S(2)}, u32[]{:S(2)}) %collective-permute-start.4) | collective-permute-done | bytes 524320 | tf_op jit(solution)/shard_map/ppermute | solution.py:716
  245.6 8.0 %collective-permute-done.6 = bf16[128,2048]{1,0:T(8,128)(2,1)} collective-permute-done((bf16[128,2048]{1,0:T(8,128)(2,1)}, bf16[128,2048]{1,0:T(8,128)(2,1)}, u32[]{:S(2)}, u32[]{:S(2)}) %collective-permute-start.6) | collective-permute-done | bytes 524320 | tf_op jit(solution)/shard_map/ppermute | solution.py:716
  255.5 17.2 %collective-permute-done.7 = bf16[128,2048]{1,0:T(8,128)(2,1)S(1)} collective-permute-done((bf16[128,2048]{1,0:T(8,128)(2,1)}, bf16[128,2048]{1,0:T(8,128)(2,1)S(1)}, u32[]{:S(2)}, u32[]{:S(2)}) %collective-permute-start.7) | collective-permute-done | bytes 524320 | tf_op jit(solution)/shard_map/ppermute | solution.py:716
  274.4 12.5 %fusion.30 = f32[512,2816]{1,0:T(8,128)} fusion(bf16[512,2048]{1,0:T(8,128)(2,1)} %constant_dynamic-update-slice_fusion.left_ref, bf16[2048,2816]{1,0:T(8,128)(2,1)} %all-gather.10.cloned.1.call-done.right_ref), kind=kOutput, calls=%fused_computation.120 | convolution fusion | flops 5905580032 | bytes 19398656 | tf_op jit(solution)/shard_map/dot_general | solution.py:37
  286.9 11.8 %all-gather.14.cloned.1.call-done.right_ref = bf16[1408,2048]{1,0:T(8,128)(2,1)} async-done(((bf16[176,2048]{1,0:T(8,128)(2,1)}), bf16[1408,2048]{1,0:T(8,128)(2,1)}) %all-gather.14.cloned.1.call-update) | async-done | bytes 5767184 | tf_op jit(solution)/shard_map/all_gather | solution.py:731
  298.8 8.9 %fusion.21 = (f32[512,1408]{1,0:T(8,128)S(1)}, f32[512,1408]{1,0:T(8,128)S(1)}, bf16[512,1408]{1,0:T(8,128)(2,1)}) fusion(f32[512,2816]{1,0:T(8,128)} %fusion.30, bf16[512,2048]{1,0:T(8,128)(2,1)S(1)} %shard_map.243.right_ref, bf16[1408,2048]{1,0:T(8,128)(2,1)} %all-gather.14.cloned.1.call-done.right_ref), kind=kOutput, calls=%fused_computation.52 | convolution fusion | flops 2962882560 | bytes 20840448 | tf_op jit(solution)/shard_map/dot_general | solution.py:45
  308.0 10.5 %shard_map.245 = (f32[128,2048]{1,0:T(8,128)S(1)}, bf16[128,2048]{1,0:T(8,128)(2,1)}, bf16[128,2048]{1,0:T(8,128)(2,1)S(1)}, bf16[128,2048]{1,0:T(8,128)(2,1)S(1)}) custom-call(bf16[512,2816]{1,0:T(8,128)(2,1)S(1)} %add_convert_fusion.left_ref.refs_0_, bf16[2048,2816]{1,0:T(8,128)(2,1)} %all-gather.10.cloned.1.call-done.right_ref), custom_call_target="tpu_custom_call" | custom-call | tf_op jit(solution)/shard_map/pallas_call | solution.py:277
  325.3 7.8 %shard_map.247.refs_1_.refs_0_ = bf16[1408,2048]{1,0:T(8,128)(2,1)} custom-call(bf16[512,1408]{1,0:T(8,128)(2,1)S(1)} %copy-done.17, bf16[512,2048]{1,0:T(8,128)(2,1)S(1)} %shard_map.243.right_ref), custom_call_target="tpu_custom_call" | custom-call | tf_op jit(solution)/shard_map/pallas_call | solution.py:277
  335.0 10.6 %shard_map.249.refs_1_.refs_0_ = bf16[2048,2816]{1,0:T(8,128)(2,1)} custom-call(bf16[512,2048]{1,0:T(8,128)(2,1)} %constant_dynamic-update-slice_fusion.left_ref, bf16[512,2816]{1,0:T(8,128)(2,1)S(1)} %copy-done.1), custom_call_target="tpu_custom_call" | custom-call | tf_op jit(solution)/shard_map/pallas_call | solution.py:277
  345.6 22.9 %collective-permute-done.13.refs_1_.refs_3_ = bf16[128,2048]{1,0:T(8,128)(2,1)} collective-permute-done((bf16[128,2048]{1,0:T(8,128)(2,1)S(1)}, bf16[128,2048]{1,0:T(8,128)(2,1)}, u32[]{:S(2)}, u32[]{:S(2)}) %collective-permute-start.13) | collective-permute-done | bytes 524320 | tf_op jit(solution)/shard_map/ppermute | solution.py:716
  372.2 4.5 shard_map.251
  384.6 6.0 shard_map.253
  393.9 4.2 dynamic-slice_bitcast_fusion
  400.2 14.0 %collective-permute-done.16.refs_4_.refs_2_ = bf16[128,2048]{1,0:T(8,128)(2,1)} collective-permute-done((bf16[128,2048]{1,0:T(8,128)(2,1)}, bf16[128,2048]{1,0:T(8,128)(2,1)}, u32[]{:S(2)}, u32[]{:S(2)}) %collective-permute-start.16) | collective-permute-done | bytes 524320 | tf_op jit(solution)/shard_map/ppermute | solution.py:716
  414.2 12.0 %collective-permute-start.18 = (bf16[128,2048]{1,0:T(8,128)(2,1)}, bf16[128,2048]{1,0:T(8,128)(2,1)}, u32[]{:S(2)}, u32[]{:S(2)}) collective-permute-start(bf16[128,2048]{1,0:T(8,128)(2,1)} %get-tuple-element.76), channel_id=1, source_target_pairs={{0,24},{1,25},{2,26},{3,27},{4,28},{5,29},{6,30},{7,31},{8,0},{9,1... | collective-permute-start | bytes 1572872 | tf_op jit(solution)/shard_map/ppermute | solution.py:716
  428.1 17.9 %shard_map.256 = (bf16[512,2176]{1,0:T(8,128)(2,1)}, f32[8,1536]{1,0:T(8,128)S(1)}) custom-call(f32[4,4]{1,0:T(4,128)S(1)} %multiply_reduce_fusion.layout_ref, f32[512,2176]{1,0:T(8,128)} %get-tuple-element.56.pre_ref, f32[8,1536]{1,0:T(8,128)S(1)} %copy-done.52, bf16[512,2048]{1,0:T(8,128)(2,1)S(1)} %copy-done.25, ...), custom_call_target="tpu_custom_call" | custom-call | flops 60000002048 | tf_op jit(solution)/shard_map/pallas_call | solution.py:277
  448.3 8.3 %shard_map.257.refs_0_ = bf16[2048,2176]{1,0:T(8,128)(2,1)} custom-call(bf16[512,2048]{1,0:T(8,128)(2,1)S(1)} %copy-done.57, bf16[512,2176]{1,0:T(8,128)(2,1)S(1)} %copy-done.39), custom_call_target="tpu_custom_call" | custom-call | flops 20000000000 | tf_op jit(solution)/shard_map/pallas_call | solution.py:277
  458.2 8.3 %shard_map.261 = (f32[128,2048]{1,0:T(8,128)S(1)}, bf16[128,2048]{1,0:T(8,128)(2,1)S(1)}, bf16[128,2048]{1,0:T(8,128)(2,1)S(1)}, bf16[128,2048]{1,0:T(8,128)(2,1)S(1)}) custom-call(bf16[512,2176]{1,0:T(8,128)(2,1)S(1)} %copy-done.40, bf16[2048,2176]{1,0:T(8,128)(2,1)} %all-gather.8.cloned.1.call-done.weight_ref.right_ref), custom_call_target="tpu_custom_call" | custom-call | flops 149999992832 | tf_op jit(solution)/shard_map/pallas_call | solution.py:277
  486.3 5.3 all-to-all-start.3
  497.7 18.8 %collective-permute-done.25 = bf16[2,176,1024]{2,1,0:T(8,128)(2,1)} collective-permute-done((bf16[2,176,1024]{2,1,0:T(8,128)(2,1)}, bf16[2,176,1024]{2,1,0:T(8,128)(2,1)}, u32[]{:S(2)}, u32[]{:S(2)}) %collective-permute-start.25) | collective-permute-done | bytes 720928 | tf_op jit(solution)/shard_map/ppermute | solution.py:747
  520.2 19.5 %collective-permute-done.22.refs_1_ = bf16[128,2048]{1,0:T(8,128)(2,1)} collective-permute-done((bf16[128,2048]{1,0:T(8,128)(2,1)}, bf16[128,2048]{1,0:T(8,128)(2,1)}, u32[]{:S(2)}, u32[]{:S(2)}) %collective-permute-start.22) | collective-permute-done | bytes 524320 | tf_op jit(solution)/shard_map/ppermute | solution.py:716
  559.0 7.9 %all-to-all-done.2 = f32[32,16,128]{2,1,0:T(8,128)} async-done(((f32[32,16,128]{2,1,0:T(8,128)}), f32[32,16,128]{2,1,0:T(8,128)}, u32[]{:S(2)}, u32[]{:S(2)}) %all-to-all-start.2) | async-done | bytes 262176 | tf_op jit(solution)/shard_map/all_to_all | solution.py:915
  582.7 7.0 %collective-permute-done.30 = bf16[2,64,1024]{2,1,0:T(8,128)(2,1)S(1)} collective-permute-done((bf16[2,64,1024]{2,1,0:T(8,128)(2,1)S(1)}, bf16[2,64,1024]{2,1,0:T(8,128)(2,1)S(1)}, u32[]{:S(2)}, u32[]{:S(2)}) %collective-permute-start.30) | collective-permute-done | bytes 262176 | tf_op jit(solution)/shard_map/ppermute | solution.py:747
  (430 shorter events, 169.5 us)
Async XLA Ops:
  7.2 41.1 %all-gather.6.cloned.1.call-start = ((), (), s32[]{:S(2)}) async-start(), calls=%async_computation.7 | async-start | bytes 2359296 | tf_op jit(solution)/shard_map/all_gather | solution.py:731
  10.2 123.9 %all-gather.8.cloned.1.call-start = ((), (), s32[]{:S(2)}) async-start(), calls=%async_computation.8 | async-start | bytes 10027008 | tf_op jit(solution)/shard_map/all_gather | solution.py:731
  48.4 190.9 %all-gather.12.cloned.1.call-start = ((), (), s32[]{:S(2)}) async-start(), calls=%async_computation.10 | async-start | bytes 2621440 | tf_op jit(solution)/shard_map/all_gather | solution.py:825
  51.1 37.1 %collective-permute-start.1 = (bf16[128,2048]{1,0:T(8,128)(2,1)}, bf16[128,2048]{1,0:T(8,128)(2,1)S(1)}, u32[]{:S(2)}, u32[]{:S(2)}) collective-permute-start(bf16[128,2048]{1,0:T(8,128)(2,1)} %shard_map.233.refs_0_.refs_3_), channel_id=1, source_target_pairs={{0,16},{1,17},{2,18},{3,19},{4,20},{5,21},{6,22},{7,23},{8,24},{9,... | collective-permute-start | bytes 1572872 | tf_op jit(solution)/shard_map/ppermute | solution.py:716
  52.7 35.5 %collective-permute-start.2 = (bf16[128,2048]{1,0:T(8,128)(2,1)}, bf16[128,2048]{1,0:T(8,128)(2,1)S(1)}, u32[]{:S(2)}, u32[]{:S(2)}) collective-permute-start(bf16[128,2048]{1,0:T(8,128)(2,1)} %shard_map.233.refs_0_.refs_3_), channel_id=1, source_target_pairs={{0,24},{1,25},{2,26},{3,27},{4,28},{5,29},{6,30},{7,31},{8,0},{9,1... | collective-permute-start | bytes 1572872 | tf_op jit(solution)/shard_map/ppermute | solution.py:716
  110.7 163.8 %all-gather.10.cloned.1.call-start = ((), (), s32[]{:S(2)}) async-start(), calls=%async_computation.9 | async-start | bytes 12976128 | tf_op jit(solution)/shard_map/all_gather | solution.py:731
  112.7 53.6 %collective-permute-start.9 = (bf16[64,2816]{1,0:T(8,128)(2,1)}, bf16[64,2816]{1,0:T(8,128)(2,1)S(1)}, u32[]{:S(2)}, u32[]{:S(2)}) collective-permute-start(bf16[64,2816]{1,0:T(8,128)(2,1)} %get-tuple-element.63), channel_id=1, source_target_pairs={{0,8},{1,9},{2,10},{3,11},{4,12},{5,13},{6,14},{7,15},{8,16},{9,17... | collective-permute-start | bytes 1081352 | tf_op jit(solution)/shard_map/ppermute | solution.py:716
  114.5 51.8 %collective-permute-start.10 = (bf16[64,2816]{1,0:T(8,128)(2,1)}, bf16[64,2816]{1,0:T(8,128)(2,1)S(1)}, u32[]{:S(2)}, u32[]{:S(2)}) collective-permute-start(bf16[64,2816]{1,0:T(8,128)(2,1)} %get-tuple-element.64), channel_id=1, source_target_pairs={{0,16},{1,17},{2,18},{3,19},{4,20},{5,21},{6,22},{7,23},{8,24},{9,... | collective-permute-start | bytes 1081352 | tf_op jit(solution)/shard_map/ppermute | solution.py:716
  116.9 49.4 %collective-permute-start.11 = (bf16[64,2816]{1,0:T(8,128)(2,1)}, bf16[64,2816]{1,0:T(8,128)(2,1)S(1)}, u32[]{:S(2)}, u32[]{:S(2)}) collective-permute-start(bf16[64,2816]{1,0:T(8,128)(2,1)} %get-tuple-element.65), channel_id=1, source_target_pairs={{0,24},{1,25},{2,26},{3,27},{4,28},{5,29},{6,30},{7,31},{8,0},{9,1... | collective-permute-start | bytes 1081352 | tf_op jit(solution)/shard_map/ppermute | solution.py:716
  167.8 131.0 %all-gather.14.cloned.1.call-start = ((), (), s32[]{:S(2)}) async-start(), calls=%async_computation.11 | async-start | bytes 6488064 | tf_op jit(solution)/shard_map/all_gather | solution.py:731
  168.3 288.3 %reduce-scatter.3.cloned.1.call-start = ((), (), s32[]{:S(2)}) async-start(), calls=%async_computation.12 | async-start | bytes 12976128 | tf_op jit(solution)/shard_map/reduce_scatter | solution.py:734
  168.4 31.8 %collective-permute-start.3 = (bf16[128,2048]{1,0:T(8,128)(2,1)S(1)}, bf16[128,2048]{1,0:T(8,128)(2,1)S(1)}, u32[]{:S(2)}, u32[]{:S(2)}) collective-permute-start(bf16[128,2048]{1,0:T(8,128)(2,1)S(1)} %get-tuple-element.59.refs_3_), channel_id=1, source_target_pairs={{0,24},{1,25},{2,26},{3,27},{4,28},{5,29},{6,30},{7,31},{8,0},{9,1... | collective-permute-start | bytes 1572872 | tf_op jit(solution)/shard_map/ppermute | solution.py:716
  187.8 44.9 %collective-permute-start.4 = (bf16[128,2048]{1,0:T(8,128)(2,1)S(1)}, bf16[128,2048]{1,0:T(8,128)(2,1)S(1)}, u32[]{:S(2)}, u32[]{:S(2)}) collective-permute-start(bf16[128,2048]{1,0:T(8,128)(2,1)S(1)} %get-tuple-element.60.refs_4_), channel_id=1, source_target_pairs={{0,16},{1,17},{2,18},{3,19},{4,20},{5,21},{6,22},{7,23},{8,24},{9,... | collective-permute-start | bytes 1572872 | tf_op jit(solution)/shard_map/ppermute | solution.py:716
  188.4 44.2 %collective-permute-start.5 = (bf16[128,2048]{1,0:T(8,128)(2,1)S(1)}, bf16[128,2048]{1,0:T(8,128)(2,1)S(1)}, u32[]{:S(2)}, u32[]{:S(2)}) collective-permute-start(bf16[128,2048]{1,0:T(8,128)(2,1)S(1)} %get-tuple-element.61.refs_5_), channel_id=1, source_target_pairs={{0,8},{1,9},{2,10},{3,11},{4,12},{5,13},{6,14},{7,15},{8,16},{9,17... | collective-permute-start | bytes 1572872 | tf_op jit(solution)/shard_map/ppermute | solution.py:716
  237.3 35.4 %collective-permute-start.7 = (bf16[128,2048]{1,0:T(8,128)(2,1)}, bf16[128,2048]{1,0:T(8,128)(2,1)S(1)}, u32[]{:S(2)}, u32[]{:S(2)}) collective-permute-start(bf16[128,2048]{1,0:T(8,128)(2,1)} %get-tuple-element.62), channel_id=1, source_target_pairs={{0,16},{1,17},{2,18},{3,19},{4,20},{5,21},{6,22},{7,23},{8,24},{9,... | collective-permute-start | bytes 1572872 | tf_op jit(solution)/shard_map/ppermute | solution.py:716
  241.9 31.7 %collective-permute-start.8 = (bf16[128,2048]{1,0:T(8,128)(2,1)S(1)}, bf16[128,2048]{1,0:T(8,128)(2,1)S(1)}, u32[]{:S(2)}, u32[]{:S(2)}) collective-permute-start(bf16[128,2048]{1,0:T(8,128)(2,1)S(1)} %copy-done.72), channel_id=1, source_target_pairs={{0,24},{1,25},{2,26},{3,27},{4,28},{5,29},{6,30},{7,31},{8,0},{9,1... | collective-permute-start | bytes 1572872 | tf_op jit(solution)/shard_map/ppermute | solution.py:716
  322.8 45.7 %collective-permute-start.13 = (bf16[128,2048]{1,0:T(8,128)(2,1)S(1)}, bf16[128,2048]{1,0:T(8,128)(2,1)}, u32[]{:S(2)}, u32[]{:S(2)}) collective-permute-start(bf16[128,2048]{1,0:T(8,128)(2,1)S(1)} %get-tuple-element.67.refs_2_), channel_id=1, source_target_pairs={{0,16},{1,17},{2,18},{3,19},{4,20},{5,21},{6,22},{7,23},{8,24},{9,... | collective-permute-start | bytes 1572872 | tf_op jit(solution)/shard_map/ppermute | solution.py:716
  322.8 45.7 %collective-permute-start.14 = (bf16[128,2048]{1,0:T(8,128)(2,1)S(1)}, bf16[128,2048]{1,0:T(8,128)(2,1)}, u32[]{:S(2)}, u32[]{:S(2)}) collective-permute-start(bf16[128,2048]{1,0:T(8,128)(2,1)S(1)} %get-tuple-element.68.refs_3_), channel_id=1, source_target_pairs={{0,8},{1,9},{2,10},{3,11},{4,12},{5,13},{6,14},{7,15},{8,16},{9,17... | collective-permute-start | bytes 1572872 | tf_op jit(solution)/shard_map/ppermute | solution.py:716
  368.6 190.4 %reduce-scatter.5.cloned.1.call-start = ((), (), s32[]{:S(2)}) async-start(), calls=%async_computation.13 | async-start | bytes 10027008 | tf_op jit(solution)/shard_map/reduce_scatter | solution.py:734
  376.8 37.5 %collective-permute-start.16 = (bf16[128,2048]{1,0:T(8,128)(2,1)}, bf16[128,2048]{1,0:T(8,128)(2,1)}, u32[]{:S(2)}, u32[]{:S(2)}) collective-permute-start(bf16[128,2048]{1,0:T(8,128)(2,1)} %get-tuple-element.71.refs_1_.refs_0_), channel_id=1, source_target_pairs={{0,16},{1,17},{2,18},{3,19},{4,20},{5,21},{6,22},{7,23},{8,24},{9,... | collective-permute-start | bytes 1572872 | tf_op jit(solution)/shard_map/ppermute | solution.py:716
  379.3 34.9 %collective-permute-start.17 = (bf16[128,2048]{1,0:T(8,128)(2,1)}, bf16[128,2048]{1,0:T(8,128)(2,1)}, u32[]{:S(2)}, u32[]{:S(2)}) collective-permute-start(bf16[128,2048]{1,0:T(8,128)(2,1)} %get-tuple-element.71.refs_1_.refs_0_), channel_id=1, source_target_pairs={{0,24},{1,25},{2,26},{3,27},{4,28},{5,29},{6,30},{7,31},{8,0},{9,1... | collective-permute-start | bytes 1572872 | tf_op jit(solution)/shard_map/ppermute | solution.py:716
  398.1 79.8 %collective-permute-start.24 = (bf16[2,2,176,2048]{3,2,1,0:T(8,128)(2,1)}, bf16[2,2,176,2048]{3,2,1,0:T(8,128)(2,1)}, u32[]{:S(2)}, u32[]{:S(2)}) collective-permute-start(bf16[2,2,176,2048]{3,2,1,0:T(8,128)(2,1)} %dynamic-slice_bitcast_fusion), channel_id=1, source_target_pairs={{0,1},{1,0},{2,3},{3,2},{4,5},{5,4},{6,7},{7,6},{8,9},{9,8},{10,11... | collective-permute-start | bytes 8650760 | tf_op jit(solution)/shard_map/ppermute | solution.py:747
  414.2 55.8 %collective-permute-start.18 = (bf16[128,2048]{1,0:T(8,128)(2,1)}, bf16[128,2048]{1,0:T(8,128)(2,1)}, u32[]{:S(2)}, u32[]{:S(2)}) collective-permute-start(bf16[128,2048]{1,0:T(8,128)(2,1)} %get-tuple-element.76), channel_id=1, source_target_pairs={{0,24},{1,25},{2,26},{3,27},{4,28},{5,29},{6,30},{7,31},{8,0},{9,1... | collective-permute-start | bytes 1572872 | tf_op jit(solution)/shard_map/ppermute | solution.py:716
  426.2 45.2 %collective-permute-start.19 = (bf16[128,2048]{1,0:T(8,128)(2,1)}, bf16[128,2048]{1,0:T(8,128)(2,1)}, u32[]{:S(2)}, u32[]{:S(2)}) collective-permute-start(bf16[128,2048]{1,0:T(8,128)(2,1)} %get-tuple-element.77), channel_id=1, source_target_pairs={{0,16},{1,17},{2,18},{3,19},{4,20},{5,21},{6,22},{7,23},{8,24},{9,... | collective-permute-start | bytes 1572872 | tf_op jit(solution)/shard_map/ppermute | solution.py:716
  426.5 44.9 %collective-permute-start.20 = (bf16[128,2048]{1,0:T(8,128)(2,1)}, bf16[128,2048]{1,0:T(8,128)(2,1)}, u32[]{:S(2)}, u32[]{:S(2)}) collective-permute-start(bf16[128,2048]{1,0:T(8,128)(2,1)} %get-tuple-element.78), channel_id=1, source_target_pairs={{0,8},{1,9},{2,10},{3,11},{4,12},{5,13},{6,14},{7,15},{8,16},{9,17... | collective-permute-start | bytes 1572872 | tf_op jit(solution)/shard_map/ppermute | solution.py:716
  475.2 45.0 %collective-permute-start.21 = (bf16[128,2048]{1,0:T(8,128)(2,1)}, bf16[128,2048]{1,0:T(8,128)(2,1)}, u32[]{:S(2)}, u32[]{:S(2)}) collective-permute-start(bf16[128,2048]{1,0:T(8,128)(2,1)} %get-tuple-element.89.refs_1_), channel_id=1, source_target_pairs={{0,24},{1,25},{2,26},{3,27},{4,28},{5,29},{6,30},{7,31},{8,0},{9,1... | collective-permute-start | bytes 1572872 | tf_op jit(solution)/shard_map/ppermute | solution.py:716
  476.9 62.7 %collective-permute-start.22 = (bf16[128,2048]{1,0:T(8,128)(2,1)}, bf16[128,2048]{1,0:T(8,128)(2,1)}, u32[]{:S(2)}, u32[]{:S(2)}) collective-permute-start(bf16[128,2048]{1,0:T(8,128)(2,1)} %get-tuple-element.90.refs_2_), channel_id=1, source_target_pairs={{0,16},{1,17},{2,18},{3,19},{4,20},{5,21},{6,22},{7,23},{8,24},{9,... | collective-permute-start | bytes 1572872 | tf_op jit(solution)/shard_map/ppermute | solution.py:716
  477.4 62.3 %collective-permute-start.23 = (bf16[128,2048]{1,0:T(8,128)(2,1)}, bf16[128,2048]{1,0:T(8,128)(2,1)}, u32[]{:S(2)}, u32[]{:S(2)}) collective-permute-start(bf16[128,2048]{1,0:T(8,128)(2,1)} %get-tuple-element.91.refs_3_), channel_id=1, source_target_pairs={{0,8},{1,9},{2,10},{3,11},{4,12},{5,13},{6,14},{7,15},{8,16},{9,17... | collective-permute-start | bytes 1572872 | tf_op jit(solution)/shard_map/ppermute | solution.py:716
  483.1 33.3 %collective-permute-start.25 = (bf16[2,176,1024]{2,1,0:T(8,128)(2,1)}, bf16[2,176,1024]{2,1,0:T(8,128)(2,1)}, u32[]{:S(2)}, u32[]{:S(2)}) collective-permute-start(bf16[2,176,1024]{2,1,0:T(8,128)(2,1)} %dynamic-slice_bitcast_fusion.3), channel_id=1, source_target_pairs={{0,2},{1,3},{2,0},{3,1},{4,6},{5,7},{6,4},{7,5},{8,10},{9,11},{10,... | collective-permute-start | bytes 2162696 | tf_op jit(solution)/shard_map/ppermute | solution.py:747
  485.4 33.7 %collective-permute-start.26 = (bf16[2,176,1024]{2,1,0:T(8,128)(2,1)}, bf16[2,176,1024]{2,1,0:T(8,128)(2,1)S(1)}, u32[]{:S(2)}, u32[]{:S(2)}) collective-permute-start(bf16[2,176,1024]{2,1,0:T(8,128)(2,1)} %dynamic-slice_bitcast_fusion.2), channel_id=1, source_target_pairs={{0,4},{1,5},{2,6},{3,7},{4,0},{5,1},{6,2},{7,3},{8,12},{9,13},{10,... | collective-permute-start | bytes 2162696 | tf_op jit(solution)/shard_map/ppermute | solution.py:747
  486.3 66.3 %all-to-all-start.3 = ((bf16[4,64,2816]{2,1,0:T(8,128)(2,1)}), bf16[4,64,2816]{2,1,0:T(8,128)(2,1)S(1)}, u32[]{:S(2)}, u32[]{:S(2)}) async-start(bf16[4,64,2816]{2,1,0:T(8,128)(2,1)} %bitcast.140), calls=%async_computation.5 | async-start | bytes 2883584 | tf_op jit(solution)/shard_map/all_to_all | solution.py:706
  567.0 31.1 %all-to-all-start.4 = ((bf16[4,64,2176]{2,1,0:T(8,128)(2,1)}), bf16[4,64,2176]{2,1,0:T(8,128)(2,1)S(1)}, u32[]{:S(2)}, u32[]{:S(2)}) async-start(bf16[4,64,2176]{2,1,0:T(8,128)(2,1)} %bitcast.48), calls=%async_computation.6 | async-start | bytes 2228224 | tf_op jit(solution)/shard_map/all_to_all | solution.py:706
  (103 other events, 932.7 us)
Sparse Core Ops, SparseCore 0:
  10.5 30.5 all-gather.5
  48.5 55.7 all-gather.7
  105.8 79.0 all-gather.11
  187.2 66.4 all-gather.9
  255.4 43.3 all-gather.13
  368.7 85.9 reduce-scatter.2
  458.3 88.4 reduce-scatter.4

commit v3 on v1

--- a/solution.py
+++ b/solution.py
@@ -917,12 +917,12 @@
 
     updown_grad = tie(updown_grad, mixer_terms).reshape(parts, rows_own, 2 * units)
     updown_grad = exchange(updown_grad)
-    mixer_grad = tie(mixer_grad, updown_grad, input_grad)
+    mixer_grad = tie(mixer_grad, input_grad)
     updown_shard = updown_from_parts(tie(updown_grad, mixer_grad))
     down_shard = halve_second(tie_all(down_grad, input_grad), mixer_grad)
-    out_grads = tie(halve_cores(tie(out_grads, input_grad)), mixer_grad)
+    out_grads = tie(halve_cores(tie(out_grads, input_grad)), mixer_grad, down_shard)
     out_shard = halve_second(halve_first(out_grads))
-    mixer_grad = exchange(mixer_grad.reshape(parts, rows_own, wide))
+    mixer_grad = exchange_apart(mixer_grad.reshape(parts, rows_own, wide), [input_grad])
     qkv_shard, gate_shard, strengths = mixer_from_parts(mixer_grad, width)
     beta_shard = strengths.reshape(rows_own, parts, SMALL)[:, :, :heads_part]
     return (

time: 616 us -> 622 us (level)
  the two profiles are of different devices: /device:TPU:0 before, /device:TPU:8 now
where the time goes in v3:
time: 622 us; the launch traced here: 612 us
  waiting for transfers between devices  259 us (42%)
  Pallas kernels  128 us (21%)
  local copies, waits for them, and re-layouts  69.3 us (11%)
  starting transfers between devices  64.5 us (10%)
  blocking collectives  30.9 us (5%)
  other arithmetic  22.3 us (4%)
  matrix products  21.5 us (3%)
  between operations  16.4 us (3%)
    ppermute x27, waiting for transfers between devices, shift(): return lax.ppermute(values, 'dp', pairs)  204 us
    pallas_call x12, Pallas kernels, call(): pl.pallas_call(kernel, grid=grid, in_specs=in_specs, out_specs=out_specs,...  99.9 us
    ppermute x27, starting transfers between devices, shift(): return lax.ppermute(values, 'dp', pairs)  43 us
    unnamed x184, local copies, waits for them, and re-layouts  38.7 us
    all_to_all x1, blocking collectives, exchange(): lax.all_to_all(values, 'dp', split_axis=0, concat_axis=0, axis_index_grou...  30.9 us
    ppermute x10, waiting for transfers between devices, halves_across(): return (own, lax.ppermute(other, 'dp', pairs))  29.6 us
    all_to_all x1, waiting for transfers between devices, exchange(): lax.all_to_all(values, 'dp', split_axis=0, concat_axis=0, axis_index_grou...  13.9 us
    pallas_call x4, Pallas kernels, by_rows(): pl.pallas_call(kernel, grid=(GROUP_ROWS // block,), in_specs=[spec(array....  13.6 us
  transfers between devices with their start and end apart: 47, of which 26 were waited for; matrix products, arithmetic and copies ran while one was open for 11% of the time, Pallas kernels for 19%

profile of v3, /device:TPU:8, one launch (start us, length us, event | category | flops | bytes accessed | tf_op | source)
XLA Modules:
  0.0 611.7 jit_solution(13609148060369367463)
XLA Ops:
  14.8 30.9 %all_to_all.20.refs_0_ = bf16[4,64,2176]{2,1,0:T(8,128)(2,1)} all-to-all(bf16[4,64,2176]{2,1,0:T(8,128)(2,1)} %shard_map.230), channel_id=1, replica_groups={{0,8,16,24},{1,9,17,25},{2,10,18,26},{3,11,19,27},{4,12,20,28},{5,13,21..., dimensions={0} | all-to-all | bytes 2228224 | tf_op jit(solution)/shard_map/all_to_all | solution.py:706
  53.5 30.3 %collective-permute-done.refs_1_.refs_3_ = bf16[128,2048]{1,0:T(8,128)(2,1)S(1)} collective-permute-done((bf16[128,2048]{1,0:T(8,128)(2,1)}, bf16[128,2048]{1,0:T(8,128)(2,1)S(1)}, u32[]{:S(2)}, u32[]{:S(2)}) %collective-permute-start) | collective-permute-done | bytes 524320 | tf_op jit(solution)/shard_map/ppermute | solution.py:716
  83.8 9.4 %collective-permute-done.1.refs_2_.refs_4_ = bf16[128,2048]{1,0:T(8,128)(2,1)S(1)} collective-permute-done((bf16[128,2048]{1,0:T(8,128)(2,1)}, bf16[128,2048]{1,0:T(8,128)(2,1)S(1)}, u32[]{:S(2)}, u32[]{:S(2)}) %collective-permute-start.1) | collective-permute-done | bytes 524320 | tf_op jit(solution)/shard_map/ppermute | solution.py:716
  101.3 4.8 all-to-all-start.1
  120.8 10.9 %shard_map.236 = (bf16[512,2048]{1,0:T(8,128)(2,1)S(1)}, f32[512,2176]{1,0:T(8,128)}) custom-call(f32[1,2048]{1,0:T(1,128)S(1)} %copy-done.57, bf16[2048,2176]{1,0:T(8,128)(2,1)} %all-gather.8.cloned.1.call-done.weight_ref.right_ref, bf16[128,2048]{1,0:T(8,128)(2,1)S(1)} %copy-done.5, bf16[128,2048]{1,0:T(8,128)(2,1)S(1)} %copy-done.9, ...), custom_call_target="tpu_custom_call" | custom-call | tf_op jit(solution)/shard_map/pallas_call | solution.py:277
  135.3 14.7 %shard_map.237 = (bf16[512,512]{1,0:T(8,128)(2,1)S(1)}, f32[16,128,128]{2,1,0:T(8,128)}, f32[16,128,128]{2,1,0:T(8,128)}, f32[16,128,128]{2,1,0:T(8,128)}, f32[16,128,128]{2,1,0:T(8,128)}) custom-call(f32[4,4]{1,0:T(4,128)S(1)} %multiply_reduce_fusion.layout_ref, f32[512,2176]{1,0:T(8,128)S(1)} %copy-done.40, f32[8,1536]{1,0:T(8,128)S(1)} %pad.57.param_ref.refs_0_), custom_call_target="tpu_custom_call" | custom-call | tf_op jit(solution)/shard_map/pallas_call | solution.py:277
  152.2 25.0 %collective-permute-done.10.refs_1_ = bf16[64,2816]{1,0:T(8,128)(2,1)S(1)} collective-permute-done((bf16[64,2816]{1,0:T(8,128)(2,1)}, bf16[64,2816]{1,0:T(8,128)(2,1)S(1)}, u32[]{:S(2)}, u32[]{:S(2)}) %collective-permute-start.10) | collective-permute-done | bytes 360480 | tf_op jit(solution)/shard_map/ppermute | solution.py:716
  186.0 32.2 %collective-permute-done.3.refs_0_ = bf16[128,2048]{1,0:T(8,128)(2,1)S(1)} collective-permute-done((bf16[128,2048]{1,0:T(8,128)(2,1)S(1)}, bf16[128,2048]{1,0:T(8,128)(2,1)S(1)}, u32[]{:S(2)}, u32[]{:S(2)}) %collective-permute-start.3) | collective-permute-done | bytes 524320 | tf_op jit(solution)/shard_map/ppermute | solution.py:716
  218.2 8.7 %collective-permute-done.5.refs_2_ = bf16[128,2048]{1,0:T(8,128)(2,1)S(1)} collective-permute-done((bf16[128,2048]{1,0:T(8,128)(2,1)S(1)}, bf16[128,2048]{1,0:T(8,128)(2,1)S(1)}, u32[]{:S(2)}, u32[]{:S(2)}) %collective-permute-start.5) | collective-permute-done | bytes 524320 | tf_op jit(solution)/shard_map/ppermute | solution.py:716
  239.8 28.7 %collective-permute-done.6 = bf16[128,2048]{1,0:T(8,128)(2,1)S(1)} collective-permute-done((bf16[128,2048]{1,0:T(8,128)(2,1)}, bf16[128,2048]{1,0:T(8,128)(2,1)S(1)}, u32[]{:S(2)}, u32[]{:S(2)}) %collective-permute-start.6) | collective-permute-done | bytes 524320 | tf_op jit(solution)/shard_map/ppermute | solution.py:716
  269.4 8.6 %collective-permute-done.7 = bf16[128,2048]{1,0:T(8,128)(2,1)S(1)} collective-permute-done((bf16[128,2048]{1,0:T(8,128)(2,1)}, bf16[128,2048]{1,0:T(8,128)(2,1)S(1)}, u32[]{:S(2)}, u32[]{:S(2)}) %collective-permute-start.7) | collective-permute-done | bytes 524320 | tf_op jit(solution)/shard_map/ppermute | solution.py:716
  281.1 12.6 %fusion.33 = f32[512,2816]{1,0:T(8,128)} fusion(bf16[512,2048]{1,0:T(8,128)(2,1)} %constant_dynamic-update-slice_fusion.left_ref, bf16[2048,2816]{1,0:T(8,128)(2,1)} %all-gather.10.cloned.1.call-done.right_ref), kind=kOutput, calls=%fused_computation.127 | convolution fusion | flops 5905580032 | bytes 19398656 | tf_op jit(solution)/shard_map/dot_general | solution.py:37
  294.7 8.9 %fusion.21 = (f32[512,1408]{1,0:T(8,128)S(1)}, f32[512,1408]{1,0:T(8,128)S(1)}, bf16[512,1408]{1,0:T(8,128)(2,1)}) fusion(f32[512,2816]{1,0:T(8,128)} %fusion.33, bf16[512,2048]{1,0:T(8,128)(2,1)S(1)} %shard_map.243.right_ref, bf16[1408,2048]{1,0:T(8,128)(2,1)} %all-gather.14.cloned.1.call-done.right_ref), kind=kOutput, calls=%fused_computation.52 | convolution fusion | flops 2962882560 | bytes 20840448 | tf_op jit(solution)/shard_map/dot_general | solution.py:45
  304.0 10.6 %shard_map.245 = (f32[128,2048]{1,0:T(8,128)S(1)}, bf16[128,2048]{1,0:T(8,128)(2,1)}, bf16[128,2048]{1,0:T(8,128)(2,1)S(1)}, bf16[128,2048]{1,0:T(8,128)(2,1)S(1)}) custom-call(bf16[512,2816]{1,0:T(8,128)(2,1)S(1)} %add_convert_fusion.left_ref.refs_0_, bf16[2048,2816]{1,0:T(8,128)(2,1)} %all-gather.10.cloned.1.call-done.right_ref), custom_call_target="tpu_custom_call" | custom-call | tf_op jit(solution)/shard_map/pallas_call | solution.py:277
  322.2 7.8 %shard_map.247.refs_1_.refs_0_ = bf16[1408,2048]{1,0:T(8,128)(2,1)} custom-call(bf16[512,1408]{1,0:T(8,128)(2,1)S(1)} %copy-done.20, bf16[512,2048]{1,0:T(8,128)(2,1)S(1)} %shard_map.243.right_ref), custom_call_target="tpu_custom_call" | custom-call | tf_op jit(solution)/shard_map/pallas_call | solution.py:277
  331.9 10.6 %shard_map.249.refs_1_.refs_0_ = bf16[2048,2816]{1,0:T(8,128)(2,1)} custom-call(bf16[512,2048]{1,0:T(8,128)(2,1)} %constant_dynamic-update-slice_fusion.left_ref, bf16[512,2816]{1,0:T(8,128)(2,1)S(1)} %copy-done.1), custom_call_target="tpu_custom_call" | custom-call | tf_op jit(solution)/shard_map/pallas_call | solution.py:277
  342.5 10.7 %collective-permute-done.13.refs_1_.refs_3_ = bf16[128,2048]{1,0:T(8,128)(2,1)} collective-permute-done((bf16[128,2048]{1,0:T(8,128)(2,1)S(1)}, bf16[128,2048]{1,0:T(8,128)(2,1)}, u32[]{:S(2)}, u32[]{:S(2)}) %collective-permute-start.13) | collective-permute-done | bytes 524320 | tf_op jit(solution)/shard_map/ppermute | solution.py:716
  353.2 10.3 %collective-permute-done.14.refs_2_.refs_4_ = bf16[128,2048]{1,0:T(8,128)(2,1)} collective-permute-done((bf16[128,2048]{1,0:T(8,128)(2,1)S(1)}, bf16[128,2048]{1,0:T(8,128)(2,1)}, u32[]{:S(2)}, u32[]{:S(2)}) %collective-permute-start.14) | collective-permute-done | bytes 524320 | tf_op jit(solution)/shard_map/ppermute | solution.py:716
  378.4 6.3 %shard_map.253 = (f32[128,2048]{1,0:T(8,128)S(1)}, bf16[128,2048]{1,0:T(8,128)(2,1)S(1)}, bf16[128,2048]{1,0:T(8,128)(2,1)S(1)}, bf16[128,2048]{1,0:T(8,128)(2,1)S(1)}) custom-call(bf16[512,1408]{1,0:T(8,128)(2,1)S(1)} %copy-done.21, bf16[1408,2048]{1,0:T(8,128)(2,1)} %all-gather.14.cloned.1.call-done.right_ref), custom_call_target="tpu_custom_call" | custom-call | tf_op jit(solution)/shard_map/pallas_call | solution.py:277
  394.4 15.2 %collective-permute-done.15.refs_3_.refs_1_ = bf16[128,2048]{1,0:T(8,128)(2,1)S(1)} collective-permute-done((bf16[128,2048]{1,0:T(8,128)(2,1)}, bf16[128,2048]{1,0:T(8,128)(2,1)S(1)}, u32[]{:S(2)}, u32[]{:S(2)}) %collective-permute-start.15) | collective-permute-done | bytes 524320 | tf_op jit(solution)/shard_map/ppermute | solution.py:716
  409.6 8.5 %collective-permute-done.16.refs_4_.refs_2_ = bf16[128,2048]{1,0:T(8,128)(2,1)} collective-permute-done((bf16[128,2048]{1,0:T(8,128)(2,1)}, bf16[128,2048]{1,0:T(8,128)(2,1)}, u32[]{:S(2)}, u32[]{:S(2)}) %collective-permute-start.16) | collective-permute-done | bytes 524320 | tf_op jit(solution)/shard_map/ppermute | solution.py:716
  425.7 17.8 %shard_map.256 = (bf16[512,2176]{1,0:T(8,128)(2,1)}, f32[8,1536]{1,0:T(8,128)S(1)}) custom-call(f32[4,4]{1,0:T(4,128)S(1)} %copy-done.61, f32[512,2176]{1,0:T(8,128)} %get-tuple-element.59.pre_ref, f32[8,1536]{1,0:T(8,128)S(1)} %copy-done.55, bf16[512,2048]{1,0:T(8,128)(2,1)S(1)} %copy-done.28, f32[16,128,128]{2,1,0:T(8,128)} %get-tuple-element.82.inverse_ref, ...), custom_call_target="tpu_custom_call" | custom-call | flops 60000002048 | tf_op jit(solution)/shard_map/pallas_call | solution.py:277
  445.8 8.3 %shard_map.257.refs_0_ = bf16[2048,2176]{1,0:T(8,128)(2,1)} custom-call(bf16[512,2048]{1,0:T(8,128)(2,1)S(1)} %copy-done.63, bf16[512,2176]{1,0:T(8,128)(2,1)S(1)} %copy-done.42), custom_call_target="tpu_custom_call" | custom-call | flops 20000000000 | tf_op jit(solution)/shard_map/pallas_call | solution.py:277
  455.7 8.0 %shard_map.261 = (f32[128,2048]{1,0:T(8,128)S(1)}, bf16[128,2048]{1,0:T(8,128)(2,1)S(1)}, bf16[128,2048]{1,0:T(8,128)(2,1)S(1)}, bf16[128,2048]{1,0:T(8,128)(2,1)S(1)}) custom-call(bf16[512,2176]{1,0:T(8,128)(2,1)S(1)} %copy-done.43, bf16[2048,2176]{1,0:T(8,128)(2,1)} %all-gather.8.cloned.1.call-done.weight_ref.right_ref), custom_call_target="tpu_custom_call" | custom-call | flops 149999992832 | tf_op jit(solution)/shard_map/pallas_call | solution.py:277
  489.5 23.7 %collective-permute-done.25 = bf16[2,176,1024]{2,1,0:T(8,128)(2,1)} collective-permute-done((bf16[2,176,1024]{2,1,0:T(8,128)(2,1)}, bf16[2,176,1024]{2,1,0:T(8,128)(2,1)}, u32[]{:S(2)}, u32[]{:S(2)}) %collective-permute-start.25) | collective-permute-done | bytes 720928 | tf_op jit(solution)/shard_map/ppermute | solution.py:749
  525.6 4.2 all-to-all-start.2
  535.8 3.9 all-to-all-done.2
  539.7 4.4 all-to-all-start.3
  547.8 5.9 reduce-scatter.5.cloned.1.call-done.refs_0_
  568.2 4.9 collective-permute-done.35
  574.5 13.9 %all-to-all-done.3.refs_0_ = bf16[4,64,2816]{2,1,0:T(8,128)(2,1)S(1)} async-done(((bf16[4,64,2816]{2,1,0:T(8,128)(2,1)}), bf16[4,64,2816]{2,1,0:T(8,128)(2,1)S(1)}, u32[]{:S(2)}, u32[]{:S(2)}) %all-to-all-start.3) | async-done | bytes 1441824 | tf_op jit(solution)/shard_map/all_to_all | solution.py:706
  594.3 4.9 collective-permute-done.28.refs_1_
  (431 shorter events, 189.5 us)
Async XLA Ops:
  7.2 38.5 %all-gather.6.cloned.1.call-start = ((), (), s32[]{:S(2)}) async-start(), calls=%async_computation.6 | async-start | bytes 2359296 | tf_op jit(solution)/shard_map/all_gather | solution.py:733
  10.2 109.8 %all-gather.8.cloned.1.call-start = ((), (), s32[]{:S(2)}) async-start(), calls=%async_computation.7 | async-start | bytes 10027008 | tf_op jit(solution)/shard_map/all_gather | solution.py:733
  45.7 190.6 %all-gather.12.cloned.1.call-start = ((), (), s32[]{:S(2)}) async-start(), calls=%async_computation.9 | async-start | bytes 2621440 | tf_op jit(solution)/shard_map/all_gather | solution.py:825
  48.6 44.6 %collective-permute-start.1 = (bf16[128,2048]{1,0:T(8,128)(2,1)}, bf16[128,2048]{1,0:T(8,128)(2,1)S(1)}, u32[]{:S(2)}, u32[]{:S(2)}) collective-permute-start(bf16[128,2048]{1,0:T(8,128)(2,1)} %shard_map.232.refs_0_.refs_3_), channel_id=1, source_target_pairs={{0,16},{1,17},{2,18},{3,19},{4,20},{5,21},{6,22},{7,23},{8,24},{9,... | collective-permute-start | bytes 1572872 | tf_op jit(solution)/shard_map/ppermute | solution.py:716
  52.1 43.9 %collective-permute-start.2 = (bf16[128,2048]{1,0:T(8,128)(2,1)}, bf16[128,2048]{1,0:T(8,128)(2,1)S(1)}, u32[]{:S(2)}, u32[]{:S(2)}) collective-permute-start(bf16[128,2048]{1,0:T(8,128)(2,1)} %shard_map.232.refs_0_.refs_3_), channel_id=1, source_target_pairs={{0,24},{1,25},{2,26},{3,27},{4,28},{5,29},{6,30},{7,31},{8,0},{9,1... | collective-permute-start | bytes 1572872 | tf_op jit(solution)/shard_map/ppermute | solution.py:716
  106.1 175.1 %all-gather.10.cloned.1.call-start = ((), (), s32[]{:S(2)}) async-start(), calls=%async_computation.8 | async-start | bytes 12976128 | tf_op jit(solution)/shard_map/all_gather | solution.py:733
  112.8 39.4 %collective-permute-start.9 = (bf16[64,2816]{1,0:T(8,128)(2,1)}, bf16[64,2816]{1,0:T(8,128)(2,1)S(1)}, u32[]{:S(2)}, u32[]{:S(2)}) collective-permute-start(bf16[64,2816]{1,0:T(8,128)(2,1)} %get-tuple-element.66), channel_id=1, source_target_pairs={{0,8},{1,9},{2,10},{3,11},{4,12},{5,13},{6,14},{7,15},{8,16},{9,17... | collective-permute-start | bytes 1081352 | tf_op jit(solution)/shard_map/ppermute | solution.py:716
  114.4 62.8 %collective-permute-start.10 = (bf16[64,2816]{1,0:T(8,128)(2,1)}, bf16[64,2816]{1,0:T(8,128)(2,1)S(1)}, u32[]{:S(2)}, u32[]{:S(2)}) collective-permute-start(bf16[64,2816]{1,0:T(8,128)(2,1)} %get-tuple-element.67), channel_id=1, source_target_pairs={{0,16},{1,17},{2,18},{3,19},{4,20},{5,21},{6,22},{7,23},{8,24},{9,... | collective-permute-start | bytes 1081352 | tf_op jit(solution)/shard_map/ppermute | solution.py:716
  115.5 63.5 %collective-permute-start.11 = (bf16[64,2816]{1,0:T(8,128)(2,1)}, bf16[64,2816]{1,0:T(8,128)(2,1)S(1)}, u32[]{:S(2)}, u32[]{:S(2)}) collective-permute-start(bf16[64,2816]{1,0:T(8,128)(2,1)} %get-tuple-element.68), channel_id=1, source_target_pairs={{0,24},{1,25},{2,26},{3,27},{4,28},{5,29},{6,30},{7,31},{8,0},{9,1... | collective-permute-start | bytes 1081352 | tf_op jit(solution)/shard_map/ppermute | solution.py:716
  180.2 114.5 %all-gather.14.cloned.1.call-start = ((), (), s32[]{:S(2)}) async-start(), calls=%async_computation.10 | async-start | bytes 6488064 | tf_op jit(solution)/shard_map/all_gather | solution.py:733
  180.8 273.2 %reduce-scatter.3.cloned.1.call-start = ((), (), s32[]{:S(2)}) async-start(), calls=%async_computation.11 | async-start | bytes 12976128 | tf_op jit(solution)/shard_map/reduce_scatter | solution.py:736
  180.9 37.3 %collective-permute-start.3 = (bf16[128,2048]{1,0:T(8,128)(2,1)S(1)}, bf16[128,2048]{1,0:T(8,128)(2,1)S(1)}, u32[]{:S(2)}, u32[]{:S(2)}) collective-permute-start(bf16[128,2048]{1,0:T(8,128)(2,1)S(1)} %get-tuple-element.62.refs_3_), channel_id=1, source_target_pairs={{0,24},{1,25},{2,26},{3,27},{4,28},{5,29},{6,30},{7,31},{8,0},{9,1... | collective-permute-start | bytes 1572872 | tf_op jit(solution)/shard_map/ppermute | solution.py:716
  180.9 37.3 %collective-permute-start.4 = (bf16[128,2048]{1,0:T(8,128)(2,1)S(1)}, bf16[128,2048]{1,0:T(8,128)(2,1)S(1)}, u32[]{:S(2)}, u32[]{:S(2)}) collective-permute-start(bf16[128,2048]{1,0:T(8,128)(2,1)S(1)} %get-tuple-element.63.refs_4_), channel_id=1, source_target_pairs={{0,16},{1,17},{2,18},{3,19},{4,20},{5,21},{6,22},{7,23},{8,24},{9,... | collective-permute-start | bytes 1572872 | tf_op jit(solution)/shard_map/ppermute | solution.py:716
  182.4 44.5 %collective-permute-start.5 = (bf16[128,2048]{1,0:T(8,128)(2,1)S(1)}, bf16[128,2048]{1,0:T(8,128)(2,1)S(1)}, u32[]{:S(2)}, u32[]{:S(2)}) collective-permute-start(bf16[128,2048]{1,0:T(8,128)(2,1)S(1)} %get-tuple-element.64.refs_5_), channel_id=1, source_target_pairs={{0,8},{1,9},{2,10},{3,11},{4,12},{5,13},{6,14},{7,15},{8,16},{9,17... | collective-permute-start | bytes 1572872 | tf_op jit(solution)/shard_map/ppermute | solution.py:716
  230.7 37.9 %collective-permute-start.6 = (bf16[128,2048]{1,0:T(8,128)(2,1)}, bf16[128,2048]{1,0:T(8,128)(2,1)S(1)}, u32[]{:S(2)}, u32[]{:S(2)}) collective-permute-start(bf16[128,2048]{1,0:T(8,128)(2,1)} %get-tuple-element.65), channel_id=1, source_target_pairs={{0,8},{1,9},{2,10},{3,11},{4,12},{5,13},{6,14},{7,15},{8,16},{9,17... | collective-permute-start | bytes 1572872 | tf_op jit(solution)/shard_map/ppermute | solution.py:716
  233.4 44.6 %collective-permute-start.7 = (bf16[128,2048]{1,0:T(8,128)(2,1)}, bf16[128,2048]{1,0:T(8,128)(2,1)S(1)}, u32[]{:S(2)}, u32[]{:S(2)}) collective-permute-start(bf16[128,2048]{1,0:T(8,128)(2,1)} %get-tuple-element.65), channel_id=1, source_target_pairs={{0,16},{1,17},{2,18},{3,19},{4,20},{5,21},{6,22},{7,23},{8,24},{9,... | collective-permute-start | bytes 1572872 | tf_op jit(solution)/shard_map/ppermute | solution.py:716
  239.0 41.3 %collective-permute-start.8 = (bf16[128,2048]{1,0:T(8,128)(2,1)S(1)}, bf16[128,2048]{1,0:T(8,128)(2,1)S(1)}, u32[]{:S(2)}, u32[]{:S(2)}) collective-permute-start(bf16[128,2048]{1,0:T(8,128)(2,1)S(1)} %copy-done.69), channel_id=1, source_target_pairs={{0,24},{1,25},{2,26},{3,27},{4,28},{5,29},{6,30},{7,31},{8,0},{9,1... | collective-permute-start | bytes 1572872 | tf_op jit(solution)/shard_map/ppermute | solution.py:716
  318.5 45.1 %collective-permute-start.14 = (bf16[128,2048]{1,0:T(8,128)(2,1)S(1)}, bf16[128,2048]{1,0:T(8,128)(2,1)}, u32[]{:S(2)}, u32[]{:S(2)}) collective-permute-start(bf16[128,2048]{1,0:T(8,128)(2,1)S(1)} %get-tuple-element.71.refs_3_), channel_id=1, source_target_pairs={{0,8},{1,9},{2,10},{3,11},{4,12},{5,13},{6,14},{7,15},{8,16},{9,17... | collective-permute-start | bytes 1572872 | tf_op jit(solution)/shard_map/ppermute | solution.py:716
  363.6 190.1 %reduce-scatter.5.cloned.1.call-start = ((), (), s32[]{:S(2)}) async-start(), calls=%async_computation.12 | async-start | bytes 10027008 | tf_op jit(solution)/shard_map/reduce_scatter | solution.py:736
  370.9 38.7 %collective-permute-start.15 = (bf16[128,2048]{1,0:T(8,128)(2,1)}, bf16[128,2048]{1,0:T(8,128)(2,1)S(1)}, u32[]{:S(2)}, u32[]{:S(2)}) collective-permute-start(bf16[128,2048]{1,0:T(8,128)(2,1)} %get-tuple-element.74.refs_1_.refs_0_), channel_id=1, source_target_pairs={{0,8},{1,9},{2,10},{3,11},{4,12},{5,13},{6,14},{7,15},{8,16},{9,17... | collective-permute-start | bytes 1572872 | tf_op jit(solution)/shard_map/ppermute | solution.py:716
  374.5 43.6 %collective-permute-start.16 = (bf16[128,2048]{1,0:T(8,128)(2,1)}, bf16[128,2048]{1,0:T(8,128)(2,1)}, u32[]{:S(2)}, u32[]{:S(2)}) collective-permute-start(bf16[128,2048]{1,0:T(8,128)(2,1)} %get-tuple-element.74.refs_1_.refs_0_), channel_id=1, source_target_pairs={{0,16},{1,17},{2,18},{3,19},{4,20},{5,21},{6,22},{7,23},{8,24},{9,... | collective-permute-start | bytes 1572872 | tf_op jit(solution)/shard_map/ppermute | solution.py:716
  375.7 44.0 %collective-permute-start.17 = (bf16[128,2048]{1,0:T(8,128)(2,1)}, bf16[128,2048]{1,0:T(8,128)(2,1)}, u32[]{:S(2)}, u32[]{:S(2)}) collective-permute-start(bf16[128,2048]{1,0:T(8,128)(2,1)} %get-tuple-element.74.refs_1_.refs_0_), channel_id=1, source_target_pairs={{0,24},{1,25},{2,26},{3,27},{4,28},{5,29},{6,30},{7,31},{8,0},{9,1... | collective-permute-start | bytes 1572872 | tf_op jit(solution)/shard_map/ppermute | solution.py:716
  391.9 83.7 %collective-permute-start.24 = (bf16[2,2,176,2048]{3,2,1,0:T(8,128)(2,1)}, bf16[2,2,176,2048]{3,2,1,0:T(8,128)(2,1)}, u32[]{:S(2)}, u32[]{:S(2)}) collective-permute-start(bf16[2,2,176,2048]{3,2,1,0:T(8,128)(2,1)} %dynamic-slice_bitcast_fusion), channel_id=1, source_target_pairs={{0,1},{1,0},{2,3},{3,2},{4,5},{5,4},{6,7},{7,6},{8,9},{9,8},{10,11... | collective-permute-start | bytes 8650760 | tf_op jit(solution)/shard_map/ppermute | solution.py:749
  419.8 47.3 %collective-permute-start.18 = (bf16[128,2048]{1,0:T(8,128)(2,1)}, bf16[128,2048]{1,0:T(8,128)(2,1)}, u32[]{:S(2)}, u32[]{:S(2)}) collective-permute-start(bf16[128,2048]{1,0:T(8,128)(2,1)} %get-tuple-element.79), channel_id=1, source_target_pairs={{0,24},{1,25},{2,26},{3,27},{4,28},{5,29},{6,30},{7,31},{8,0},{9,1... | collective-permute-start | bytes 1572872 | tf_op jit(solution)/shard_map/ppermute | solution.py:716
  419.8 47.3 %collective-permute-start.19 = (bf16[128,2048]{1,0:T(8,128)(2,1)}, bf16[128,2048]{1,0:T(8,128)(2,1)}, u32[]{:S(2)}, u32[]{:S(2)}) collective-permute-start(bf16[128,2048]{1,0:T(8,128)(2,1)} %get-tuple-element.80), channel_id=1, source_target_pairs={{0,16},{1,17},{2,18},{3,19},{4,20},{5,21},{6,22},{7,23},{8,24},{9,... | collective-permute-start | bytes 1572872 | tf_op jit(solution)/shard_map/ppermute | solution.py:716
  421.6 45.5 %collective-permute-start.20 = (bf16[128,2048]{1,0:T(8,128)(2,1)}, bf16[128,2048]{1,0:T(8,128)(2,1)}, u32[]{:S(2)}, u32[]{:S(2)}) collective-permute-start(bf16[128,2048]{1,0:T(8,128)(2,1)} %get-tuple-element.81), channel_id=1, source_target_pairs={{0,8},{1,9},{2,10},{3,11},{4,12},{5,13},{6,14},{7,15},{8,16},{9,17... | collective-permute-start | bytes 1572872 | tf_op jit(solution)/shard_map/ppermute | solution.py:716
  470.8 46.2 %collective-permute-start.21 = (bf16[128,2048]{1,0:T(8,128)(2,1)}, bf16[128,2048]{1,0:T(8,128)(2,1)}, u32[]{:S(2)}, u32[]{:S(2)}) collective-permute-start(bf16[128,2048]{1,0:T(8,128)(2,1)} %get-tuple-element.92.refs_1_), channel_id=1, source_target_pairs={{0,24},{1,25},{2,26},{3,27},{4,28},{5,29},{6,30},{7,31},{8,0},{9,1... | collective-permute-start | bytes 1572872 | tf_op jit(solution)/shard_map/ppermute | solution.py:716
  471.9 45.2 %collective-permute-start.22 = (bf16[128,2048]{1,0:T(8,128)(2,1)}, bf16[128,2048]{1,0:T(8,128)(2,1)}, u32[]{:S(2)}, u32[]{:S(2)}) collective-permute-start(bf16[128,2048]{1,0:T(8,128)(2,1)} %get-tuple-element.93.refs_2_), channel_id=1, source_target_pairs={{0,16},{1,17},{2,18},{3,19},{4,20},{5,21},{6,22},{7,23},{8,24},{9,... | collective-permute-start | bytes 1572872 | tf_op jit(solution)/shard_map/ppermute | solution.py:716
  472.6 44.4 %collective-permute-start.23 = (bf16[128,2048]{1,0:T(8,128)(2,1)}, bf16[128,2048]{1,0:T(8,128)(2,1)}, u32[]{:S(2)}, u32[]{:S(2)}) collective-permute-start(bf16[128,2048]{1,0:T(8,128)(2,1)} %get-tuple-element.94.refs_3_), channel_id=1, source_target_pairs={{0,8},{1,9},{2,10},{3,11},{4,12},{5,13},{6,14},{7,15},{8,16},{9,17... | collective-permute-start | bytes 1572872 | tf_op jit(solution)/shard_map/ppermute | solution.py:716
  539.7 48.7 %all-to-all-start.3 = ((bf16[4,64,2816]{2,1,0:T(8,128)(2,1)}), bf16[4,64,2816]{2,1,0:T(8,128)(2,1)S(1)}, u32[]{:S(2)}, u32[]{:S(2)}) async-start(bf16[4,64,2816]{2,1,0:T(8,128)(2,1)} %bitcast.148), calls=%async_computation.5 | async-start | bytes 2883584 | tf_op jit(solution)/shard_map/all_to_all | solution.py:706
  561.8 37.4 %collective-permute-start.28 = (bf16[64,2176]{1,0:T(8,128)(2,1)}, bf16[64,2176]{1,0:T(8,128)(2,1)S(1)}, u32[]{:S(2)}, u32[]{:S(2)}) collective-permute-start(bf16[64,2176]{1,0:T(8,128)(2,1)} %get-tuple-element.99), channel_id=1, source_target_pairs={{0,16},{1,17},{2,18},{3,19},{4,20},{5,21},{6,22},{7,23},{8,24},{9,... | collective-permute-start | bytes 835592 | tf_op jit(solution)/shard_map/ppermute | solution.py:716
  563.3 37.8 %collective-permute-start.29 = (bf16[64,2176]{1,0:T(8,128)(2,1)}, bf16[64,2176]{1,0:T(8,128)(2,1)S(1)}, u32[]{:S(2)}, u32[]{:S(2)}) collective-permute-start(bf16[64,2176]{1,0:T(8,128)(2,1)} %get-tuple-element.100), channel_id=1, source_target_pairs={{0,24},{1,25},{2,26},{3,27},{4,28},{5,29},{6,30},{7,31},{8,0},{9,1... | collective-permute-start | bytes 835592 | tf_op jit(solution)/shard_map/ppermute | solution.py:716
  (102 other events, 1103.7 us)
Sparse Core Ops, SparseCore 0:
  10.5 29.0 all-gather.5
  45.8 56.8 all-gather.7
  104.3 72.9 all-gather.11
  180.4 69.2 all-gather.9
  251.4 43.3 all-gather.13
  363.7 86.9 reduce-scatter.2
  454.3 99.3 reduce-scatter.4

commit v4 on v1

--- a/solution.py
+++ b/solution.py
@@ -414,8 +414,10 @@
     )
 
 
-def grad_product(left, right, block=256, micros=0):
+def grad_product(left, right, block=512, micros=0):
     rows, features = left.shape
+    if features <= block:
+        block = 256
     if features % block:
         block = 128
 

time: 616 us -> 615 us (level)
  no operation moved by 1% of the time
where the time goes in v4:
time: 615 us; the launch traced here: 605 us
  waiting for transfers between devices  221 us (36%)
  Pallas kernels  126 us (20%)
  starting transfers between devices  93.1 us (15%)
  local copies, waits for them, and re-layouts  68.9 us (11%)
  blocking collectives  33.6 us (5%)
  other arithmetic  23.3 us (4%)
  matrix products  22.3 us (4%)
  between operations  16.3 us (3%)
    ppermute x24, waiting for transfers between devices, shift(): return lax.ppermute(values, 'dp', pairs)  173 us
    pallas_call x12, Pallas kernels, call(): pl.pallas_call(kernel, grid=grid, in_specs=in_specs, out_specs=out_specs,...  97.2 us
    ppermute x24, starting transfers between devices, shift(): return lax.ppermute(values, 'dp', pairs)  59.9 us
    unnamed x188, local copies, waits for them, and re-layouts  38.3 us
    all_to_all x1, blocking collectives, exchange(): lax.all_to_all(values, 'dp', split_axis=0, concat_axis=0, axis_index_grou...  33.6 us
    ppermute x10, waiting for transfers between devices, halves_across(): return (own, lax.ppermute(other, 'dp', pairs))  29.7 us
    pallas_call x4, Pallas kernels, by_rows(): pl.pallas_call(kernel, grid=(GROUP_ROWS // block,), in_specs=[spec(array....  14.6 us
    dot_general x1, matrix products, plain_product(): return jnp.dot(left, right, preferred_element_type=f32)  13.4 us
  transfers between devices with their start and end apart: 45, of which 20 were waited for; matrix products, arithmetic and copies ran while one was open for 12% of the time, Pallas kernels for 19%

profile of v4, /device:TPU:0, one launch (start us, length us, event | category | flops | bytes accessed | tf_op | source)
XLA Modules:
  0.0 605.0 jit_solution(4007224954992134331)
XLA Ops:
  14.8 33.6 %all_to_all.25.refs_0_ = bf16[4,64,2176]{2,1,0:T(8,128)(2,1)} all-to-all(bf16[4,64,2176]{2,1,0:T(8,128)(2,1)} %shard_map.230), channel_id=1, replica_groups={{0,8,16,24},{1,9,17,25},{2,10,18,26},{3,11,19,27},{4,12,20,28},{5,13,21..., dimensions={0} | all-to-all | bytes 2228224 | tf_op jit(solution)/shard_map/all_to_all | solution.py:708
  56.0 11.7 %collective-permute-done.refs_1_.refs_3_ = bf16[128,2048]{1,0:T(8,128)(2,1)S(1)} collective-permute-done((bf16[128,2048]{1,0:T(8,128)(2,1)}, bf16[128,2048]{1,0:T(8,128)(2,1)S(1)}, u32[]{:S(2)}, u32[]{:S(2)}) %collective-permute-start) | collective-permute-done | bytes 524320 | tf_op jit(solution)/shard_map/ppermute | solution.py:718
  67.7 20.5 %collective-permute-done.1.refs_2_.refs_4_ = bf16[128,2048]{1,0:T(8,128)(2,1)S(1)} collective-permute-done((bf16[128,2048]{1,0:T(8,128)(2,1)}, bf16[128,2048]{1,0:T(8,128)(2,1)S(1)}, u32[]{:S(2)}, u32[]{:S(2)}) %collective-permute-start.1) | collective-permute-done | bytes 524320 | tf_op jit(solution)/shard_map/ppermute | solution.py:718
  94.5 12.8 %all-to-all-start.1 = ((bf16[32,16,256]{2,1,0:T(8,128)(2,1)}), bf16[32,16,256]{2,1,0:T(8,128)(2,1)S(1)}, u32[]{:S(2)}, u32[]{:S(2)}) async-start(bf16[32,16,256]{2,1,0:T(8,128)(2,1)} %shard_map.233), calls=%async_computation.1 | async-start | bytes 524288 | tf_op jit(solution)/shard_map/all_to_all | solution.py:803
  123.3 10.9 %shard_map.236 = (bf16[512,2048]{1,0:T(8,128)(2,1)S(1)}, f32[512,2176]{1,0:T(8,128)}) custom-call(f32[1,2048]{1,0:T(1,128)S(1)} %copy-done.54, bf16[2048,2176]{1,0:T(8,128)(2,1)} %all-gather.8.cloned.1.call-done.weight_ref.right_ref, bf16[128,2048]{1,0:T(8,128)(2,1)S(1)} %copy-done.2, bf16[128,2048]{1,0:T(8,128)(2,1)S(1)} %copy-done.6, ...), custom_call_target="tpu_custom_call" | custom-call | tf_op jit(solution)/shard_map/pallas_call | solution.py:277
  137.8 14.7 %shard_map.237 = (bf16[512,512]{1,0:T(8,128)(2,1)S(1)}, f32[16,128,128]{2,1,0:T(8,128)}, f32[16,128,128]{2,1,0:T(8,128)}, f32[16,128,128]{2,1,0:T(8,128)}, f32[16,128,128]{2,1,0:T(8,128)}) custom-call(f32[4,4]{1,0:T(4,128)S(1)} %multiply_reduce_fusion.layout_ref, f32[512,2176]{1,0:T(8,128)S(1)} %copy-done.37, f32[8,1536]{1,0:T(8,128)S(1)} %pad.57.param_ref.refs_0_), custom_call_target="tpu_custom_call" | custom-call | tf_op jit(solution)/shard_map/pallas_call | solution.py:277
  154.7 5.8 collective-permute-done.10.refs_1_
  164.5 20.3 %collective-permute-start.3 = (bf16[128,2048]{1,0:T(8,128)(2,1)S(1)}, bf16[128,2048]{1,0:T(8,128)(2,1)S(1)}, u32[]{:S(2)}, u32[]{:S(2)}) collective-permute-start(bf16[128,2048]{1,0:T(8,128)(2,1)S(1)} %get-tuple-element.59.refs_3_), channel_id=1, source_target_pairs={{0,24},{1,25},{2,26},{3,27},{4,28},{5,29},{6,30},{7,31},{8,0},{9,1... | collective-permute-start | bytes 1572872 | tf_op jit(solution)/shard_map/ppermute | solution.py:718
  186.2 11.1 %collective-permute-done.3.refs_0_ = bf16[128,2048]{1,0:T(8,128)(2,1)S(1)} collective-permute-done((bf16[128,2048]{1,0:T(8,128)(2,1)S(1)}, bf16[128,2048]{1,0:T(8,128)(2,1)S(1)}, u32[]{:S(2)}, u32[]{:S(2)}) %collective-permute-start.3) | collective-permute-done | bytes 524320 | tf_op jit(solution)/shard_map/ppermute | solution.py:718
  197.3 33.5 %collective-permute-done.4.refs_1_ = bf16[128,2048]{1,0:T(8,128)(2,1)S(1)} collective-permute-done((bf16[128,2048]{1,0:T(8,128)(2,1)S(1)}, bf16[128,2048]{1,0:T(8,128)(2,1)S(1)}, u32[]{:S(2)}, u32[]{:S(2)}) %collective-permute-start.4) | collective-permute-done | bytes 524320 | tf_op jit(solution)/shard_map/ppermute | solution.py:718
  242.3 9.7 %collective-permute-done.6 = bf16[128,2048]{1,0:T(8,128)(2,1)} collective-permute-done((bf16[128,2048]{1,0:T(8,128)(2,1)}, bf16[128,2048]{1,0:T(8,128)(2,1)}, u32[]{:S(2)}, u32[]{:S(2)}) %collective-permute-start.6) | collective-permute-done | bytes 524320 | tf_op jit(solution)/shard_map/ppermute | solution.py:718
  253.9 18.5 %collective-permute-done.7 = bf16[128,2048]{1,0:T(8,128)(2,1)S(1)} collective-permute-done((bf16[128,2048]{1,0:T(8,128)(2,1)}, bf16[128,2048]{1,0:T(8,128)(2,1)S(1)}, u32[]{:S(2)}, u32[]{:S(2)}) %collective-permute-start.7) | collective-permute-done | bytes 524320 | tf_op jit(solution)/shard_map/ppermute | solution.py:718
  274.1 13.4 %fusion.30 = f32[512,2816]{1,0:T(8,128)} fusion(bf16[512,2048]{1,0:T(8,128)(2,1)} %constant_dynamic-update-slice_fusion.left_ref, bf16[2048,2816]{1,0:T(8,128)(2,1)} %all-gather.10.cloned.1.call-done.right_ref), kind=kOutput, calls=%fused_computation.120 | convolution fusion | flops 5905580032 | bytes 19398656 | tf_op jit(solution)/shard_map/dot_general | solution.py:37
  287.5 8.7 %all-gather.14.cloned.1.call-done.right_ref = bf16[1408,2048]{1,0:T(8,128)(2,1)} async-done(((bf16[176,2048]{1,0:T(8,128)(2,1)}), bf16[1408,2048]{1,0:T(8,128)(2,1)}) %all-gather.14.cloned.1.call-update) | async-done | bytes 5767184 | tf_op jit(solution)/shard_map/all_gather | solution.py:735
  296.3 8.9 %fusion.21 = (f32[512,1408]{1,0:T(8,128)S(1)}, f32[512,1408]{1,0:T(8,128)S(1)}, bf16[512,1408]{1,0:T(8,128)(2,1)}) fusion(f32[512,2816]{1,0:T(8,128)} %fusion.30, bf16[512,2048]{1,0:T(8,128)(2,1)S(1)} %shard_map.243.right_ref, bf16[1408,2048]{1,0:T(8,128)(2,1)} %all-gather.14.cloned.1.call-done.right_ref), kind=kOutput, calls=%fused_computation.52 | convolution fusion | flops 2962882560 | bytes 20840448 | tf_op jit(solution)/shard_map/dot_general | solution.py:45
  305.5 10.5 %shard_map.245 = (f32[128,2048]{1,0:T(8,128)S(1)}, bf16[128,2048]{1,0:T(8,128)(2,1)}, bf16[128,2048]{1,0:T(8,128)(2,1)S(1)}, bf16[128,2048]{1,0:T(8,128)(2,1)S(1)}) custom-call(bf16[512,2816]{1,0:T(8,128)(2,1)S(1)} %add_convert_fusion.left_ref.refs_0_, bf16[2048,2816]{1,0:T(8,128)(2,1)} %all-gather.10.cloned.1.call-done.right_ref), custom_call_target="tpu_custom_call" | custom-call | tf_op jit(solution)/shard_map/pallas_call | solution.py:277
  322.8 7.8 %shard_map.247.refs_1_.refs_0_ = bf16[1408,2048]{1,0:T(8,128)(2,1)} custom-call(bf16[512,1408]{1,0:T(8,128)(2,1)S(1)} %copy-done.17, bf16[512,2048]{1,0:T(8,128)(2,1)S(1)} %shard_map.243.right_ref), custom_call_target="tpu_custom_call" | custom-call | tf_op jit(solution)/shard_map/pallas_call | solution.py:277
  332.5 9.6 %shard_map.249.refs_1_.refs_0_ = bf16[2048,2816]{1,0:T(8,128)(2,1)} custom-call(bf16[512,2048]{1,0:T(8,128)(2,1)} %constant_dynamic-update-slice_fusion.left_ref, bf16[512,2816]{1,0:T(8,128)(2,1)S(1)} %copy-done.1), custom_call_target="tpu_custom_call" | custom-call | tf_op jit(solution)/shard_map/pallas_call | solution.py:277
  342.1 24.0 %collective-permute-done.13.refs_1_.refs_3_ = bf16[128,2048]{1,0:T(8,128)(2,1)} collective-permute-done((bf16[128,2048]{1,0:T(8,128)(2,1)S(1)}, bf16[128,2048]{1,0:T(8,128)(2,1)}, u32[]{:S(2)}, u32[]{:S(2)}) %collective-permute-start.13) | collective-permute-done | bytes 524320 | tf_op jit(solution)/shard_map/ppermute | solution.py:718
  369.8 4.5 shard_map.251
  382.2 6.0 shard_map.253
  391.5 4.2 dynamic-slice_bitcast_fusion
  397.9 13.9 %collective-permute-done.16.refs_4_.refs_2_ = bf16[128,2048]{1,0:T(8,128)(2,1)} collective-permute-done((bf16[128,2048]{1,0:T(8,128)(2,1)}, bf16[128,2048]{1,0:T(8,128)(2,1)}, u32[]{:S(2)}, u32[]{:S(2)}) %collective-permute-start.16) | collective-permute-done | bytes 524320 | tf_op jit(solution)/shard_map/ppermute | solution.py:718
  411.8 12.0 %collective-permute-start.18 = (bf16[128,2048]{1,0:T(8,128)(2,1)}, bf16[128,2048]{1,0:T(8,128)(2,1)}, u32[]{:S(2)}, u32[]{:S(2)}) collective-permute-start(bf16[128,2048]{1,0:T(8,128)(2,1)} %get-tuple-element.76), channel_id=1, source_target_pairs={{0,24},{1,25},{2,26},{3,27},{4,28},{5,29},{6,30},{7,31},{8,0},{9,1... | collective-permute-start | bytes 1572872 | tf_op jit(solution)/shard_map/ppermute | solution.py:718
  425.7 17.9 %shard_map.256 = (bf16[512,2176]{1,0:T(8,128)(2,1)}, f32[8,1536]{1,0:T(8,128)S(1)}) custom-call(f32[4,4]{1,0:T(4,128)S(1)} %multiply_reduce_fusion.layout_ref, f32[512,2176]{1,0:T(8,128)} %get-tuple-element.56.pre_ref, f32[8,1536]{1,0:T(8,128)S(1)} %copy-done.52, bf16[512,2048]{1,0:T(8,128)(2,1)S(1)} %copy-done.25, ...), custom_call_target="tpu_custom_call" | custom-call | flops 60000002048 | tf_op jit(solution)/shard_map/pallas_call | solution.py:277
  445.9 7.3 %shard_map.257.refs_0_ = bf16[2048,2176]{1,0:T(8,128)(2,1)} custom-call(bf16[512,2048]{1,0:T(8,128)(2,1)S(1)} %copy-done.57, bf16[512,2176]{1,0:T(8,128)(2,1)S(1)} %copy-done.39), custom_call_target="tpu_custom_call" | custom-call | flops 20000000000 | tf_op jit(solution)/shard_map/pallas_call | solution.py:277
  454.9 7.7 %shard_map.261 = (f32[128,2048]{1,0:T(8,128)S(1)}, bf16[128,2048]{1,0:T(8,128)(2,1)S(1)}, bf16[128,2048]{1,0:T(8,128)(2,1)S(1)}, bf16[128,2048]{1,0:T(8,128)(2,1)S(1)}) custom-call(bf16[512,2176]{1,0:T(8,128)(2,1)S(1)} %copy-done.40, bf16[2048,2176]{1,0:T(8,128)(2,1)} %all-gather.8.cloned.1.call-done.weight_ref.right_ref), custom_call_target="tpu_custom_call" | custom-call | flops 149999992832 | tf_op jit(solution)/shard_map/pallas_call | solution.py:277
  483.8 3.9 all-to-all-start.3
  493.7 20.4 %collective-permute-done.25 = bf16[2,176,1024]{2,1,0:T(8,128)(2,1)} collective-permute-done((bf16[2,176,1024]{2,1,0:T(8,128)(2,1)}, bf16[2,176,1024]{2,1,0:T(8,128)(2,1)}, u32[]{:S(2)}, u32[]{:S(2)}) %collective-permute-start.25) | collective-permute-done | bytes 720928 | tf_op jit(solution)/shard_map/ppermute | solution.py:751
  517.8 19.0 %collective-permute-done.22.refs_1_ = bf16[128,2048]{1,0:T(8,128)(2,1)} collective-permute-done((bf16[128,2048]{1,0:T(8,128)(2,1)}, bf16[128,2048]{1,0:T(8,128)(2,1)}, u32[]{:S(2)}, u32[]{:S(2)}) %collective-permute-start.22) | collective-permute-done | bytes 524320 | tf_op jit(solution)/shard_map/ppermute | solution.py:718
  556.5 7.9 %all-to-all-done.2 = f32[32,16,128]{2,1,0:T(8,128)} async-done(((f32[32,16,128]{2,1,0:T(8,128)}), f32[32,16,128]{2,1,0:T(8,128)}, u32[]{:S(2)}, u32[]{:S(2)}) %all-to-all-start.2) | async-done | bytes 262176 | tf_op jit(solution)/shard_map/all_to_all | solution.py:915
  580.1 7.0 %collective-permute-done.30 = bf16[2,64,1024]{2,1,0:T(8,128)(2,1)S(1)} collective-permute-done((bf16[2,64,1024]{2,1,0:T(8,128)(2,1)S(1)}, bf16[2,64,1024]{2,1,0:T(8,128)(2,1)S(1)}, u32[]{:S(2)}, u32[]{:S(2)}) %collective-permute-start.30) | collective-permute-done | bytes 262176 | tf_op jit(solution)/shard_map/ppermute | solution.py:751
  (428 shorter events, 170.5 us)
Async XLA Ops:
  7.2 41.1 %all-gather.6.cloned.1.call-start = ((), (), s32[]{:S(2)}) async-start(), calls=%async_computation.7 | async-start | bytes 2359296 | tf_op jit(solution)/shard_map/all_gather | solution.py:735
  10.2 112.3 %all-gather.8.cloned.1.call-start = ((), (), s32[]{:S(2)}) async-start(), calls=%async_computation.8 | async-start | bytes 10027008 | tf_op jit(solution)/shard_map/all_gather | solution.py:735
  48.4 187.6 %all-gather.12.cloned.1.call-start = ((), (), s32[]{:S(2)}) async-start(), calls=%async_computation.10 | async-start | bytes 2621440 | tf_op jit(solution)/shard_map/all_gather | solution.py:827
  51.1 37.1 %collective-permute-start.1 = (bf16[128,2048]{1,0:T(8,128)(2,1)}, bf16[128,2048]{1,0:T(8,128)(2,1)S(1)}, u32[]{:S(2)}, u32[]{:S(2)}) collective-permute-start(bf16[128,2048]{1,0:T(8,128)(2,1)} %shard_map.232.refs_0_.refs_3_), channel_id=1, source_target_pairs={{0,16},{1,17},{2,18},{3,19},{4,20},{5,21},{6,22},{7,23},{8,24},{9,... | collective-permute-start | bytes 1572872 | tf_op jit(solution)/shard_map/ppermute | solution.py:718
  52.7 35.5 %collective-permute-start.2 = (bf16[128,2048]{1,0:T(8,128)(2,1)}, bf16[128,2048]{1,0:T(8,128)(2,1)S(1)}, u32[]{:S(2)}, u32[]{:S(2)}) collective-permute-start(bf16[128,2048]{1,0:T(8,128)(2,1)} %shard_map.232.refs_0_.refs_3_), channel_id=1, source_target_pairs={{0,24},{1,25},{2,26},{3,27},{4,28},{5,29},{6,30},{7,31},{8,0},{9,1... | collective-permute-start | bytes 1572872 | tf_op jit(solution)/shard_map/ppermute | solution.py:718
  107.4 166.8 %all-gather.10.cloned.1.call-start = ((), (), s32[]{:S(2)}) async-start(), calls=%async_computation.9 | async-start | bytes 12976128 | tf_op jit(solution)/shard_map/all_gather | solution.py:735
  114.1 40.5 %collective-permute-start.9 = (bf16[64,2816]{1,0:T(8,128)(2,1)}, bf16[64,2816]{1,0:T(8,128)(2,1)S(1)}, u32[]{:S(2)}, u32[]{:S(2)}) collective-permute-start(bf16[64,2816]{1,0:T(8,128)(2,1)} %get-tuple-element.63), channel_id=1, source_target_pairs={{0,8},{1,9},{2,10},{3,11},{4,12},{5,13},{6,14},{7,15},{8,16},{9,17... | collective-permute-start | bytes 1081352 | tf_op jit(solution)/shard_map/ppermute | solution.py:718
  116.0 44.6 %collective-permute-start.10 = (bf16[64,2816]{1,0:T(8,128)(2,1)}, bf16[64,2816]{1,0:T(8,128)(2,1)S(1)}, u32[]{:S(2)}, u32[]{:S(2)}) collective-permute-start(bf16[64,2816]{1,0:T(8,128)(2,1)} %get-tuple-element.64), channel_id=1, source_target_pairs={{0,16},{1,17},{2,18},{3,19},{4,20},{5,21},{6,22},{7,23},{8,24},{9,... | collective-permute-start | bytes 1081352 | tf_op jit(solution)/shard_map/ppermute | solution.py:718
  118.4 44.3 %collective-permute-start.11 = (bf16[64,2816]{1,0:T(8,128)(2,1)}, bf16[64,2816]{1,0:T(8,128)(2,1)S(1)}, u32[]{:S(2)}, u32[]{:S(2)}) collective-permute-start(bf16[64,2816]{1,0:T(8,128)(2,1)} %get-tuple-element.65), channel_id=1, source_target_pairs={{0,24},{1,25},{2,26},{3,27},{4,28},{5,29},{6,30},{7,31},{8,0},{9,1... | collective-permute-start | bytes 1081352 | tf_op jit(solution)/shard_map/ppermute | solution.py:718
  163.9 132.4 %all-gather.14.cloned.1.call-start = ((), (), s32[]{:S(2)}) async-start(), calls=%async_computation.11 | async-start | bytes 6488064 | tf_op jit(solution)/shard_map/all_gather | solution.py:735
  164.5 288.8 %reduce-scatter.3.cloned.1.call-start = ((), (), s32[]{:S(2)}) async-start(), calls=%async_computation.12 | async-start | bytes 12976128 | tf_op jit(solution)/shard_map/reduce_scatter | solution.py:738
  164.5 32.8 %collective-permute-start.3 = (bf16[128,2048]{1,0:T(8,128)(2,1)S(1)}, bf16[128,2048]{1,0:T(8,128)(2,1)S(1)}, u32[]{:S(2)}, u32[]{:S(2)}) collective-permute-start(bf16[128,2048]{1,0:T(8,128)(2,1)S(1)} %get-tuple-element.59.refs_3_), channel_id=1, source_target_pairs={{0,24},{1,25},{2,26},{3,27},{4,28},{5,29},{6,30},{7,31},{8,0},{9,1... | collective-permute-start | bytes 1572872 | tf_op jit(solution)/shard_map/ppermute | solution.py:718
  184.9 46.0 %collective-permute-start.4 = (bf16[128,2048]{1,0:T(8,128)(2,1)S(1)}, bf16[128,2048]{1,0:T(8,128)(2,1)S(1)}, u32[]{:S(2)}, u32[]{:S(2)}) collective-permute-start(bf16[128,2048]{1,0:T(8,128)(2,1)S(1)} %get-tuple-element.60.refs_4_), channel_id=1, source_target_pairs={{0,16},{1,17},{2,18},{3,19},{4,20},{5,21},{6,22},{7,23},{8,24},{9,... | collective-permute-start | bytes 1572872 | tf_op jit(solution)/shard_map/ppermute | solution.py:718
  185.5 45.4 %collective-permute-start.5 = (bf16[128,2048]{1,0:T(8,128)(2,1)S(1)}, bf16[128,2048]{1,0:T(8,128)(2,1)S(1)}, u32[]{:S(2)}, u32[]{:S(2)}) collective-permute-start(bf16[128,2048]{1,0:T(8,128)(2,1)S(1)} %get-tuple-element.61.refs_5_), channel_id=1, source_target_pairs={{0,8},{1,9},{2,10},{3,11},{4,12},{5,13},{6,14},{7,15},{8,16},{9,17... | collective-permute-start | bytes 1572872 | tf_op jit(solution)/shard_map/ppermute | solution.py:718
  234.9 37.5 %collective-permute-start.7 = (bf16[128,2048]{1,0:T(8,128)(2,1)}, bf16[128,2048]{1,0:T(8,128)(2,1)S(1)}, u32[]{:S(2)}, u32[]{:S(2)}) collective-permute-start(bf16[128,2048]{1,0:T(8,128)(2,1)} %get-tuple-element.62), channel_id=1, source_target_pairs={{0,16},{1,17},{2,18},{3,19},{4,20},{5,21},{6,22},{7,23},{8,24},{9,... | collective-permute-start | bytes 1572872 | tf_op jit(solution)/shard_map/ppermute | solution.py:718
  238.6 34.7 %collective-permute-start.8 = (bf16[128,2048]{1,0:T(8,128)(2,1)S(1)}, bf16[128,2048]{1,0:T(8,128)(2,1)S(1)}, u32[]{:S(2)}, u32[]{:S(2)}) collective-permute-start(bf16[128,2048]{1,0:T(8,128)(2,1)S(1)} %copy-done.71), channel_id=1, source_target_pairs={{0,24},{1,25},{2,26},{3,27},{4,28},{5,29},{6,30},{7,31},{8,0},{9,1... | collective-permute-start | bytes 1572872 | tf_op jit(solution)/shard_map/ppermute | solution.py:718
  320.3 45.7 %collective-permute-start.13 = (bf16[128,2048]{1,0:T(8,128)(2,1)S(1)}, bf16[128,2048]{1,0:T(8,128)(2,1)}, u32[]{:S(2)}, u32[]{:S(2)}) collective-permute-start(bf16[128,2048]{1,0:T(8,128)(2,1)S(1)} %get-tuple-element.67.refs_2_), channel_id=1, source_target_pairs={{0,16},{1,17},{2,18},{3,19},{4,20},{5,21},{6,22},{7,23},{8,24},{9,... | collective-permute-start | bytes 1572872 | tf_op jit(solution)/shard_map/ppermute | solution.py:718
  320.3 45.7 %collective-permute-start.14 = (bf16[128,2048]{1,0:T(8,128)(2,1)S(1)}, bf16[128,2048]{1,0:T(8,128)(2,1)}, u32[]{:S(2)}, u32[]{:S(2)}) collective-permute-start(bf16[128,2048]{1,0:T(8,128)(2,1)S(1)} %get-tuple-element.68.refs_3_), channel_id=1, source_target_pairs={{0,8},{1,9},{2,10},{3,11},{4,12},{5,13},{6,14},{7,15},{8,16},{9,17... | collective-permute-start | bytes 1572872 | tf_op jit(solution)/shard_map/ppermute | solution.py:718
  366.1 190.4 %reduce-scatter.5.cloned.1.call-start = ((), (), s32[]{:S(2)}) async-start(), calls=%async_computation.13 | async-start | bytes 10027008 | tf_op jit(solution)/shard_map/reduce_scatter | solution.py:738
  374.3 37.5 %collective-permute-start.16 = (bf16[128,2048]{1,0:T(8,128)(2,1)}, bf16[128,2048]{1,0:T(8,128)(2,1)}, u32[]{:S(2)}, u32[]{:S(2)}) collective-permute-start(bf16[128,2048]{1,0:T(8,128)(2,1)} %get-tuple-element.71.refs_1_.refs_0_), channel_id=1, source_target_pairs={{0,16},{1,17},{2,18},{3,19},{4,20},{5,21},{6,22},{7,23},{8,24},{9,... | collective-permute-start | bytes 1572872 | tf_op jit(solution)/shard_map/ppermute | solution.py:718
  376.9 34.9 %collective-permute-start.17 = (bf16[128,2048]{1,0:T(8,128)(2,1)}, bf16[128,2048]{1,0:T(8,128)(2,1)}, u32[]{:S(2)}, u32[]{:S(2)}) collective-permute-start(bf16[128,2048]{1,0:T(8,128)(2,1)} %get-tuple-element.71.refs_1_.refs_0_), channel_id=1, source_target_pairs={{0,24},{1,25},{2,26},{3,27},{4,28},{5,29},{6,30},{7,31},{8,0},{9,1... | collective-permute-start | bytes 1572872 | tf_op jit(solution)/shard_map/ppermute | solution.py:718
  395.7 79.7 %collective-permute-start.24 = (bf16[2,2,176,2048]{3,2,1,0:T(8,128)(2,1)}, bf16[2,2,176,2048]{3,2,1,0:T(8,128)(2,1)}, u32[]{:S(2)}, u32[]{:S(2)}) collective-permute-start(bf16[2,2,176,2048]{3,2,1,0:T(8,128)(2,1)} %dynamic-slice_bitcast_fusion), channel_id=1, source_target_pairs={{0,1},{1,0},{2,3},{3,2},{4,5},{5,4},{6,7},{7,6},{8,9},{9,8},{10,11... | collective-permute-start | bytes 8650760 | tf_op jit(solution)/shard_map/ppermute | solution.py:751
  411.8 54.1 %collective-permute-start.18 = (bf16[128,2048]{1,0:T(8,128)(2,1)}, bf16[128,2048]{1,0:T(8,128)(2,1)}, u32[]{:S(2)}, u32[]{:S(2)}) collective-permute-start(bf16[128,2048]{1,0:T(8,128)(2,1)} %get-tuple-element.76), channel_id=1, source_target_pairs={{0,24},{1,25},{2,26},{3,27},{4,28},{5,29},{6,30},{7,31},{8,0},{9,1... | collective-permute-start | bytes 1572872 | tf_op jit(solution)/shard_map/ppermute | solution.py:718
  423.8 45.2 %collective-permute-start.19 = (bf16[128,2048]{1,0:T(8,128)(2,1)}, bf16[128,2048]{1,0:T(8,128)(2,1)}, u32[]{:S(2)}, u32[]{:S(2)}) collective-permute-start(bf16[128,2048]{1,0:T(8,128)(2,1)} %get-tuple-element.77), channel_id=1, source_target_pairs={{0,16},{1,17},{2,18},{3,19},{4,20},{5,21},{6,22},{7,23},{8,24},{9,... | collective-permute-start | bytes 1572872 | tf_op jit(solution)/shard_map/ppermute | solution.py:718
  424.1 45.0 %collective-permute-start.20 = (bf16[128,2048]{1,0:T(8,128)(2,1)}, bf16[128,2048]{1,0:T(8,128)(2,1)}, u32[]{:S(2)}, u32[]{:S(2)}) collective-permute-start(bf16[128,2048]{1,0:T(8,128)(2,1)} %get-tuple-element.78), channel_id=1, source_target_pairs={{0,8},{1,9},{2,10},{3,11},{4,12},{5,13},{6,14},{7,15},{8,16},{9,17... | collective-permute-start | bytes 1572872 | tf_op jit(solution)/shard_map/ppermute | solution.py:718
  472.8 45.1 %collective-permute-start.21 = (bf16[128,2048]{1,0:T(8,128)(2,1)}, bf16[128,2048]{1,0:T(8,128)(2,1)}, u32[]{:S(2)}, u32[]{:S(2)}) collective-permute-start(bf16[128,2048]{1,0:T(8,128)(2,1)} %get-tuple-element.89.refs_1_), channel_id=1, source_target_pairs={{0,24},{1,25},{2,26},{3,27},{4,28},{5,29},{6,30},{7,31},{8,0},{9,1... | collective-permute-start | bytes 1572872 | tf_op jit(solution)/shard_map/ppermute | solution.py:718
  473.1 63.8 %collective-permute-start.22 = (bf16[128,2048]{1,0:T(8,128)(2,1)}, bf16[128,2048]{1,0:T(8,128)(2,1)}, u32[]{:S(2)}, u32[]{:S(2)}) collective-permute-start(bf16[128,2048]{1,0:T(8,128)(2,1)} %get-tuple-element.90.refs_2_), channel_id=1, source_target_pairs={{0,16},{1,17},{2,18},{3,19},{4,20},{5,21},{6,22},{7,23},{8,24},{9,... | collective-permute-start | bytes 1572872 | tf_op jit(solution)/shard_map/ppermute | solution.py:718
  474.5 62.3 %collective-permute-start.23 = (bf16[128,2048]{1,0:T(8,128)(2,1)}, bf16[128,2048]{1,0:T(8,128)(2,1)}, u32[]{:S(2)}, u32[]{:S(2)}) collective-permute-start(bf16[128,2048]{1,0:T(8,128)(2,1)} %get-tuple-element.91.refs_3_), channel_id=1, source_target_pairs={{0,8},{1,9},{2,10},{3,11},{4,12},{5,13},{6,14},{7,15},{8,16},{9,17... | collective-permute-start | bytes 1572872 | tf_op jit(solution)/shard_map/ppermute | solution.py:718
  480.7 33.4 %collective-permute-start.25 = (bf16[2,176,1024]{2,1,0:T(8,128)(2,1)}, bf16[2,176,1024]{2,1,0:T(8,128)(2,1)}, u32[]{:S(2)}, u32[]{:S(2)}) collective-permute-start(bf16[2,176,1024]{2,1,0:T(8,128)(2,1)} %dynamic-slice_bitcast_fusion.3), channel_id=1, source_target_pairs={{0,2},{1,3},{2,0},{3,1},{4,6},{5,7},{6,4},{7,5},{8,10},{9,11},{10,... | collective-permute-start | bytes 2162696 | tf_op jit(solution)/shard_map/ppermute | solution.py:751
  483.0 33.7 %collective-permute-start.26 = (bf16[2,176,1024]{2,1,0:T(8,128)(2,1)}, bf16[2,176,1024]{2,1,0:T(8,128)(2,1)S(1)}, u32[]{:S(2)}, u32[]{:S(2)}) collective-permute-start(bf16[2,176,1024]{2,1,0:T(8,128)(2,1)} %dynamic-slice_bitcast_fusion.2), channel_id=1, source_target_pairs={{0,4},{1,5},{2,6},{3,7},{4,0},{5,1},{6,2},{7,3},{8,12},{9,13},{10,... | collective-permute-start | bytes 2162696 | tf_op jit(solution)/shard_map/ppermute | solution.py:751
  483.8 66.4 %all-to-all-start.3 = ((bf16[4,64,2816]{2,1,0:T(8,128)(2,1)}), bf16[4,64,2816]{2,1,0:T(8,128)(2,1)S(1)}, u32[]{:S(2)}, u32[]{:S(2)}) async-start(bf16[4,64,2816]{2,1,0:T(8,128)(2,1)} %bitcast.140), calls=%async_computation.5 | async-start | bytes 2883584 | tf_op jit(solution)/shard_map/all_to_all | solution.py:708
  564.4 31.1 %all-to-all-start.4 = ((bf16[4,64,2176]{2,1,0:T(8,128)(2,1)}), bf16[4,64,2176]{2,1,0:T(8,128)(2,1)S(1)}, u32[]{:S(2)}, u32[]{:S(2)}) async-start(bf16[4,64,2176]{2,1,0:T(8,128)(2,1)} %bitcast.48), calls=%async_computation.6 | async-start | bytes 2228224 | tf_op jit(solution)/shard_map/all_to_all | solution.py:708
  (102 other events, 882.7 us)
Sparse Core Ops, SparseCore 0:
  10.5 30.5 all-gather.5
  48.5 55.7 all-gather.7
  105.8 76.5 all-gather.11
  184.7 66.4 all-gather.9
  252.9 43.3 all-gather.13
  366.2 85.9 reduce-scatter.2
  455.8 88.5 reduce-scatter.4
